TPU v7x, 32 devices: a whole 2x2x4 slice. The times are simulated.
32 devices in a mesh: dp: 2 (over core), mp: 16 (over z, y, x).
Axes of the slice: x: 2, y: 2, z: 4, core: 2. Of those that a mesh axis runs over, the one named last changes fastest.
Arguments:
- inputs: bfloat16 [4, 8192, 768], P('dp', 'mp'), may hold values from -6 to 6
- cotangent: bfloat16 [4, 8192, 768], P('dp', 'mp'), may hold values from -6 to 6
- norm_gain: float32 [2, 2, 768], replicated, may hold values from 0.5 to 1.5
- norm_bias: float32 [2, 2, 768], replicated, may hold values from -1.5 to 1.5
- in_weight: bfloat16 [2, 768, 3, 768], P(None, None, None, 'mp'), may hold values from -0.21875 to 0.21875
- kernels: bfloat16 [2, 2, 768, 2048], P(None, None, 'mp'), may hold values from -0.125 to 0.125
- out_weight: bfloat16 [2, 768, 768], P(None, 'mp'), may hold values from -0.21875 to 0.21875
- up_weight: bfloat16 [2, 768, 3072], P(None, None, 'mp'), may hold values from -0.21875 to 0.21875
- down_weight: bfloat16 [2, 3072, 768], P(None, 'mp'), may hold values from -0.109375 to 0.109375
- taps_kept: int32 [2], replicated, may hold values from 1024 to 2048, as said below
Outputs:
- output: float32 [4, 8192, 768], P('dp', 'mp')
- input_grad: float32 [4, 8192, 768], P('dp', 'mp')
- gain_grad: float32 [2, 2, 768], replicated
- bias_grad: float32 [2, 2, 768], replicated
- in_grad: float32 [2, 768, 3, 768], P(None, None, None, 'mp')
- kernel_grad: float32 [2, 2, 768, 2048], P(None, None, 'mp')
- out_grad: float32 [2, 768, 768], P(None, 'mp')
- up_grad: float32 [2, 768, 3072], P(None, None, 'mp')
- down_grad: float32 [2, 3072, 768], P(None, 'mp')
Inputs may be any that keep to these rules, and one draw needn't show every extreme that they name: Each block's kernels use taps 0 .. taps_kept - 1 only; in every draw one of the 2 blocks uses all 2048.
All inputs are finite; a program needn't handle non-finite values.
Results may differ from a plain program's by a relative error of at most 0.024.
Values may be sent and summed in bfloat16 or wider, within the bound.
No kernel may reach another device: no remote copies, remote signals or barrier semaphores. Data moves between devices by JAX's collectives and lax.ppermute only.
A program may use at most 896 MiB of HBM per device.

v0:
```python
from functools import partial

import jax
import jax.numpy as jnp
from jax import lax
from jax.sharding import PartitionSpec as P

EPS = 1e-05


def normalize(stream, gain_row, shift_row):
    average = jnp.mean(stream, axis=-1, keepdims=True)
    centered = stream - average
    variance = jnp.mean(centered * centered, axis=-1, keepdims=True)
    inv_std = lax.rsqrt(variance + EPS)
    scaled = centered * inv_std
    return (scaled * gain_row + shift_row, scaled, inv_std)


def normalize_back(normalized_gradient, scaled, inv_std, gain_row):
    grad_scaled = normalized_gradient * gain_row
    mean_grad = jnp.mean(grad_scaled, axis=-1, keepdims=True)
    mean_cross = jnp.mean(grad_scaled * scaled, axis=-1, keepdims=True)
    grad_input = inv_std * (grad_scaled - mean_grad - scaled * mean_cross)
    gain_part = jnp.sum(normalized_gradient * scaled, axis=(0, 1))
    shift_part = jnp.sum(normalized_gradient, axis=(0, 1))
    return (grad_input, gain_part, shift_part)


def toeplitz(kernel_rows):
    window = 128
    lead = kernel_rows.shape[:-1]
    tap_blocks = kernel_rows.shape[-1] // window
    padded = jnp.pad(kernel_rows, [(0, 0)] * len(lead) + [(window, window)])
    split_rows = padded.reshape(lead + (tap_blocks + 2, window))
    joined = jnp.concatenate([split_rows[..., :-1, :], split_rows[..., 1:, :]], axis=-1)
    flipped = joined[..., ::-1]
    spread = jnp.broadcast_to(flipped[..., None, :], lead + (tap_blocks + 1, window, 2 * window))
    flat = spread.reshape(lead + (tap_blocks + 1, window * 2 * window))
    skewed = flat[..., window - 1 : window - 1 + (2 * window - 1) * window]
    return skewed.reshape(lead + (tap_blocks + 1, window, 2 * window - 1))[..., :window]


def lagged_blocks(padded, depth, block_count, earlier):
    pieces = []
    for lag in range(depth):
        begin = depth - 1 - lag if earlier else lag
        pieces.append(padded[:, :, begin : begin + block_count])
    return jnp.stack(pieces, axis=2)


def causal_conv(toeplitz_mats, signal):
    window = 128
    depth = toeplitz_mats.shape[1]
    blocks = signal.reshape(signal.shape[:-1] + (signal.shape[-1] // window, window))
    block_count = blocks.shape[2]
    padded = jnp.pad(blocks, ((0, 0), (0, 0), (depth - 1, 0), (0, 0)))
    stacked = lagged_blocks(padded, depth, block_count, True)
    total = jnp.einsum(
        "csnib,cnab->csia", stacked, toeplitz_mats, preferred_element_type=jnp.float32
    )
    return total.reshape(signal.shape)


def causal_back(toeplitz_mats, grad_result, signal):
    window = 128
    depth = toeplitz_mats.shape[1]
    grad_blocks = grad_result.reshape(
        grad_result.shape[:-1] + (grad_result.shape[-1] // window, window)
    )
    sig_blocks = signal.reshape(grad_blocks.shape)
    block_count = grad_blocks.shape[2]
    grad_padded = jnp.pad(grad_blocks, ((0, 0), (0, 0), (0, depth - 1), (0, 0)))
    sig_padded = jnp.pad(sig_blocks, ((0, 0), (0, 0), (depth - 1, 0), (0, 0)))
    ahead = lagged_blocks(grad_padded, depth, block_count, False)
    grad_signal = jnp.einsum(
        "csnia,cnab->csib", ahead, toeplitz_mats, preferred_element_type=jnp.float32
    )
    behind = lagged_blocks(sig_padded, depth, block_count, True)
    kernel_mats = jnp.einsum(
        "csia,csnib->cnab", grad_blocks, behind, preferred_element_type=jnp.float32
    )
    return (grad_signal.reshape(signal.shape), kernel_mats)


def shards(
    inputs,
    cotangent,
    norm_gain,
    norm_bias,
    in_weight,
    kernels,
    out_weight,
    up_weight,
    down_weight,
    taps_kept,
):
    layer_count = in_weight.shape[0]
    tap_total = kernels.shape[-1]
    tap_mask = (jnp.arange(tap_total)[None, :] < taps_kept[:, None]).astype(jnp.float32)
    stream = inputs.astype(jnp.float32)
    kept_values = []
    for layer_idx in range(layer_count):
        input_weight, w_out, upward_weight, w_down = (
            lax.all_gather(in_weight[layer_idx], "mp", axis=2, tiled=True),
            lax.all_gather(out_weight[layer_idx], "mp", axis=0, tiled=True),
            lax.all_gather(up_weight[layer_idx], "mp", axis=1, tiled=True),
            lax.all_gather(down_weight[layer_idx], "mp", axis=0, tiled=True),
        )
        normed, scaled_one, inv_one = normalize(
            stream, norm_gain[layer_idx, 0], norm_bias[layer_idx, 0]
        )
        first_normalized = normed.astype(jnp.bfloat16)
        mixed_in = jnp.einsum(
            "nqt,tyf->yfnq", first_normalized, input_weight, preferred_element_type=jnp.float32
        ).astype(jnp.bfloat16)
        channels = lax.all_to_all(mixed_in, "mp", split_axis=1, concat_axis=3, tiled=True)
        gate_one = channels[0]
        gate_two = channels[1]
        values_in = channels[2]
        masked = kernels[layer_idx].astype(jnp.float32) * tap_mask[layer_idx]
        toeplitz_mats = toeplitz(masked).astype(jnp.bfloat16)
        conv_one = causal_conv(toeplitz_mats[0], values_in)
        carried = (gate_one * conv_one).astype(jnp.bfloat16)
        conv_two = causal_conv(toeplitz_mats[1], carried)
        gated_out = (gate_two * conv_two).astype(jnp.bfloat16)
        gated_tok = lax.all_to_all(gated_out, "mp", split_axis=2, concat_axis=0, tiled=True)
        stream = stream + jnp.einsum(
            "dsl,de->sle", gated_tok, w_out, preferred_element_type=jnp.float32
        )
        normed, scaled_two, inv_two = normalize(
            stream, norm_gain[layer_idx, 1], norm_bias[layer_idx, 1]
        )
        second_normalized = normed.astype(jnp.bfloat16)
        preactivation = jnp.einsum(
            "tvr,ru->tvu", second_normalized, upward_weight, preferred_element_type=jnp.float32
        )
        hidden = jax.nn.gelu(preactivation, approximate=False).astype(jnp.bfloat16)
        stream = stream + jnp.einsum(
            "slf,fe->sle", hidden, w_down, preferred_element_type=jnp.float32
        )
        kept_values.append(
            (
                input_weight,
                w_out,
                upward_weight,
                w_down,
                scaled_one,
                inv_one,
                first_normalized,
                gate_one,
                gate_two,
                values_in,
                masked,
                toeplitz_mats,
                conv_one,
                carried,
                conv_two,
                gated_tok,
                scaled_two,
                inv_two,
                second_normalized,
                preactivation,
                hidden,
            )
        )
    grad_stream = cotangent.astype(jnp.float32)
    gain_rows = [None] * layer_count
    shift_rows = [None] * layer_count
    in_shards = [None] * layer_count
    out_shards = [None] * layer_count
    up_shards = [None] * layer_count
    down_shards = [None] * layer_count
    kernel_shards = [None] * layer_count
    for layer_idx in reversed(range(layer_count)):
        (
            input_weight,
            w_out,
            upward_weight,
            w_down,
            scaled_one,
            inv_one,
            first_normalized,
            gate_one,
            gate_two,
            values_in,
            masked,
            toeplitz_mats,
            conv_one,
            carried,
            conv_two,
            gated_tok,
            scaled_two,
            inv_two,
            second_normalized,
            preactivation,
            hidden,
        ) = kept_values[layer_idx]
        down_in = grad_stream.astype(jnp.bfloat16)
        grad_down = jnp.einsum("slf,sle->fe", hidden, down_in, preferred_element_type=jnp.float32)
        grad_hidden = jnp.einsum("sle,fe->slf", down_in, w_down, preferred_element_type=jnp.float32)
        unused_value, gelu_pull = jax.vjp(partial(jax.nn.gelu, approximate=False), preactivation)
        preactivation_gradient = gelu_pull(grad_hidden)[0].astype(jnp.bfloat16)
        grad_up = jnp.einsum(
            "rqi,rqa->ia",
            second_normalized,
            preactivation_gradient,
            preferred_element_type=jnp.float32,
        )
        normalized_gradient = jnp.einsum(
            "grz,kz->grk", preactivation_gradient, upward_weight, preferred_element_type=jnp.float32
        )
        back_two, gain_two, shift_two = normalize_back(
            normalized_gradient, scaled_two, inv_two, norm_gain[layer_idx, 1]
        )
        grad_stream = grad_stream + back_two
        out_in = grad_stream.astype(jnp.bfloat16)
        grad_out = jnp.einsum("dsl,sle->de", gated_tok, out_in, preferred_element_type=jnp.float32)
        grad_gated = jnp.einsum(
            "sle,de->dsl", out_in, w_out, preferred_element_type=jnp.float32
        ).astype(jnp.bfloat16)
        grad_chan = lax.all_to_all(grad_gated, "mp", split_axis=0, concat_axis=2, tiled=True)
        grad_two = grad_chan * conv_two
        grad_conv_two = grad_chan * gate_two
        grad_carried, mats_two = causal_back(toeplitz_mats[1], grad_conv_two, carried)
        grad_gate_one = grad_carried * conv_one
        grad_conv_one = (grad_carried * gate_one).astype(jnp.bfloat16)
        grad_values, mats_one = causal_back(toeplitz_mats[0], grad_conv_one, values_in)
        grad_mixed = jnp.stack([grad_gate_one, grad_two, grad_values]).astype(jnp.bfloat16)
        token_gradient = lax.all_to_all(grad_mixed, "mp", split_axis=3, concat_axis=1, tiled=True)
        grad_in = jnp.einsum(
            "jew,nhje->wnh", first_normalized, token_gradient, preferred_element_type=jnp.float32
        )
        grad_norm_one = jnp.einsum(
            "jmrz,tjm->rzt", token_gradient, input_weight, preferred_element_type=jnp.float32
        )
        back_one, gain_one, shift_one = normalize_back(
            grad_norm_one, scaled_one, inv_one, norm_gain[layer_idx, 0]
        )
        grad_stream = grad_stream + back_one
        unused_mats, mats_pull = jax.vjp(toeplitz, masked)
        grad_kernel = mats_pull(jnp.stack([mats_one, mats_two]))[0] * tap_mask[layer_idx]
        gain_rows[layer_idx] = jnp.stack([gain_one, gain_two])
        shift_rows[layer_idx] = jnp.stack([shift_one, shift_two])
        in_part, out_part, up_part, down_part = (
            lax.psum_scatter(grad_in, "mp", scatter_dimension=2, tiled=True),
            lax.psum_scatter(grad_out, "mp", scatter_dimension=0, tiled=True),
            lax.psum_scatter(grad_up, "mp", scatter_dimension=1, tiled=True),
            lax.psum_scatter(grad_down, "mp", scatter_dimension=0, tiled=True),
        )
        in_shard, out_shard, up_shard, down_shard, kernel_shard = (
            lax.psum(in_part.astype(jnp.bfloat16), "dp").astype(jnp.float32),
            lax.psum(out_part.astype(jnp.bfloat16), "dp").astype(jnp.float32),
            lax.psum(up_part.astype(jnp.bfloat16), "dp").astype(jnp.float32),
            lax.psum(down_part.astype(jnp.bfloat16), "dp").astype(jnp.float32),
            lax.psum(grad_kernel.astype(jnp.bfloat16), "dp").astype(jnp.float32),
        )
        in_shards[layer_idx] = in_shard
        out_shards[layer_idx] = out_shard
        up_shards[layer_idx] = up_shard
        down_shards[layer_idx] = down_shard
        kernel_shards[layer_idx] = kernel_shard
    gain_total, shift_total = lax.psum((jnp.stack(gain_rows), jnp.stack(shift_rows)), ("dp", "mp"))
    return (
        stream,
        grad_stream,
        gain_total,
        shift_total,
        jnp.stack(in_shards),
        jnp.stack(kernel_shards),
        jnp.stack(out_shards),
        jnp.stack(up_shards),
        jnp.stack(down_shards),
    )


def solution(mesh):
    return jax.shard_map(
        shards,
        mesh=mesh,
        in_specs=(
            P("dp", "mp", None),
            P("dp", "mp", None),
            P(),
            P(),
            P(None, None, None, "mp"),
            P(None, None, "mp", None),
            P(None, "mp", None),
            P(None, None, "mp"),
            P(None, "mp", None),
            P(),
        ),
        out_specs=(
            P("dp", "mp", None),
            P("dp", "mp", None),
            P(),
            P(),
            P(None, None, None, "mp"),
            P(None, None, "mp", None),
            P(None, "mp", None),
            P(None, None, "mp"),
            P(None, "mp", None),
        ),
        check_vma=False,
    )
```

profile of v0, /device:TPU:1, one launch (start us, length us, event | category | flops | bytes accessed | tf_op | source)
XLA Modules:
  0.0 4711.8 jit_solution(4090054968601935060)
XLA Ops:
  15.3 68.2 %all-gather.17.cloned.1.call-done = bf16[1,768,3,768]{1,3,2,0:T(8,128)(2,1)} async-done(((bf16[1,768,3,48]{1,3,2,0:T(8,128)(2,1)}), bf16[1,768,3,768]{1,3,2,0:T(8,128)(2,1)}) %all-gather.17.cloned.1.call-update) | async-done | bytes 3538960 | tf_op jit(solution)/shard_map/all_gather | solution.py:105
  147.2 156.3 %reshape.346 = bf16[2,48,17,32768]{3,1,2,0:T(8,128)(2,1)} reshape(bf16[2,48,17,128,256]{4,3,1,2,0:T(8,128)(2,1)} %broadcast_in_dim.4) | data formatting | bytes 213909504 | tf_op jit(solution)/shard_map/reshape | solution.py:39
  303.5 70.9 %slice.770 = bf16[2,48,17,32640]{3,1,2,0:T(8,128)(2,1)} slice(bf16[2,48,17,32768]{3,1,2,0:T(8,128)(2,1)} %reshape.346), slice={[0:2], [0:48], [0:17], [127:32767]} | slice | bytes 213073920 | tf_op jit(solution)/shard_map/slice | solution.py:40
  374.4 349.8 %reshape.347 = bf16[2,48,17,128,255]{4,3,1,2,0:T(8,128)(2,1)} reshape(bf16[2,48,17,32640]{3,1,2,0:T(8,128)(2,1)} %slice.770) | data formatting | bytes 213073920 | tf_op jit(solution)/shard_map/reshape | solution.py:41
  724.2 36.3 slice_bitcast_fusion.1
  1108.2 156.2 %reshape.350 = bf16[2,48,17,32768]{3,1,2,0:T(8,128)(2,1)} reshape(bf16[2,48,17,128,256]{4,3,1,2,0:T(8,128)(2,1)} %broadcast_in_dim.5) | data formatting | bytes 213909504 | tf_op jit(solution)/shard_map/reshape | solution.py:39
  1264.3 70.5 %slice.779 = bf16[2,48,17,32640]{3,1,2,0:T(8,128)(2,1)} slice(bf16[2,48,17,32768]{3,1,2,0:T(8,128)(2,1)} %reshape.350), slice={[0:2], [0:48], [0:17], [127:32767]} | slice | bytes 213073920 | tf_op jit(solution)/shard_map/slice | solution.py:40
  1334.9 349.8 %reshape.351 = bf16[2,48,17,128,255]{4,3,1,2,0:T(8,128)(2,1)} reshape(bf16[2,48,17,32640]{3,1,2,0:T(8,128)(2,1)} %slice.779) | data formatting | bytes 213073920 | tf_op jit(solution)/shard_map/reshape | solution.py:41
  2275.8 93.3 %all-to-all-done.5 = bf16[16,2,73728]{2,1,0:T(2,128)(2,1)} async-done(((bf16[16,2,73728]{2,1,0:T(2,128)(2,1)}), bf16[16,2,73728]{2,1,0:T(2,128)(2,1)}, u32[]{:S(2)}, u32[]{:S(2)}) %all-to-all-start.5) | async-done | bytes 4718624 | tf_op jit(solution)/shard_map/all_to_all | solution.py:230
  2837.3 69.9 %pad_maximum_fusion.1 = f32[2,48,17,128,128]{3,4,2,1,0:T(8,128)} fusion(f32[1,48,17,128,128]{3,4,2,1,0:T(8,128)} %fusion.27, f32[1,48,17,128,128]{3,4,2,1,0:T(8,128)} %convolution_bitcast_fusion), kind=kLoop, calls=%fused_computation.1 | loop fusion | flops 26738688 | bytes 213909504 | tf_op jit(solution)/shard_map/stack | solution.py:242
  2907.2 104.1 %copy.944 = f32[2,48,17,128,128]{4,3,1,2,0:T(8,128)} copy(f32[2,48,17,128,128]{3,4,2,1,0:T(8,128)} %pad_maximum_fusion.1) | data formatting | bytes 213909504
  3011.3 107.4 %pad.85.clone = f32[2,48,17,128,255]{4,3,1,2,0:T(8,128)} pad(f32[2,48,17,128,128]{4,3,1,2,0:T(8,128)} %copy.944, f32[]{:T(128)} %constant.34.clone.1), padding=0_0x0_0x0_0x0_0x0_127 | pad | bytes 320028672 | tf_op jit(solution)/shard_map/transpose(jvp())/pad | solution.py:41
  3118.7 193.1 %reshape.358 = f32[2,48,17,32640]{3,1,2,0:T(8,128)} reshape(f32[2,48,17,128,255]{4,3,1,2,0:T(8,128)} %pad.85.clone) | data formatting | bytes 426147840 | tf_op jit(solution)/shard_map/transpose(jvp())/reshape | solution.py:41
  3311.9 140.0 %pad.86 = f32[2,48,17,32768]{3,1,2,0:T(8,128)} pad(f32[2,48,17,32640]{3,1,2,0:T(8,128)} %reshape.358, f32[]{:T(128)} %constant.34.clone.1), padding=0_0x0_0x0_0x127_1 | pad | bytes 426983424 | tf_op jit(solution)/shard_map/transpose(jvp())/pad | solution.py:40
  3451.9 141.9 %copy.948 = f32[204,8,128,256]{3,2,1,0:T(8,128)} copy(f32[204,8,128,256]{3,1,2,0:T(8,128)} %bitcast.496) | data formatting | bytes 427819008
  3593.7 64.0 %reduce_sum.267 = f32[2,48,17,256]{3,1,2,0:T(8,128)S(1)} reduce(f32[2,48,17,128,256]{4,3,1,2,0:T(8,128)} %bitcast.499, f32[]{:T(128)} %constant.34.clone.1), dimensions={3}, to_apply=%region_32.33 | reduce | flops 53059584 | bytes 215580672 | tf_op jit(solution)/shard_map/transpose(jvp())/reduce_sum | solution.py:38
  3778.8 71.4 %pad_maximum_fusion = f32[2,48,17,128,128]{3,4,2,1,0:T(8,128)} fusion(f32[1,48,17,128,128]{3,4,2,1,0:T(8,128)} %fusion.24, f32[1,48,17,128,128]{3,4,2,1,0:T(8,128)} %convolution_bitcast_fusion.1), kind=kLoop, calls=%fused_computation | loop fusion | flops 26738688 | bytes 213909504 | tf_op jit(solution)/shard_map/stack | solution.py:242
  3850.1 103.7 %copy.943 = f32[2,48,17,128,128]{4,3,1,2,0:T(8,128)} copy(f32[2,48,17,128,128]{3,4,2,1,0:T(8,128)} %pad_maximum_fusion) | data formatting | bytes 213909504
  3953.8 106.0 %pad.80.clone = f32[2,48,17,128,255]{4,3,1,2,0:T(8,128)} pad(f32[2,48,17,128,128]{4,3,1,2,0:T(8,128)} %copy.943, f32[]{:T(128)} %constant.34.clone.1), padding=0_0x0_0x0_0x0_0x0_127 | pad | bytes 320028672 | tf_op jit(solution)/shard_map/transpose(jvp())/pad | solution.py:41
  4059.9 206.9 %reshape.355 = f32[2,48,17,32640]{3,1,2,0:T(8,128)} reshape(f32[2,48,17,128,255]{4,3,1,2,0:T(8,128)} %pad.80.clone) | data formatting | bytes 426147840 | tf_op jit(solution)/shard_map/transpose(jvp())/reshape | solution.py:41
  4266.8 137.3 %pad.81 = f32[2,48,17,32768]{3,1,2,0:T(8,128)} pad(f32[2,48,17,32640]{3,1,2,0:T(8,128)} %reshape.355, f32[]{:T(128)} %constant.34.clone.1), padding=0_0x0_0x0_0x127_1 | pad | bytes 426983424 | tf_op jit(solution)/shard_map/transpose(jvp())/pad | solution.py:40
  4404.1 140.4 %copy.947 = f32[204,8,128,256]{3,2,1,0:T(8,128)} copy(f32[204,8,128,256]{3,1,2,0:T(8,128)} %bitcast.487) | data formatting | bytes 427819008
  4544.5 64.0 %reduce_sum.266 = f32[2,48,17,256]{3,1,2,0:T(8,128)S(1)} reduce(f32[2,48,17,128,256]{4,3,1,2,0:T(8,128)} %bitcast.490, f32[]{:T(128)} %constant.34.clone.1), dimensions={3}, to_apply=%region_30.31 | reduce | flops 53059584 | bytes 215580672 | tf_op jit(solution)/shard_map/transpose(jvp())/reduce_sum | solution.py:38
  4634.1 59.0 %all-reduce.18 = (f32[2,2,768]{2,1,0:T(2,128)}, f32[2,2,768]{2,1,0:T(2,128)}) all-reduce(f32[2,2,768]{2,1,0:T(2,128)S(1)} %pad_maximum_fusion.6, f32[2,2,768]{2,1,0:T(2,128)S(1)} %pad_maximum_fusion.7), channel_id=1, replica_groups=mesh['dp'=2,'mp'=16] {'dp','mp'}, use_global_device_ids=true, to_apply=%region_20.21 | all-reduce | flops 6144 | bytes 49152 | tf_op jit(solution)/shard_map/psum | solution.py:263
  (630 shorter events, 1634.8 us)
Async XLA Ops:
  7.2 76.3 %all-gather.17.cloned.1.call-start = ((), (), s32[]{:S(2)}) async-start(), calls=%async_computation.24 | async-start | bytes 3760128 | tf_op jit(solution)/shard_map/all_gather | solution.py:105
  9.2 970.1 %all-gather.19.cloned.1.call-start = ((), (), s32[]{:S(2)}) async-start(), calls=%async_computation.25 | async-start | bytes 1253376 | tf_op jit(solution)/shard_map/all_gather | solution.py:106
  10.9 974.1 %all-gather.21.cloned.1.call-start = ((), (), s32[]{:S(2)}) async-start(), calls=%async_computation.26 | async-start | bytes 5013504 | tf_op jit(solution)/shard_map/all_gather | solution.py:107
  103.9 656.7 %all-to-all-start = ((bf16[3,768,2,512]{3,2,0,1:T(2,128)(2,1)}), bf16[3,768,2,512]{3,2,0,1:T(2,128)(2,1)}, u32[]{:S(2)}, u32[]{:S(2)}) async-start(bf16[3,768,2,512]{3,2,0,1:T(2,128)(2,1)} %copy.746), calls=%async_computation | async-start | bytes 9437184 | tf_op jit(solution)/shard_map/all_to_all | solution.py:117
  109.1 922.3 %all-gather.23.cloned.1.call-start = ((), (), s32[]{:S(2)}) async-start(), calls=%async_computation.27 | async-start | bytes 5013504 | tf_op jit(solution)/shard_map/all_gather | solution.py:108
  921.9 42.8 all-to-all-start.1
  928.1 113.5 %all-gather.25.cloned.1.call-start = ((), (), s32[]{:S(2)}) async-start(), calls=%async_computation.28 | async-start | bytes 3760128 | tf_op jit(solution)/shard_map/all_gather | solution.py:105
  1062.4 658.3 %all-to-all-start.2 = ((bf16[3,768,2,512]{3,2,0,1:T(2,128)(2,1)}), bf16[3,768,2,512]{3,2,0,1:T(2,128)(2,1)}, u32[]{:S(2)}, u32[]{:S(2)}) async-start(bf16[3,768,2,512]{3,2,0,1:T(2,128)(2,1)} %copy.777), calls=%async_computation.2 | async-start | bytes 9437184 | tf_op jit(solution)/shard_map/all_to_all | solution.py:117
  1071.2 873.2 %all-gather.27.cloned.1.call-start = ((), (), s32[]{:S(2)}) async-start(), calls=%async_computation.29 | async-start | bytes 1253376 | tf_op jit(solution)/shard_map/all_gather | solution.py:106
  1071.7 879.2 %all-gather.29.cloned.1.call-start = ((), (), s32[]{:S(2)}) async-start(), calls=%async_computation.30 | async-start | bytes 5013504 | tf_op jit(solution)/shard_map/all_gather | solution.py:107
  1888.2 108.7 %all-gather.31.cloned.1.call-start = ((), (), s32[]{:S(2)}) async-start(), calls=%async_computation.31 | async-start | bytes 5013504 | tf_op jit(solution)/shard_map/all_gather | solution.py:108
  2035.1 48.9 %all-to-all-start.4 = ((bf16[768,2,512]{2,1,0:T(2,128)(2,1)}), bf16[768,2,512]{2,1,0:T(2,128)(2,1)}, u32[]{:S(2)}, u32[]{:S(2)}) async-start(bf16[768,2,512]{2,1,0:T(2,128)(2,1)} %copy.807), calls=%async_computation.4 | async-start | bytes 3145728 | tf_op jit(solution)/shard_map/all_to_all | solution.py:222
  2262.0 107.1 %all-to-all-start.5 = ((bf16[16,2,73728]{2,1,0:T(2,128)(2,1)}), bf16[16,2,73728]{2,1,0:T(2,128)(2,1)}, u32[]{:S(2)}, u32[]{:S(2)}) async-start(bf16[16,2,73728]{2,1,0:T(2,128)(2,1)} %reshape.433), calls=%async_computation.5 | async-start | bytes 9437184 | tf_op jit(solution)/shard_map/all_to_all | solution.py:230
  2271.4 1448.6 %reduce-scatter.15.cloned.1.call-start = ((), (), s32[]{:S(2)}) async-start(), calls=%async_computation.19 | async-start | bytes 2506752 | tf_op jit(solution)/shard_map/reduce_scatter | solution.py:247
  2275.8 2335.9 %reduce-scatter.13.cloned.1.call-start = ((), (), s32[]{:S(2)}) async-start(), calls=%async_computation.18 | async-start | bytes 2506752 | tf_op jit(solution)/shard_map/reduce_scatter | solution.py:247
  2460.7 2152.5 %reduce-scatter.19.cloned.1.call-start = ((), (), s32[]{:S(2)}) async-start(), calls=%async_computation.21 | async-start | bytes 10027008 | tf_op jit(solution)/shard_map/reduce_scatter | solution.py:248
  2472.1 2143.1 %reduce-scatter.23.cloned.1.call-start = ((), (), s32[]{:S(2)}) async-start(), calls=%async_computation.23 | async-start | bytes 10027008 | tf_op jit(solution)/shard_map/reduce_scatter | solution.py:249
  2482.1 2134.9 %reduce-scatter.11.cloned.1.call-start = ((), (), s32[]{:S(2)}) async-start(), calls=%async_computation.17 | async-start | bytes 7520256 | tf_op jit(solution)/shard_map/reduce_scatter | solution.py:246
  2492.4 2126.3 %reduce-scatter.17.cloned.1.call-start = ((), (), s32[]{:S(2)}) async-start(), calls=%async_computation.20 | async-start | bytes 10027008 | tf_op jit(solution)/shard_map/reduce_scatter | solution.py:248
  2532.3 54.1 %all-to-all-start.6 = ((bf16[768,2,512]{2,1,0:T(2,128)(2,1)}), bf16[768,2,512]{2,1,0:T(2,128)(2,1)}, u32[]{:S(2)}, u32[]{:S(2)}) async-start(bf16[768,2,512]{2,1,0:T(2,128)(2,1)} %copy.837), calls=%async_computation.6 | async-start | bytes 3145728 | tf_op jit(solution)/shard_map/all_to_all | solution.py:222
  2554.6 2066.0 %reduce-scatter.21.cloned.1.call-start = ((), (), s32[]{:S(2)}) async-start(), calls=%async_computation.22 | async-start | bytes 10027008 | tf_op jit(solution)/shard_map/reduce_scatter | solution.py:249
  2766.9 890.8 %all-to-all-start.7 = ((bf16[16,2,73728]{2,1,0:T(2,128)(2,1)}), bf16[16,2,73728]{2,1,0:T(2,128)(2,1)}, u32[]{:S(2)}, u32[]{:S(2)}) async-start(bf16[16,2,73728]{2,1,0:T(2,128)(2,1)} %reshape.435), calls=%async_computation.7 | async-start | bytes 9437184 | tf_op jit(solution)/shard_map/all_to_all | solution.py:230
  2782.6 1839.8 %reduce-scatter.9.cloned.1.call-start = ((), (), s32[]{:S(2)}) async-start(), calls=%async_computation.16 | async-start | bytes 7520256 | tf_op jit(solution)/shard_map/reduce_scatter | solution.py:246
  3713.8 983.9 %all-reduce.22.cloned.1.call-start = ((), (), s32[]{:S(2)}) async-start(), calls=%async_computation.32 | async-start | bytes 5111808 | tf_op jit(solution)/shard_map/psum | solution.py:252
  (115 other events, 1545.2 us)
Sparse Core Ops, SparseCore 0:
  11.3 72.1 all-gather.16
  86.3 104.1 all-gather.18
  193.8 92.6 all-gather.20
  289.1 79.0 all-gather.22
  931.3 79.7 all-gather.24
  1074.5 93.6 all-gather.26
  1171.6 83.0 all-gather.28
  1892.5 92.3 all-gather.30
  2277.1 181.2 reduce-scatter.14
  2464.0 150.0 reduce-scatter.12
  2619.8 196.9 reduce-scatter.18
  2823.2 227.2 reduce-scatter.22
  3055.8 150.1 reduce-scatter.10
  3211.6 169.9 reduce-scatter.16
  3388.1 169.9 reduce-scatter.20
  3713.9 169.9 reduce-scatter.8
  4624.2 43.6 all-reduce.21
where the time goes:
time: 4740 us; the launch traced here: 4710 us
  local copies, waits for them, and re-layouts  3380 us (71%)
  matrix products  506 us (11%)
  other arithmetic  404 us (9%)
  waiting for transfers between devices  259 us (5%)
  starting transfers between devices  91.5 us (2%)
  blocking collectives  59 us (1%)
    reshape x4, local copies, waits for them, and re-layouts, toeplitz(): skewed.reshape(lead + (tap_blocks + 1, window, 2 * window - 1))  1100 us
    unnamed x366, local copies, waits for them, and re-layouts  842 us
    reshape x2, local copies, waits for them, and re-layouts, toeplitz(): flat = spread.reshape(lead + (tap_blocks + 1, window * 2 * window))  313 us
    pad x2, local copies, waits for them, and re-layouts, toeplitz(): skewed = flat[..., window - 1:window - 1 + (2 * window - 1) * window]  277 us
    pad x2, local copies, waits for them, and re-layouts, toeplitz(): skewed.reshape(lead + (tap_blocks + 1, window, 2 * window - 1))  213 us
    slice x2, local copies, waits for them, and re-layouts, toeplitz(): skewed = flat[..., window - 1:window - 1 + (2 * window - 1) * window]  141 us
    another operation x2, other arithmetic, shards(): jnp.stack([mats_one, mats_two])  141 us
    reduce_sum x2, other arithmetic, toeplitz(): jnp.broadcast_to(flipped[..., None, :], lead + (tap_blocks + 1, window, 2...  128 us
  transfers between devices with their start and end apart: 25, of which 6 were waited for; matrix products, arithmetic and copies ran while one was open for 85% of the time, Pallas kernels for 0%

commit v1 on v0

v1 whole, which is shorter than its diff:
```python
import functools
import math

import jax
import jax.numpy as jnp
import ml_dtypes
import numpy as np
from jax import lax
from jax.experimental import pallas as pl
from jax.experimental.pallas import tpu as pltpu
from jax.sharding import PartitionSpec as P

EPS = 1e-05
LANES = 128
RADIX = 32
HALF = RADIX // 2
FREQS = HALF + 1
POINTS = LANES * RADIX
SPAN = POINTS // 2
BF16 = jnp.bfloat16
F32 = jnp.float32
VMEM_BYTES = 56 * 2**20
PASSES = 1


def params():
    return pltpu.CompilerParams(vmem_limit_bytes=VMEM_BYTES)


def whole(array):
    rank = array.ndim
    return pl.BlockSpec(array.shape, lambda *_: (0,) * rank, pipeline_mode=pl.Buffered(1))


def add(a, b):
    if a is None:
        return b
    return a if b is None else a + b


def sub(a, b):
    if b is None:
        return a
    return -b if a is None else a - b


def tidy(v):
    for exact in (0.0, 1.0, -1.0):
        if abs(v - exact) < 1e-12:
            return exact
    return v


def scaled(v, factor):
    if v is None or factor == 0.0:
        return None
    if factor == 1.0:
        return v
    return -v if factor == -1.0 else v * factor


def turn(z, angle):
    re, im = z
    c, s = tidy(math.cos(angle)), tidy(math.sin(angle))
    if re is not None and im is not None and abs(abs(c) - abs(s)) < 1e-12:
        r = math.copysign(abs(c), c)
        if c * s > 0:
            return ((re - im) * r, (re + im) * r)
        return ((re + im) * r, (im - re) * r)
    return (sub(scaled(re, c), scaled(im, s)), add(scaled(im, c), scaled(re, s)))


def analyse(x):
    n = len(x)
    if n == 1:
        return [(x[0], None)]
    even, odd = analyse(x[0::2]), analyse(x[1::2])
    if n == 2:
        return [(add(even[0][0], odd[0][0]), None), (sub(even[0][0], odd[0][0]), None)]
    half, quarter = n // 2, n // 4
    out = [None] * (half + 1)
    for k in range(quarter + 1):
        t = turn(odd[k], -2 * math.pi * k / n)
        out[k] = (add(even[k][0], t[0]), add(even[k][1], t[1]))
        if k != quarter:
            out[half - k] = (sub(even[k][0], t[0]), sub(t[1], even[k][1]))
    return out


def synthesise(x, n, upper):
    if n == 2:
        return [sub(x[0][0], x[1][0]) if upper else add(x[0][0], x[1][0])]
    half, quarter = n // 2, n // 4
    even, odd = [], []
    for k in range(quarter + 1):
        a, b = x[k], x[half - k]
        if k == 0:
            even.append((add(a[0], b[0]), None))
            odd.append((sub(a[0], b[0]), None))
        elif k == quarter:
            even.append((a[0] * 2.0, None))
            odd.append((a[1] * -2.0, None))
        else:
            even.append((add(a[0], b[0]), sub(a[1], b[1])))
            odd.append(turn((sub(a[0], b[0]), add(a[1], b[1])), 2 * math.pi * k / n))
    out = [None] * half
    out[0::2] = synthesise(even, half, upper)
    out[1::2] = synthesise(odd, half, upper)
    return out


def split_bf16(matrix):
    matrix = matrix.astype(np.float32)
    high = matrix.astype(ml_dtypes.bfloat16)
    low = (matrix - high.astype(np.float32)).astype(ml_dtypes.bfloat16)
    return jnp.asarray(np.stack([high, low][: 1 if PASSES == 1 else 2]))


def tables():
    j = np.arange(LANES)
    angle = 2 * np.pi * np.outer(j, j) / LANES
    c, s = np.cos(angle), np.sin(angle)
    twist = 2 * np.pi * np.outer(np.arange(FREQS), j) / POINTS
    return [
        split_bf16(np.block([[c, -s], [s, c]])),
        split_bf16(np.block([[c, s], [-s, c]]) / POINTS),
        jnp.asarray(np.cos(twist), F32),
        jnp.asarray(np.sin(twist), F32),
    ]


def lane_product(a, matrix):
    high = a.astype(BF16)
    y = jnp.dot(high, matrix[0], preferred_element_type=F32)
    if PASSES > 1:
        y = y + jnp.dot(high, matrix[1], preferred_element_type=F32)
    if PASSES > 2:
        low = (a - high.astype(F32)).astype(BF16)
        y = y + jnp.dot(low, matrix[0], preferred_element_type=F32)
    return y


class Convolver:
    def __init__(self, sources, groups, pieces, blocks, rows, refs):
        self.sources, self.groups, self.pieces = sources, groups, pieces
        self.blocks, self.rows = blocks, rows
        self.forward, self.backward, self.cos, self.sin, self.left, self.right, self.freq = refs

    def places(self):
        for i in range(self.sources * self.groups * self.pieces):
            chunk, piece = divmod(i, self.pieces)
            group, source = divmod(chunk, self.sources)
            begin = (group * self.pieces + piece) * LANES
            yield i, source, slice(begin, begin + LANES)

    def load(self, ref, dst):
        for i, source, lanes in self.places():
            dst[i] = ref[source, :, lanes].astype(F32)

    def store(self, src, ref, part=None):
        for i, source, lanes in self.places():
            if part is None:
                ref[source, :, lanes] = src[i].astype(ref.dtype)
            else:
                ref[source, part, :, lanes] = src[i].astype(ref.dtype)

    def subtiles(self):
        return [pl.ds(8 * t, 8) for t in range(self.rows // 8)]

    def spectrum(self, read, count, base):
        for b in range(count):
            for rows in self.subtiles():
                x = analyse([read(b, i, rows) for i in range(HALF)] + [None] * HALF)
                for f, (re, im) in enumerate(x):
                    if f:
                        c, s = self.cos[f : f + 1, :], self.sin[f : f + 1, :]
                        if im is None:
                            re, im = re * c, -(re * s)
                        else:
                            re, im = re * c + im * s, im * c - re * s
                    self.left[b * FREQS + f, rows, 0:LANES] = re
                    self.left[b * FREQS + f, rows, LANES:] = jnp.zeros_like(re) if im is None else im
            y = lane_product(self.stacked(b), self.forward)
            begin = (base + b) * FREQS
            self.freq[begin : begin + FREQS] = y.reshape(FREQS, self.rows, 2 * LANES)

    def stacked(self, b):
        return self.left[b * FREQS : (b + 1) * FREQS].reshape(FREQS * self.rows, 2 * LANES)

    def entry(self, row, rows):
        return self.freq[row, rows, 0:LANES], self.freq[row, rows, LANES:]

    def window(self, base, b, f, rows, ahead):
        re, im = self.entry((base + b) * FREQS + f, rows)
        other = b + 1 if ahead else b - 1
        if not ahead and f % 2:
            re, im = -re, -im
        if 0 <= other < self.blocks:
            ore, oim = self.entry((base + other) * FREQS + f, rows)
            if ahead and f % 2:
                return re - ore, im - oim
            return re + ore, im + oim
        return re, im

    def inverse(self, b, upper, write):
        y = lane_product(self.stacked(b), self.backward)
        begin = b * FREQS
        self.right[begin : begin + FREQS] = y.reshape(FREQS, self.rows, 2 * LANES)
        for rows in self.subtiles():
            parts = []
            for f in range(FREQS):
                re = self.right[begin + f, rows, 0:LANES]
                im = self.right[begin + f, rows, LANES:]
                c, s = self.cos[f : f + 1, :], self.sin[f : f + 1, :]
                if f == 0:
                    parts.append((re, None))
                elif f == HALF:
                    parts.append((re * c - im * s, None))
                else:
                    parts.append((re * c - im * s, im * c + re * s))
            for i, value in enumerate(synthesise(parts, RADIX, upper)):
                write(b, i, rows, value)

    def convolve(self, signal, kernel, ahead, write):
        for b in range(self.blocks):
            for rows in self.subtiles():
                for f in range(FREQS):
                    re, im = self.window(signal, b, f, rows, ahead)
                    kre, kim = self.entry(kernel * FREQS + f, rows)
                    if ahead:
                        pre, pim = re * kre + im * kim, im * kre - re * kim
                    else:
                        pre, pim = re * kre - im * kim, re * kim + im * kre
                    self.left[b * FREQS + f, rows, 0:LANES] = pre
                    self.left[b * FREQS + f, rows, LANES:] = pim
            self.inverse(b, not ahead, write)

    def taps(self, signal, grads, write):
        for rows in self.subtiles():
            for f in range(FREQS):
                re = im = None
                for b in range(self.blocks):
                    gre, gim = self.window(grads, b, f, rows, True)
                    sre, sim = self.entry((signal + b) * FREQS + f, rows)
                    re = add(re, sre * gre + sim * gim)
                    im = add(im, sre * gim - sim * gre)
                self.left[f, rows, 0:LANES] = re
                self.left[f, rows, LANES:] = im
        self.inverse(0, False, write)


def kernel_reader(k_ref, j):
    def read(_, i, rows):
        value = k_ref[j, :, i * LANES : (i + 1) * LANES].astype(F32)
        return value[rows.start : rows.start + rows.size]

    return read


def mix_body(shape, v_ref, g_ref, k_ref, *refs):
    (fwd, bwd, cos, sin, out_ref, one_ref, carried_ref, xs, gs, left, right, freq) = refs
    cv = Convolver(*shape, v_ref.shape[1], (fwd, bwd, cos, sin, left, right, freq))
    n = cv.blocks
    cv.load(v_ref, xs)
    cv.load(g_ref, gs)

    def read(b, i, rows):
        return xs[b * HALF + i, rows, :]

    cv.spectrum(kernel_reader(k_ref, 0), 1, n)
    cv.spectrum(kernel_reader(k_ref, 1), 1, n + 1)
    cv.spectrum(read, n, 0)

    def gate(b, i, rows, value):
        r = b * HALF + i
        xs[r, rows, :] = (gs[r, rows, :] * value).astype(BF16).astype(F32)
        gs[r, rows, :] = value

    cv.convolve(0, n, False, gate)
    one_ref[...] = gs[...].astype(BF16)
    carried_ref[...] = xs[...].astype(BF16)
    cv.spectrum(read, n, 0)

    def keep(b, i, rows, value):
        gs[b * HALF + i, rows, :] = value

    cv.convolve(0, n + 1, False, keep)
    cv.store(gs, out_ref)


def unmix_body(shape, d_ref, v_ref, g_ref, one_ref, carried_ref, k_ref, *refs):
    (fwd, bwd, cos, sin, out_ref, dk_ref, xs, gs, left, right, freq) = refs
    cv = Convolver(*shape, v_ref.shape[1], (fwd, bwd, cos, sin, left, right, freq))
    n = cv.blocks
    cv.load(d_ref, xs)
    cv.load(g_ref, gs)

    def read(b, i, rows):
        return xs[b * HALF + i, rows, :]

    def read_carried(b, i, rows):
        return carried_ref[b * HALF + i].astype(F32)[rows.start : rows.start + rows.size]

    def put(j):
        def write(_, i, rows, value):
            dk_ref[j, rows, i * LANES : (i + 1) * LANES] = value

        return write

    cv.spectrum(kernel_reader(k_ref, 1), 1, 2 * n)
    cv.spectrum(read, n, 0)
    cv.spectrum(read_carried, n, n)
    cv.taps(n, 0, put(1))

    def gate(b, i, rows, value):
        r = b * HALF + i
        xs[r, rows, :] = (gs[r, rows, :] * value).astype(BF16).astype(F32)
        gs[r, rows, :] = value

    cv.convolve(0, 2 * n, True, gate)
    gs[...] = gs[...] * one_ref[...].astype(F32)
    cv.store(gs, out_ref, 0)
    cv.spectrum(read, n, 0)
    cv.load(v_ref, xs)
    cv.spectrum(kernel_reader(k_ref, 0), 1, 2 * n)
    cv.spectrum(read, n, n)
    cv.taps(n, 0, put(0))

    def keep(b, i, rows, value):
        gs[b * HALF + i, rows, :] = value

    cv.convolve(0, 2 * n, True, keep)
    cv.store(gs, out_ref, 1)


def conv_sizes(gates):
    sources, groups, _, shard, length = gates.shape
    tile = 16
    pieces = length // (groups * LANES)
    total = sources * length
    return sources, groups, shard, length, tile, pieces, total // LANES, total // SPAN


def conv_scratch(tile, rows, blocks, spectra):
    return [
        pltpu.VMEM((rows, tile, LANES), F32),
        pltpu.VMEM((rows, tile, LANES), F32),
        pltpu.VMEM((blocks * FREQS, tile, 2 * LANES), F32),
        pltpu.VMEM((blocks * FREQS, tile, 2 * LANES), F32),
        pltpu.VMEM((spectra * FREQS, tile, 2 * LANES), F32),
    ]


def mix(gates, taps):
    q, g, shard, length, tile, pieces, rows, blocks = conv_sizes(gates)
    consts = tables()
    by_source = (q, None, None, tile, length)
    nat = pl.BlockSpec((None, rows, tile, LANES), lambda a, b: (a, 0, b, 0))
    return pl.pallas_call(
        functools.partial(mix_body, (q, g, pieces, blocks)),
        grid=(g, shard // tile),
        in_specs=[
            pl.BlockSpec(by_source, lambda a, b: (0, a, 1, b, 0)),
            pl.BlockSpec(by_source, lambda a, b: (0, a, 0, b, 0)),
            pl.BlockSpec((None, 2, tile, SPAN), lambda a, b: (a, 0, b, 0)),
        ]
        + [whole(c) for c in consts],
        out_specs=[pl.BlockSpec((q, None, tile, length), lambda a, b: (0, a, b, 0)), nat, nat],
        out_shape=[
            jax.ShapeDtypeStruct((q, g, shard, length), BF16),
            jax.ShapeDtypeStruct((g, rows, shard, LANES), BF16),
            jax.ShapeDtypeStruct((g, rows, shard, LANES), BF16),
        ],
        scratch_shapes=conv_scratch(tile, rows, blocks, blocks + 2),
        compiler_params=params(),
        name="mix",
    )(gates, gates, taps, *consts)


def unmix(grads, gates, conv_one, carried, taps):
    q, g, shard, length, tile, pieces, rows, blocks = conv_sizes(gates)
    consts = tables()
    by_source = (q, None, None, tile, length)
    nat = pl.BlockSpec((None, rows, tile, LANES), lambda a, b: (a, 0, b, 0))
    kern = pl.BlockSpec((None, 2, tile, SPAN), lambda a, b: (a, 0, b, 0))
    return pl.pallas_call(
        functools.partial(unmix_body, (q, g, pieces, blocks)),
        grid=(g, shard // tile),
        in_specs=[
            pl.BlockSpec((q, None, tile, length), lambda a, b: (0, a, b, 0)),
            pl.BlockSpec(by_source, lambda a, b: (0, a, 1, b, 0)),
            pl.BlockSpec(by_source, lambda a, b: (0, a, 0, b, 0)),
            nat,
            nat,
            kern,
        ]
        + [whole(c) for c in consts],
        out_specs=[
            pl.BlockSpec((q, None, 2, tile, length), lambda a, b: (0, a, 0, b, 0)),
            kern,
        ],
        out_shape=[
            jax.ShapeDtypeStruct((q, g, 2, shard, length), BF16),
            jax.ShapeDtypeStruct((g, 2, shard, SPAN), F32),
        ],
        scratch_shapes=conv_scratch(tile, rows, blocks, 2 * blocks + 1),
        compiler_params=params(),
        name="unmix",
    )(grads, gates, gates, conv_one, carried, taps, *consts)


def standardise(stream):
    average = jnp.mean(stream, axis=0, keepdims=True)
    centered = stream - average
    inv_std = lax.rsqrt(jnp.mean(centered * centered, axis=0, keepdims=True) + EPS)
    return centered * inv_std, inv_std


def standardise_back(grad, gain, stream):
    unit, inv_std = standardise(stream)
    g = grad * gain
    mean_grad = jnp.mean(g, axis=0, keepdims=True)
    mean_cross = jnp.mean(g * unit, axis=0, keepdims=True)
    back = inv_std * (g - mean_grad - unit * mean_cross)
    gain_part = jnp.sum(grad * unit, axis=1, keepdims=True)
    bias_part = jnp.sum(grad, axis=1, keepdims=True)
    return back, gain_part, bias_part


def transposed(x):
    return jnp.transpose(x.astype(F32))


def gelu_pair(x):
    z = jnp.abs(x) * math.sqrt(0.5)
    t = 1.0 / (1.0 + 0.3275911 * z)
    e = jnp.exp(-(z * z))
    poly = t * (
        0.127414796 + t * (-0.142248368 + t * (0.710706871 + t * (-0.726576014 + t * 0.530702714)))
    )
    tail = poly * e
    phi = jnp.where(x >= 0, 1.0 - tail, tail)
    return x * phi, phi + x * (e * (1.0 / math.sqrt(2 * math.pi)))


def first(axis_is_zero, refs, cut, body):
    if len(refs) == 1:
        body(refs[0].at[:, 0 : 2 * cut], refs[0].at[:, 2 * cut : 3 * cut])
        return

    @pl.when(axis_is_zero)
    def _():
        body(refs[0], refs[1].at[:, 0:cut])

    @pl.when(jnp.logical_not(axis_is_zero))
    def _():
        body(refs[1], refs[0].at[:, 0:cut])


class Pieces:
    def __init__(self, arrays, begin, rows):
        self.arrays, self.begin, self.rows = arrays, begin, rows

    def specs(self):
        mp, _, width = self.arrays[0].shape
        block = self.begin // self.rows
        shape = (mp, self.rows, width)
        spec = pl.BlockSpec(shape, lambda *_: (0, block, 0), pipeline_mode=pl.Buffered(1))
        return [spec] * len(self.arrays)

    def __len__(self):
        return len(self.arrays)


SCALARS = pl.BlockSpec(memory_space=pltpu.SMEM)


def by_channel(blocks, groups):
    peers = blocks.shape[0] // groups
    order = [h * peers + q for q in range(peers) for h in range(groups)]
    return jnp.concatenate([blocks[m : m + 1] for m in order], axis=0)


def project_body(natural, ways, groups, place_ref, x_ref, gain_ref, bias_ref, *rest):
    dense, rest = rest[:ways], rest[ways:]
    if natural:
        s_ref, op_ref, two_ref, n_ref, pair_w, value_w = rest
        x = transposed(x_ref[...])
        s_ref[...] = x
    else:
        op_ref, two_ref, n_ref, pair_w, value_w = rest
        x = x_ref[...]
    mp, cut, t = two_ref.shape

    @pl.when(pl.program_id(0) == 0)
    def _():
        def body(pair, value):
            pair_w[...] = by_channel(pair, groups)
            value_w[...] = by_channel(value, groups)

        first(place_ref[0] == 0, dense, cut, body)

    unit, _ = standardise(x)
    normed = unit * gain_ref[...] + bias_ref[...]
    n_ref[...] = transposed(normed).astype(BF16)
    normed = normed.astype(BF16)
    width = normed.shape[0]
    y = jnp.dot(
        pair_w[...].reshape(mp * 2 * cut, width), normed, preferred_element_type=F32
    )
    y = y.astype(BF16).reshape(mp, 2, cut, t)
    op_ref[:, 0] = y[:, 0]
    two_ref[...] = y[:, 1]
    y = jnp.dot(value_w[...].reshape(mp * cut, width), normed, preferred_element_type=F32)
    op_ref[:, 1] = y.astype(BF16).reshape(mp, cut, t)


def token_tile(length):
    return min(length, 256)


def project(natural, groups, place, x, dense, gain, bias, cut):
    mp, _, width = dense.arrays[0].shape
    length = x.shape[0] if natural else x.shape[1]
    t = token_tile(length)
    tall = pl.BlockSpec((t, width), lambda i: (i, 0))
    flat = pl.BlockSpec((width, t), lambda i: (0, i))
    out_specs = [
        pl.BlockSpec((mp, 2, cut, t), lambda i: (0, 0, 0, i)),
        pl.BlockSpec((mp, cut, t), lambda i: (0, 0, i)),
        tall,
    ]
    out_shape = [
        jax.ShapeDtypeStruct((mp, 2, cut, length), BF16),
        jax.ShapeDtypeStruct((mp, cut, length), BF16),
        jax.ShapeDtypeStruct((length, width), BF16),
    ]
    if natural:
        out_specs.insert(0, flat)
        out_shape.insert(0, jax.ShapeDtypeStruct((width, length), F32))
    return pl.pallas_call(
        functools.partial(project_body, natural, len(dense), groups),
        grid=(length // t,),
        in_specs=[SCALARS, tall if natural else flat, whole(gain), whole(bias)] + dense.specs(),
        out_specs=out_specs,
        out_shape=out_shape,
        scratch_shapes=[
            pltpu.VMEM((mp, 2 * cut, width), BF16),
            pltpu.VMEM((mp, cut, width), BF16),
        ],
        compiler_params=params(),
        name="project",
    )(place, x, gain, bias, *dense.arrays)


def ff_chunks(refs):
    mp, rows, width = refs[0].shape
    part = rows // 2
    step = min(mp, width // part)
    size = step * part
    for p, ref in enumerate(refs):
        for j in range(mp // step):
            begin = (p * (mp // step) + j) * size
            yield ref, slice(j * step, (j + 1) * step), part, slice(begin, begin + size)


def forward_body(natural, ways, s_ref, c_ref, g_ref, wo_ref, gain_ref, bias_ref, *rest):
    ff, rest = rest[:ways], rest[ways:]
    s1_ref, s2_ref, h_ref, d_ref, n_ref, gated_ref, wo_t, down_t = rest
    width = ff[0].shape[-1]

    @pl.when(pl.program_id(0) == 0)
    def _():
        wo_t[...] = transposed(wo_ref[...]).astype(BF16)
        for ref, blocks, part, units in ff_chunks(ff):
            block = ref[blocks, part:, :].reshape(units.stop - units.start, width)
            down_t[:, units] = transposed(block).astype(BF16)

    gated = (g_ref[...].astype(F32) * c_ref[...].astype(F32)).astype(BF16)
    gated_ref[...] = gated
    s1 = s_ref[...] + jnp.dot(wo_t[...], gated, preferred_element_type=F32)
    s1_ref[...] = s1
    unit, _ = standardise(s1)
    normed = unit * gain_ref[...] + bias_ref[...]
    n_ref[...] = transposed(normed).astype(BF16)
    normed = normed.astype(BF16)
    total = s1
    for ref, blocks, part, units in ff_chunks(ff):
        up = ref[blocks, 0:part, :].reshape(units.stop - units.start, width)
        hidden, slope = gelu_pair(jnp.dot(up, normed, preferred_element_type=F32))
        hidden = hidden.astype(BF16)
        h_ref[units, :] = hidden
        d_ref[units, :] = slope.astype(BF16)
        total = total + jnp.dot(down_t[:, units], hidden, preferred_element_type=F32)
    s2_ref[...] = transposed(total) if natural else total


def forward_block(natural, stream, conv_two, gate_two, w_out, ff, gain, bias):
    width, length = stream.shape
    channels = w_out.shape[0]
    hidden = len(ff) * ff.arrays[0].shape[0] * ff.rows // 2
    t = token_tile(length)
    tall = pl.BlockSpec((t, width), lambda i: (i, 0))
    flat = pl.BlockSpec((width, t), lambda i: (0, i))
    chan = pl.BlockSpec((channels, t), lambda i: (0, i))
    high = pl.BlockSpec((hidden, t), lambda i: (0, i))
    last = (length, width) if natural else (width, length)
    return pl.pallas_call(
        functools.partial(forward_body, natural, len(ff)),
        grid=(length // t,),
        in_specs=[flat, chan, chan, whole(w_out), whole(gain), whole(bias)] + ff.specs(),
        out_specs=[flat, tall if natural else flat, high, high, tall, chan],
        out_shape=[
            jax.ShapeDtypeStruct((width, length), F32),
            jax.ShapeDtypeStruct(last, F32),
            jax.ShapeDtypeStruct((hidden, length), BF16),
            jax.ShapeDtypeStruct((hidden, length), BF16),
            jax.ShapeDtypeStruct((length, width), BF16),
            jax.ShapeDtypeStruct((channels, length), BF16),
        ],
        scratch_shapes=[pltpu.VMEM((width, channels), BF16), pltpu.VMEM((width, hidden), BF16)],
        compiler_params=params(),
        name="forward_block",
    )(stream, conv_two, gate_two, w_out, gain, bias, *ff.arrays)


def backward_body(natural, ways, gs_ref, d_ref, s1_ref, c_ref, g_ref, wo_ref, gain_ref, *rest):
    ff, rest = rest[:ways], rest[ways:]
    pre_ref, gs1_ref, gc_ref, two_ref, dm_ref, do_ref, gain_out, bias_out, up_n = rest
    width = ff[0].shape[-1]

    @pl.when(pl.program_id(0) == 0)
    def _():
        gain_out[...] = jnp.zeros_like(gain_out)
        bias_out[...] = jnp.zeros_like(bias_out)
        for ref, blocks, part, units in ff_chunks(ff):
            block = ref[blocks, 0:part, :].reshape(units.stop - units.start, width)
            up_n[:, units] = transposed(block).astype(BF16)

    if natural:
        dm_ref[...] = gs_ref[...]
        grad = transposed(gs_ref[...])
    else:
        grad = gs_ref[...]
        dm_ref[...] = transposed(grad).astype(BF16)
    dm = grad.astype(BF16)
    total = None
    for ref, blocks, part, units in ff_chunks(ff):
        down = ref[blocks, part:, :].reshape(units.stop - units.start, width)
        pre = jnp.dot(down, dm, preferred_element_type=F32) * d_ref[units, :].astype(F32)
        pre = pre.astype(BF16)
        pre_ref[units, :] = pre
        total = add(total, jnp.dot(up_n[:, units], pre, preferred_element_type=F32))
    back, gain_part, bias_part = standardise_back(total, gain_ref[...], s1_ref[...])
    gain_out[...] += gain_part
    bias_out[...] += bias_part
    grad = grad + back
    gs1_ref[...] = grad
    do_ref[...] = transposed(grad).astype(BF16)
    gated = jnp.dot(wo_ref[...], grad.astype(BF16), preferred_element_type=F32)
    gated = gated.astype(BF16).astype(F32)
    gc_ref[...] = (gated * g_ref[...].astype(F32)).astype(BF16)
    two_ref[...] = (gated * c_ref[...].astype(F32)).astype(BF16)


def backward_block(natural, grad, slope, s1, conv_two, gate_two, w_out, ff, gain):
    width, length = s1.shape
    channels = w_out.shape[0]
    hidden = slope.shape[0]
    t = token_tile(length)
    tall = pl.BlockSpec((t, width), lambda i: (i, 0))
    flat = pl.BlockSpec((width, t), lambda i: (0, i))
    chan = pl.BlockSpec((channels, t), lambda i: (0, i))
    high = pl.BlockSpec((hidden, t), lambda i: (0, i))
    column = pl.BlockSpec((width, 1), lambda i: (0, 0))
    return pl.pallas_call(
        functools.partial(backward_body, natural, len(ff)),
        grid=(length // t,),
        in_specs=[tall if natural else flat, high, flat, chan, chan]
        + [whole(w_out), whole(gain)]
        + ff.specs(),
        out_specs=[high, flat, chan, chan, tall, tall, column, column],
        out_shape=[
            jax.ShapeDtypeStruct((hidden, length), BF16),
            jax.ShapeDtypeStruct((width, length), F32),
            jax.ShapeDtypeStruct((channels, length), BF16),
            jax.ShapeDtypeStruct((channels, length), BF16),
            jax.ShapeDtypeStruct((length, width), BF16),
            jax.ShapeDtypeStruct((length, width), BF16),
            jax.ShapeDtypeStruct((width, 1), F32),
            jax.ShapeDtypeStruct((width, 1), F32),
        ],
        scratch_shapes=[pltpu.VMEM((width, hidden), BF16)],
        compiler_params=params(),
        name="backward_block",
    )(grad, slope, s1, conv_two, gate_two, w_out, gain, *ff.arrays)


def unproject_body(natural, ways, groups, place_ref, gm_ref, two_ref, s_ref, gs_ref, gain_ref, *rest):
    dense, rest = rest[:ways], rest[ways:]
    out_ref, gain_out, bias_out, pair_t, value_t = rest
    mp, cut, t = two_ref.shape
    width = dense[0].shape[-1]

    @pl.when(pl.program_id(0) == 0)
    def _():
        gain_out[...] = jnp.zeros_like(gain_out)
        bias_out[...] = jnp.zeros_like(bias_out)

        def body(pair, value):
            rows = by_channel(pair, groups).reshape(mp * 2 * cut, width)
            pair_t[...] = transposed(rows).astype(BF16)
            rows = by_channel(value, groups).reshape(mp * cut, width)
            value_t[...] = transposed(rows).astype(BF16)

        first(place_ref[0] == 0, dense, cut, body)

    pair = jnp.concatenate([gm_ref[:, 0:1], two_ref[...][:, None]], axis=1)
    grad = jnp.dot(pair_t[...], pair.reshape(mp * 2 * cut, t), preferred_element_type=F32)
    value = gm_ref[:, 1].reshape(mp * cut, t)
    grad = grad + jnp.dot(value_t[...], value, preferred_element_type=F32)
    back, gain_part, bias_part = standardise_back(grad, gain_ref[...], s_ref[...])
    gain_out[...] += gain_part
    bias_out[...] += bias_part
    result = gs_ref[...] + back
    out_ref[...] = transposed(result) if natural else result


def unproject(natural, groups, place, grad_mixed, grad_two, dense, stream, grad, gain):
    width, length = stream.shape
    mp, cut, _ = grad_two.shape
    t = token_tile(length)
    tall = pl.BlockSpec((t, width), lambda i: (i, 0))
    flat = pl.BlockSpec((width, t), lambda i: (0, i))
    column = pl.BlockSpec((width, 1), lambda i: (0, 0))
    last = (length, width) if natural else (width, length)
    return pl.pallas_call(
        functools.partial(unproject_body, natural, len(dense), groups),
        grid=(length // t,),
        in_specs=[
            SCALARS,
            pl.BlockSpec((mp, 2, cut, t), lambda i: (0, 0, 0, i)),
            pl.BlockSpec((mp, cut, t), lambda i: (0, 0, i)),
            flat,
            flat,
            whole(gain),
        ]
        + dense.specs(),
        out_specs=[tall if natural else flat, column, column],
        out_shape=[
            jax.ShapeDtypeStruct(last, F32),
            jax.ShapeDtypeStruct((width, 1), F32),
            jax.ShapeDtypeStruct((width, 1), F32),
        ],
        scratch_shapes=[
            pltpu.VMEM((width, mp * 2 * cut), BF16),
            pltpu.VMEM((width, mp * cut), BF16),
        ],
        compiler_params=params(),
        name="unproject",
    )(place, grad_mixed, grad_two, stream, grad, gain, *dense.arrays)


GROUP = 8


def spread(out, rows, low, values):
    count = values.shape[0]
    for i in range(count):
        out[i ^ low, rows, :] = values[i]


def by_way(way, ways, a, b):
    if ways == 1:
        return jnp.concatenate([a, b], axis=1)
    return jnp.where(way == 0, a, b)


def early_body(ways, _, place_ref, pre_ref, h_ref, two_ref, gated_ref, n1_ref, n2_ref, dm_ref, do_ref, *outs):
    low = place_ref[1] % GROUP
    width = n2_ref.shape[-1]
    _, count, part, length = pre_ref.shape
    cut = two_ref.shape[1]
    a = jnp.dot(
        two_ref[...].reshape(count * cut, length), n1_ref[...], preferred_element_type=F32
    ).astype(BF16).reshape(count, cut, width)
    b = jnp.dot(
        gated_ref[...].reshape(count * cut, length), do_ref[...], preferred_element_type=F32
    ).astype(BF16).reshape(count, cut, width)
    for w in range(ways):
        rows = by_way(place_ref[0] ^ w, ways, a, b)
        spread(outs[w], slice(2 * part, 2 * part + rows.shape[1]), low, rows)
        for ref, right, begin in ((pre_ref, n2_ref, 0), (h_ref, dm_ref, part)):
            y = jnp.dot(
                ref[w].reshape(count * part, length), right[...], preferred_element_type=F32
            )
            y = y.astype(BF16).reshape(count, part, width)
            spread(outs[w], slice(begin, begin + part), low, y)


def grad_call(body, name, ways, place, mp, rows, width, plain, mixed, fixed, before=()):
    def spec(a, mixed):
        if not mixed:
            shape = (a.shape[0], GROUP) + a.shape[2:]
            return pl.BlockSpec(shape, lambda i, place: (0, i ^ (place[1] // GROUP), 0, 0))
        shape = (GROUP, None) + a.shape[2:]
        zeros = (0,) * (a.ndim - 2)
        runs = a.shape[0] // GROUP

        def index(i, place):
            run = i ^ (place[1] // GROUP)
            return (lax.rem(run, runs), run // runs) + zeros

        return pl.BlockSpec(shape, index)

    def kept(a):
        return pl.BlockSpec(a.shape, lambda i, place: (0, 0), pipeline_mode=pl.Buffered(1))

    out = pl.BlockSpec((GROUP, rows, width), lambda i, place: (i, 0, 0))
    return pl.pallas_call(
        functools.partial(body, ways, len(before)),
        grid_spec=pltpu.PrefetchScalarGridSpec(
            num_scalar_prefetch=1,
            grid=(mp // GROUP,),
            in_specs=[spec(a, False) for a in plain]
            + [spec(a, True) for a in mixed]
            + [kept(a) for a in fixed]
            + [pl.BlockSpec(memory_space=pl.ANY)] * len(before),
            out_specs=[out] * ways,
        ),
        out_shape=[jax.ShapeDtypeStruct((mp, rows, width), BF16)] * ways,
        compiler_params=params(),
        name=name,
    )(place, *plain, *mixed, *fixed, *before)


def early_grads(ways, groups, place, pre, hidden, two, gated, n1, n2, dm, do):
    mp, cut, length = two.shape
    shape = (ways, mp, pre.shape[0] // (ways * mp), length)
    rows = 2 * shape[2] + 2 * cut // ways
    plain = [pre.reshape(shape), hidden.reshape(shape)]
    mixed = [x.reshape(mp // groups, groups, cut, length) for x in (two, gated)]
    width = n1.shape[1]
    return grad_call(
        early_body, "early_grads", ways, place, mp, rows, width, plain, mixed, [n1, n2, dm, do]
    )


def late_body(ways, before, place_ref, gm_ref, n1_ref, *outs):
    outs = outs[before:]
    low = place_ref[1] % GROUP
    count, _, cut, length = gm_ref.shape
    width = n1_ref.shape[-1]
    a, b = (
        jnp.dot(
            gm_ref[:, j].reshape(count * cut, length), n1_ref[...], preferred_element_type=F32
        ).astype(BF16).reshape(count, cut, width)
        for j in range(2)
    )
    for w in range(ways):
        rows = by_way(place_ref[0] ^ w, ways, a, b)
        spread(outs[w], slice(0, rows.shape[1]), low, rows)


def late_grads(ways, groups, place, grad_mixed, n1, before=()):
    mp, _, cut, length = grad_mixed.shape
    rows = 2 * cut // ways
    width = n1.shape[1]
    mixed = [grad_mixed.reshape(mp // groups, groups, 2, cut, length)]
    return grad_call(
        late_body, "late_grads", ways, place, mp, rows, width, [], mixed, [n1], before
    )


def together(*arrays):
    return lax.optimization_barrier(arrays)


def flip(x, axis, size, bit):
    return lax.ppermute(x, axis, [(i, i ^ bit) for i in range(size)])


def butterfly(x, sizes):
    for axis, size in sizes:
        bit = 1
        while bit < size:
            x = x + flip(x, axis, size, bit)
            bit *= 2
    return x


def stage_order(mp, swapped):
    bits = list(range(mp.bit_length() - 1))
    first = [1, 0] if swapped else [0, 1]
    return first + bits[2:]


def total(parts):
    value = parts[0].astype(F32)
    for part in parts[1:]:
        value = value + part.astype(F32)
    return value


class Hop:
    def __init__(self, x, axis, size, bit):
        self.args = x, axis, size, bit

    def start(self):
        return flip(*self.args)


def scatter_chain(terms, mp, order):
    bits = mp.bit_length() - 1
    terms = [t.reshape((2,) * bits + t.shape[1:]) for t in terms]
    left = list(range(bits - 1, -1, -1))
    for bit in order:
        axis = left.index(bit)
        left.remove(bit)
        take = lambda t, k: lax.index_in_dim(t, k, axis, keepdims=False)
        sent = total([take(t, 1) for t in terms]).astype(BF16)
        got = yield Hop(sent, "mp", mp, 1 << bit)
        terms = [take(t, 0) for t in terms] + [got]
    return total(terms)


def gather_chain(x, mp, order):
    me = lax.axis_index("mp")
    done = []
    for bit in order:
        got = yield Hop(x, "mp", mp, 1 << bit)
        upper = (me >> bit) % 2 == 1
        axis = sum(b > bit for b in done)
        x = jnp.stack([jnp.where(upper, got, x), jnp.where(upper, x, got)], axis=axis)
        done.append(bit)
    return x.reshape((mp,) + x.shape[len(done) :])


def chip_chain(pieces, dp):
    if len(pieces) == 1:
        return pieces
    got = yield Hop(pieces[1], "dp", dp, 1)
    return [pieces[0], got]


def spread_chain(x, ways, dp):
    if ways == 1:
        x = yield from sum_chain(x, [("dp", dp)])
        return (x.astype(BF16),)
    x = x.astype(BF16)
    got = yield Hop(x, "dp", dp, 1)
    zero = lax.axis_index("dp") == 0
    return jnp.where(zero, x, got), jnp.where(zero, got, x)


def sum_chain(x, sizes):
    for axis, size in sizes:
        bit = 1
        while bit < size:
            x = x + (yield Hop(x, axis, size, bit))
            bit *= 2
    return x


class Chains:
    def __init__(self):
        self.waiting, self.results = {}, {}

    def add(self, name, chain):
        self.step(name, chain, None)

    def step(self, name, chain, value):
        try:
            self.waiting[name] = chain, chain.send(value)
        except StopIteration as end:
            self.waiting.pop(name, None)
            self.results[name] = end.value

    def operands(self):
        return [hop.args[0] for _, hop in self.waiting.values()]

    def start(self):
        names = list(self.waiting)
        return names, [self.waiting[n][1].start() for n in names]

    def finish(self, started, *others):
        names, got = started
        tied = together(*got, *others)
        for name, value in zip(names, tied):
            self.step(name, self.waiting[name][0], value)
        return tied[len(names) :]


def gathered_sum(terms, whole_rows, dp):
    y = lax.psum_scatter(total(terms).astype(BF16), "mp", scatter_dimension=0, tiled=True)[0]
    if whole_rows:
        y = butterfly(y.astype(F32), [("dp", dp)]).astype(BF16)
    return y


def program(dp, mp, inputs, cotangent, norm_gain, norm_bias, in_weight, kernels, *rest):
    out_weight, up_weight, down_weight, taps_kept = rest
    layers = in_weight.shape[0]
    groups, chunk, width = inputs.shape
    peers = mp // groups
    shard, hidden = in_weight.shape[3], up_weight.shape[2]
    length = groups * chunk
    cut = -(-shard // 16) * 16
    ways = 2 if dp == 2 and shard == cut and hidden % 32 == 0 else 1
    part = hidden // ways
    dense_rows = 4 * cut // ways
    me, way = lax.axis_index("mp"), lax.axis_index("dp")
    place = jnp.stack([way, me]).astype(jnp.int32)
    still = jnp.stack([way, jnp.zeros_like(me)]).astype(jnp.int32)
    zero_half = me // peers == 0
    swap = [(i, (i + peers) % mp) for i in range(mp)]
    halves = [[h * peers + q for q in range(peers)] for h in range(groups)]

    def ordered(own, got):
        return jnp.stack([jnp.where(zero_half, own, got), jnp.where(zero_half, got, own)])

    def pick(x):
        return jnp.where(zero_half, x[0], x[1]), jnp.where(zero_half, x[1], x[0])

    def to_one_sequence(x):
        own, other = pick(x)
        return ordered(own, lax.ppermute(other, "mp", swap)).reshape(length, width)

    def to_two_sequences(x):
        own, other = pick(x.reshape(groups, chunk, width))
        got = lax.ppermute(other.astype(BF16), "mp", swap)
        return ordered(own, got.astype(F32))

    def exchange(x):
        return lax.all_to_all(
            x, "mp", split_axis=0, concat_axis=0, tiled=True, axis_index_groups=halves
        )

    def widen(x, axis):
        pads = [(0, 0)] * x.ndim
        pads[axis] = (0, cut - shard)
        return x if cut == shard else jnp.pad(x, pads)

    dense = [jnp.transpose(in_weight[:, :, j], (0, 2, 1)) for j in range(3)] + [out_weight]
    dense = jnp.concatenate([widen(d, 1) for d in dense], axis=1)
    up = jnp.transpose(up_weight, (0, 2, 1))

    def my_rows(x, rows):
        return lax.dynamic_slice_in_dim(x, way * rows, rows, 1) if ways > 1 else x

    dense = my_rows(dense, dense_rows)
    ff = jnp.concatenate([my_rows(up, part), my_rows(down_weight, part)], axis=1)

    def gather(x):
        x = lax.all_gather(x, "mp", axis=0)
        return [x, flip(x, "dp", dp, 1)] if ways > 1 else [x]

    def gathered(x):
        return lax.all_gather(x, "mp", axis=0)

    def shared(x):
        return [x, flip(x, "dp", dp, 1)] if ways > 1 else [x]

    stream = to_one_sequence(inputs)
    def out_matrix(pieces):
        begin = pieces.begin + dense_rows - cut
        rows = [a[:, begin : begin + cut] for a in pieces.arrays]
        rows = jnp.where(way == 1, rows[0], rows[1]) if ways > 1 else rows[0]
        rows = rows.reshape(groups, peers, cut, width)
        return jnp.swapaxes(rows, 0, 1).reshape(mp * cut, width)

    keep = jnp.arange(kernels.shape[-1])[None, :] < taps_kept[:, None]
    kept = jnp.where(keep[:, None, None, :], kernels, jnp.zeros_like(kernels))
    kept = widen(kept, 2)
    taps = []

    chains = Chains()
    for i in range(2):
        rows = ff[0, i * part : (i + 1) * part]
        chains.add(i, gather_chain(rows, mp, stage_order(mp, i)[::-1]))
    chains.finish(chains.start())
    dense_mine = gathered(dense[0])
    dense_mine, stream = chains.finish(chains.start(), dense_mine, stream)
    dense_all = [Pieces(shared(dense_mine), 0, dense_rows)]
    ff_all = []

    gains = norm_gain[..., None]
    biases = norm_bias[..., None]
    saved, out_all = [], []
    for layer in range(layers):
        natural = layer == 0
        more = layer + 1 < layers
        if natural:
            started = chains.start()
        got = project(
            natural,
            groups,
            place,
            stream,
            dense_all[layer],
            gains[layer, 0],
            biases[layer, 0],
            cut,
        )
        if natural:
            stream, got = got[0], got[1:]
        operand, gate_two, normed_one = got
        out_all.append(out_matrix(dense_all[layer]))
        if natural:
            (operand,) = chains.finish(started, operand)
            started = chains.start()
        if more:
            mine, operand = together(dense[layer + 1], operand)
            dense_mine = gathered(mine)
        if natural:
            mine, operand = together(kept[layer], operand)
            got_taps = lax.ppermute(mine, "mp", swap)
        gates = exchange(operand.reshape(peers, groups, 2, cut, length))
        if natural:
            while len(chains.waiting):
                gates, got_taps = chains.finish(started, gates, got_taps)
                started = chains.start()
            ff_mine = jnp.concatenate([chains.results.pop(i) for i in range(2)], axis=1)
            ff_pair = shared(ff_mine)
        taps.append(ordered(kept[layer], got_taps))
        conv_two, conv_one, carried = mix(gates, taps[layer])
        if natural:
            conv_two, *ff_pair = together(conv_two, *ff_pair)
        else:
            ff_mine, conv_two = together(ff_mine, conv_two)
            ff_pair = shared(ff_mine)
        ff_all.append(Pieces(ff_pair, 0, 2 * part))
        if more:
            mine, conv_two = together(ff[layer + 1], conv_two)
            ff_mine = gathered(mine)
        conv_two = exchange(conv_two).reshape(mp * cut, length)
        if natural:
            grad, conv_two = together(cotangent, conv_two)
            grad = to_one_sequence(grad)
        if more:
            dense_mine, mine, conv_two = together(dense_mine, kept[layer + 1], conv_two)
            got_taps = lax.ppermute(mine, "mp", swap)
            dense_all.append(Pieces(shared(dense_mine), 0, dense_rows))
        gate_two = gate_two.reshape(mp * cut, length)
        s1, s2, active, slope, normed_two, gated = forward_block(
            layer == layers - 1,
            stream,
            conv_two,
            gate_two,
            out_all[layer],
            ff_all[layer],
            gains[layer, 1],
            biases[layer, 1],
        )
        if more:
            s2, grad, got_taps, *arrays = together(s2, grad, got_taps, *dense_all[-1].arrays)
            dense_all[-1].arrays = arrays
        saved.append(
            (stream, normed_one, gates, conv_one, carried, conv_two, gate_two)
            + (s1, active, slope, normed_two, gated)
        )
        stream = s2
    own_output, other = pick(stream.reshape(groups, chunk, width))
    got_output = lax.ppermute(other.astype(BF16), "mp", swap)

    gain_rows, bias_rows = [None] * layers, [None] * layers
    early_out, late_out, dks = [None] * layers, [None] * layers, [None] * layers
    later = None
    for layer in reversed(range(layers)):
        (s0, normed_one, gates, conv_one, carried, conv_two, gate_two) = saved[layer][:7]
        (s1, active, slope, normed_two, gated) = saved[layer][7:]
        pre, grad, grad_conv, grad_two, dm, do, gain_two, bias_two = backward_block(
            layer == layers - 1,
            grad,
            slope,
            s1,
            conv_two,
            gate_two,
            out_all[layer],
            ff_all[layer],
            gains[layer, 1],
        )
        waiting = []
        if later is not None:
            mixed, grad_conv = together(later[0], grad_conv)
            waiting = late_grads(ways, groups, place, mixed, later[1])
        grad_conv = exchange(grad_conv.reshape(peers, groups, cut, length))
        grad_two = grad_two.reshape(mp, cut, length)
        where_to = still if layer else place
        early = early_grads(
            ways, groups, where_to, pre, active, grad_two, gated, normed_one, normed_two, dm, do
        )
        if layer == layers - 1:
            grad_conv, got_output = together(grad_conv, got_output)
        else:
            grad_conv, got_dk = together(grad_conv, got_dk)
            dks[layer + 1] = own_dk.astype(F32) + got_dk.astype(F32)
        grad_conv, *both = together(grad_conv, *early, *waiting)
        early, waiting = both[:ways], both[ways:]
        chains.add("early", chip_chain(early, dp))
        if later is not None:
            chains.add("waiting", chip_chain(waiting, dp))
        started = chains.start()
        grad_mixed, dk = unmix(grad_conv, gates, conv_one, carried, taps[layer])
        (grad_mixed,) = chains.finish(started, grad_mixed)
        grad_mixed = exchange(grad_mixed).reshape(mp, 2, cut, length)
        own_dk, other_dk = pick(dk.astype(BF16))
        got_dk = lax.ppermute(other_dk, "mp", swap)
        early = chains.results["early"]
        gain_rows[layer], bias_rows[layer] = [None, gain_two], [None, bias_two]
        if layer:
            early_out[layer] = gathered_sum(early, ways == 1, dp)
            if later is not None:
                late_out[layer + 1] = gathered_sum(chains.results["waiting"], ways == 1, dp)
            later = grad_mixed, normed_one
        else:
            if later is not None:
                pairs = zip(early, chains.results["waiting"])
                early = [jnp.concatenate(pair, axis=1) for pair in pairs]
            rows = early[0].shape[1]
            middle = rows // 32 * 16
            spans = ((0, middle), (middle, rows))
            for i, (a, b) in enumerate(spans):
                terms = [e[:, a:b] for e in early]
                chains.add(i, scatter_chain(terms, mp, stage_order(mp, i)))
            before = chains.operands()
            started = chains.start()
            late = late_grads(ways, groups, place, grad_mixed, normed_one, before)
            got_dk, grad_mixed, *late = chains.finish(started, got_dk, grad_mixed, *late)
            dks[0] = own_dk.astype(F32) + got_dk.astype(F32)
            dk = jnp.stack(dks)
            chains.add("late", chip_chain(late, dp))
            chains.add("dk", sum_chain(dk.astype(BF16).astype(F32), [("dp", dp)]))
            started = chains.start()
        grad, gain_one, bias_one = unproject(
            layer == 0,
            groups,
            place,
            grad_mixed,
            grad_two,
            dense_all[layer],
            s0,
            grad,
            gains[layer, 0],
        )
        gain_rows[layer][0], bias_rows[layer][0] = gain_one, bias_one
    grad, gain_rows[0][0] = chains.finish(started, grad, gain_rows[0][0])
    own, other = pick(grad.reshape(groups, chunk, width))
    swapped = lax.ppermute(other.astype(BF16), "mp", swap)
    norms = jnp.stack([jnp.stack([jnp.stack(r) for r in rows]) for rows in (gain_rows, bias_rows)])
    chains.add("norms", sum_chain(norms[..., 0], [("dp", dp), ("mp", mp)]))
    chains.add("late", scatter_chain(chains.results.pop("late"), mp, stage_order(mp, 0)))
    while chains.waiting:
        chains.finish(chains.start())
        if 0 in chains.results and 1 in chains.results:
            rest = jnp.concatenate([chains.results.pop(i) for i in range(2)], axis=0)
            chains.add("rest", spread_chain(rest, ways, dp))
        if "late" in chains.results:
            chains.add("last", spread_chain(chains.results.pop("late"), ways, dp))
    input_grad = ordered(own, swapped.astype(F32))
    output = ordered(own_output, got_output.astype(F32))
    dk = chains.results["dk"][:, :, :shard]
    tap_out = jnp.where(keep[:, None, None, :], dk, 0.0)
    norms = chains.results["norms"]

    def both_ways(x):
        if ways == 1:
            return (x.astype(F32),)
        got = flip(x, "dp", dp, 1)
        pair = jnp.where(way == 0, x, got), jnp.where(way == 0, got, x)
        return tuple(p.astype(F32) for p in pair)

    rest = [x.astype(F32) for x in chains.results["rest"]]
    tall = 2 * part + 2 * cut // ways
    early_out = [[r[:tall] for r in rest]] + [both_ways(e) for e in early_out[1:]]
    late_out[0] = [x.astype(F32) for x in chains.results["last"]]
    if layers > 1:
        late_out[1] = [r[tall:] for r in rest]
    late_out[2:] = [both_ways(x) for x in late_out[2:]]

    parts = [[] for _ in range(6)]
    for early, late in zip(early_out, late_out):
        if ways == 1:
            e, l = early[0], late[0]
            up, down = e[:part], e[part : 2 * part]
            two, out = e[2 * part : 2 * part + cut], e[2 * part + cut :]
            one, value = l[:cut], l[cut:]
        else:
            up = jnp.concatenate([e[:part] for e in early], axis=0)
            down = jnp.concatenate([e[part : 2 * part] for e in early], axis=0)
            two, out = early[0][2 * part :], early[1][2 * part :]
            one, value = late
        for store, x in zip(parts, (one, two, value, out, up, down)):
            store.append(x)
    one, two, value, out, up, down = (jnp.stack(p) for p in parts)
    in_out = jnp.stack([one, two, value], axis=1)[:, :, :shard]
    return (
        output,
        input_grad,
        norms[0],
        norms[1],
        jnp.transpose(in_out, (0, 3, 1, 2)),
        tap_out,
        out[:, :shard],
        jnp.transpose(up, (0, 2, 1)),
        down,
    )


def solution(mesh):
    sizes = dict(mesh.shape)
    specs = (
        P("dp", "mp", None),
        P("dp", "mp", None),
        P(),
        P(),
        P(None, None, None, "mp"),
        P(None, None, "mp", None),
        P(None, "mp", None),
        P(None, None, "mp"),
        P(None, "mp", None),
    )
    return jax.shard_map(
        functools.partial(program, sizes["dp"], sizes["mp"]),
        mesh=mesh,
        in_specs=specs + (P(),),
        out_specs=specs,
        check_vma=False,
    )
```

time: 4740 us -> 1000 us (0.21)
  local copies, waits for them, and re-layouts: 3380 us -> 59.9 us
  matrix products: 506 us -> 0 us
  other arithmetic: 404 us -> 84.7 us
  Pallas kernels: 0 us -> 301 us
  waiting for transfers between devices: 259 us -> 420 us
  blocking collectives: 59 us -> 0 us
    reshape x12 -> x0, local copies, waits for them, and re-layouts: 1420 us -> none  [the longest x4 1100 us: toeplitz(): skewed.reshape(lead + (tap_blocks + 1, window, 2 * window - 1))]
    unnamed x366 -> x190, local copies, waits for them, and re-layouts: 842 us -> 17.1 us
    dot_general x36 -> x0, matrix products: 506 us -> none  [the longest x4 109 us: causal_back(): jnp.einsum('csia,csnib->cnab', grad_blocks, behind, preferred_element_typ...]
    pad x6 -> x0, local copies, waits for them, and re-layouts: 491 us -> none  [the longest x2 277 us: toeplitz(): skewed = flat[..., window - 1:window - 1 + (2 * window - 1) * window]]
    pallas_call x0 -> x16, Pallas kernels: none -> 301 us  [the longest x2 62.4 us: forward_block(): pl.pallas_call(functools.partial(forward_body, natural, len(ff)), grid=(l...]
    ppermute x0 -> x45, waiting for transfers between devices: none -> 230 us  [the longest x37 166 us: flip(): return lax.ppermute(x, axis, [(i, i ^ bit) for i in range(size)])]
    slice x14 -> x8, local copies, waits for them, and re-layouts: 157 us -> 6.03 us  [the longest x4 5.87 us: scatter_chain(): take = lambda t, k: lax.index_in_dim(t, k, axis, keepdims=False)]
    another operation x29 -> x50, other arithmetic: 180 us -> 33.8 us  [the longest x12 13.6 us: ordered(): jnp.stack([jnp.where(zero_half, own, got), jnp.where(zero_half, got, own)])]
  transfers between devices with their start and end apart: 25 -> 57, of which waited for: 6 -> 30; matrix products, arithmetic and copies ran while one was open for 85% -> 11% of each run, Pallas kernels for 0% -> 24%
where the time goes in v1:
time: 1000 us; the launch traced here: 994 us
  waiting for transfers between devices  420 us (42%)
  Pallas kernels  301 us (30%)
  starting transfers between devices  112 us (11%)
  other arithmetic  84.7 us (8%)
  local copies, waits for them, and re-layouts  59.9 us (6%)
  between operations  15.7 us (2%)
    ppermute x37, waiting for transfers between devices, flip(): return lax.ppermute(x, axis, [(i, i ^ bit) for i in range(size)])  166 us
    all_to_all x8, waiting for transfers between devices, exchange(): lax.all_to_all(x, 'mp', split_axis=0, concat_axis=0, tiled=True, axis_ind...  134 us
    pallas_call x2, Pallas kernels, forward_block(): pl.pallas_call(functools.partial(forward_body, natural, len(ff)), grid=(l...  62.4 us
    pallas_call x2, Pallas kernels, backward_block(): pl.pallas_call(functools.partial(backward_body, natural, len(ff)), grid=(...  55.8 us
    pallas_call x4, Pallas kernels, grad_call(): pl.pallas_call(functools.partial(body, ways, len(before)), grid_spec=pltp...  55.2 us
    all_to_all x8, starting transfers between devices, exchange(): lax.all_to_all(x, 'mp', split_axis=0, concat_axis=0, tiled=True, axis_ind...  55 us
    all_gather x3, waiting for transfers between devices, gathered(): return lax.all_gather(x, 'mp', axis=0)  49.9 us
    pallas_call x2, Pallas kernels, unmix(): pl.pallas_call(functools.partial(unmix_body, (q, g, pieces, blocks)), gri...  49.5 us
  transfers between devices with their start and end apart: 57, of which 30 were waited for; matrix products, arithmetic and copies ran while one was open for 11% of the time, Pallas kernels for 24%

profile of v1, /device:TPU:1, one launch (start us, length us, event | category | flops | bytes accessed | tf_op | source)
XLA Modules:
  0.0 993.8 jit_solution(11719835643437897531)
XLA Ops:
  17.8 43.5 %collective-permute-done = bf16[96,768]{1,0:T(8,128)(2,1)S(1)} collective-permute-done((bf16[96,768]{1,0:T(8,128)(2,1)S(1)}, bf16[96,768]{1,0:T(8,128)(2,1)S(1)}, u32[]{:S(2)}, u32[]{:S(2)}) %collective-permute-start) | collective-permute-done | bytes 147488 | tf_op jit(solution)/shard_map/ppermute | solution.py:880
  85.7 24.2 %all-gather.6.cloned.1.call-done.rest_0_ = bf16[16,96,768]{2,1,0:T(8,128)(2,1)} async-done(((bf16[1,96,768]{2,1,0:T(8,128)(2,1)}), bf16[16,96,768]{2,1,0:T(8,128)(2,1)}) %all-gather.6.cloned.1.call-update) | async-done | bytes 2359312 | tf_op jit(solution)/shard_map/all_gather | solution.py:1059
  142.0 35.1 %collective-permute-done.10 = bf16[2,48,2048]{2,1,0:T(8,128)(2,1)S(1)} collective-permute-done((bf16[2,48,2048]{2,1,0:T(8,128)(2,1)S(1)}, bf16[2,48,2048]{2,1,0:T(8,128)(2,1)S(1)}, u32[]{:S(2)}, u32[]{:S(2)}) %collective-permute-start.10) | collective-permute-done | bytes 393248 | tf_op jit(solution)/shard_map/ppermute | solution.py:1117
  177.1 18.7 %collective-permute-done.9 = bf16[2,2,2,96,768]{4,3,0,1,2:T(8,128)(2,1)S(1)} collective-permute-done((bf16[2,2,2,96,768]{4,3,0,1,2:T(8,128)(2,1)S(1)}, bf16[2,2,2,96,768]{4,3,0,1,2:T(8,128)(2,1)S(1)}, u32[]{:S(2)}, u32[]{:S(2)}) %collective-permute-start.9) | collective-permute-done | bytes 1179680 | tf_op jit(solution)/shard_map/ppermute | solution.py:880
  213.2 16.0 %mix.2 = (bf16[8,2,48,1024]{3,2,1,0:T(8,128)(2,1)}, bf16[2,64,48,128]{3,2,1,0:T(8,128)(2,1)}, bf16[2,64,48,128]{3,2,1,0:T(8,128)(2,1)}) custom-call(bf16[8,2,2,48,1024]{4,3,2,1,0:T(8,128)(2,1)} %copy-done.3, bf16[8,2,2,48,1024]{4,3,2,1,0:T(8,128)(2,1)} %copy-done.3, bf16[2,2,48,2048]{3,2,1,0:T(8,128)(2,1)} %pad_maximum_fusion.12.k_ref, ...), custom_call_target="tpu_custom_call" | custom-call | tf_op jit(solution)/shard_map/mix/pallas_call | solution.py:359
  233.6 23.2 %all-to-all-done.1 = bf16[8,2,48,1024]{3,2,1,0:T(8,128)(2,1)S(1)} async-done(((bf16[8,2,48,1024]{3,2,1,0:T(8,128)(2,1)}), bf16[8,2,48,1024]{3,2,1,0:T(8,128)(2,1)S(1)}, u32[]{:S(2)}, u32[]{:S(2)}) %all-to-all-start.1) | async-done | bytes 1572896 | tf_op jit(solution)/shard_map/all_to_all | solution.py:1035
  256.8 25.7 %all-gather.8.cloned.1.call-done = bf16[1536,768]{1,0:T(8,128)(2,1)} async-done(((bf16[96,768]{1,0:T(8,128)(2,1)}), bf16[1536,768]{1,0:T(8,128)(2,1)}) %all-gather.8.cloned.1.call-update) | async-done | bytes 2359312 | tf_op jit(solution)/shard_map/all_gather | solution.py:1059
  294.0 31.3 %forward_block.2 = (f32[768,1024]{1,0:T(8,128)}, f32[768,1024]{1,0:T(8,128)}, bf16[3072,1024]{1,0:T(8,128)(2,1)}, bf16[3072,1024]{1,0:T(8,128)(2,1)}, bf16[1024,...) custom-call(f32[768,1024]{1,0:T(8,128)} %get-tuple-element.152.s_ref, bf16[768,1024]{1,0:T(8,128)(2,1)} %bitcast.373, ...), custom_call_target="tpu_custom_call" | custom-call | tf_op jit(solution)/shard_map/forward_block/pallas_call | solution.py:608
  361.5 54.0 %all-to-all-done.2.v_ref.g_ref = bf16[8,2,2,48,1024]{4,3,2,1,0:T(8,128)(2,1)S(1)} async-done(((bf16[8,2,2,48,1024]{4,3,2,1,0:T(8,128)(2,1)}), bf16[8,2,2,48,1024]{4,3,2,1,0:T(8,128)(2,1)S(1)}, u32[]{:S(2)}, u32[]{:S(2)}) %all-to-all-start.2) | async-done | bytes 3145760 | tf_op jit(solution)/shard_map/all_to_all | solution.py:1035
  417.1 16.0 %mix.3 = (bf16[8,2,48,1024]{3,2,1,0:T(8,128)(2,1)}, bf16[2,64,48,128]{3,2,1,0:T(8,128)(2,1)}, bf16[2,64,48,128]{3,2,1,0:T(8,128)(2,1)}) custom-call(bf16[8,2,2,48,1024]{4,3,2,1,0:T(8,128)(2,1)} %copy-done.2, bf16[8,2,2,48,1024]{4,3,2,1,0:T(8,128)(2,1)} %copy-done.2, bf16[2,2,48,2048]{3,2,1,0:T(8,128)(2,1)} %pad_maximum_fusion.13.k_ref, ...), custom_call_target="tpu_custom_call" | custom-call | tf_op jit(solution)/shard_map/mix/pallas_call | solution.py:359
  434.5 15.1 %all-to-all-start.3 = ((bf16[8,2,48,1024]{3,2,1,0:T(8,128)(2,1)}), bf16[8,2,48,1024]{3,2,1,0:T(8,128)(2,1)}, u32[]{:S(2)}, u32[]{:S(2)}) async-start(bf16[8,2,48,1024]{3,2,1,0:T(8,128)(2,1)} %get-tuple-element.186), calls=%async_computation.3 | async-start | bytes 3145728 | tf_op jit(solution)/shard_map/all_to_all | solution.py:1035
  454.0 16.5 %all-to-all-done.3 = bf16[8,2,48,1024]{3,2,1,0:T(8,128)(2,1)} async-done(((bf16[8,2,48,1024]{3,2,1,0:T(8,128)(2,1)}), bf16[8,2,48,1024]{3,2,1,0:T(8,128)(2,1)}, u32[]{:S(2)}, u32[]{:S(2)}) %all-to-all-start.3) | async-done | bytes 1572896 | tf_op jit(solution)/shard_map/all_to_all | solution.py:1035
  470.5 31.1 %forward_block.3 = (f32[768,1024]{1,0:T(8,128)}, f32[1024,768]{1,0:T(8,128)}, bf16[3072,1024]{1,0:T(8,128)(2,1)}, bf16[3072,1024]{1,0:T(8,128)(2,1)}, bf16[1024,...) custom-call(f32[768,1024]{1,0:T(8,128)} %get-tuple-element.179.x_ref.s_ref, bf16[768,1024]{1,0:T(8,128)(2,1)} %bitcast.64.c_ref, ...), custom_call_target="tpu_custom_call" | custom-call | tf_op jit(solution)/shard_map/forward_block/pallas_call | solution.py:608
  501.6 27.9 %backward_block.2 = (bf16[3072,1024]{1,0:T(8,128)(2,1)}, f32[768,1024]{1,0:T(8,128)}, bf16[768,1024]{1,0:T(8,128)(2,1)}, bf16[768,1024]{1,0:T(8,128)(2,1)}, bf16...) custom-call(bf16[1024,768]{1,0:T(8,128)(2,1)} %bitcast.400, ...), custom_call_target="tpu_custom_call" | custom-call | tf_op jit(solution)/shard_map/backward_block/pallas_call | solution.py:676
  536.1 21.0 %early_grads.2 = (bf16[16,240,768]{2,1,0:T(8,128)(2,1)}, bf16[16,240,768]{2,1,0:T(8,128)(2,1)}) custom-call(s32[2]{0:T(128)} %pad_add_fusion.1.place_ref, bf16[2,16,96,1024]{3,2,1,0:T(8,128)(2,1)} %bitcast.404, bf16[2,16,96,1024]{3,2,1,0:T(8,128)(2,1)} %bitcast.403, bf16[8,2,48,1024]{3,2,1,0:T(8,128)(2,1)} %bitcast.395, bf16[8,2,48,1024]{3,2,1,0:T(8,128)(2,1)} %bitcast.414, ...), custom_call_target="tpu_custom_call" | custom-call | tf_op jit(solution)/shard_map/early_grads/pallas_call | solution.py:820
  573.4 24.7 %unmix.2 = (bf16[8,2,2,48,1024]{4,3,2,1,0:T(8,128)(2,1)}, f32[2,2,48,2048]{3,2,1,0:T(8,128)}) custom-call(bf16[8,2,48,1024]{3,2,1,0:T(8,128)(2,1)} %all-to-all-done.4.d_ref, bf16[8,2,2,48,1024]{4,3,2,1,0:T(8,128)(2,1)} %copy-done.2, bf16[8,2,2,48,1024]{4,3,2,1,0:T(8,128)(2,1)} %copy-done.2, bf16[2,64,48,128]{3,2,1,0:T(8,128)(2,1)} %get-tuple-element.208.one_ref, ...), custom_call_target="tpu_custom_call" | custom-call | tf_op jit(solution)/shard_map/unmix/pallas_call | solution.py:386
  610.8 33.0 %all-to-all-done.5 = bf16[8,2,2,48,1024]{4,3,2,1,0:T(8,128)(2,1)S(1)} async-done(((bf16[8,2,2,48,1024]{4,3,2,1,0:T(8,128)(2,1)}), bf16[8,2,2,48,1024]{4,3,2,1,0:T(8,128)(2,1)S(1)}, u32[]{:S(2)}, u32[]{:S(2)}) %all-to-all-start.5) | async-done | bytes 3145760 | tf_op jit(solution)/shard_map/all_to_all | solution.py:1035
  657.8 27.9 %backward_block.3 = (bf16[3072,1024]{1,0:T(8,128)(2,1)}, f32[768,1024]{1,0:T(8,128)}, bf16[768,1024]{1,0:T(8,128)(2,1)}, bf16[768,1024]{1,0:T(8,128)(2,1)}, bf16...) custom-call(f32[768,1024]{1,0:T(8,128)} %get-tuple-element.213.gs_ref, ...), custom_call_target="tpu_custom_call" | custom-call | tf_op jit(solution)/shard_map/backward_block/pallas_call | solution.py:676
  685.8 14.6 %all-to-all-start.6 = ((bf16[8,2,48,1024]{3,2,1,0:T(8,128)(2,1)}), bf16[8,2,48,1024]{3,2,1,0:T(8,128)(2,1)}, u32[]{:S(2)}, u32[]{:S(2)}) async-start(bf16[8,2,48,1024]{3,2,1,0:T(8,128)(2,1)} %bitcast.415), calls=%async_computation.6 | async-start | bytes 3145728 | tf_op jit(solution)/shard_map/all_to_all | solution.py:1035
  709.0 21.3 %early_grads.3 = (bf16[16,240,768]{2,1,0:T(8,128)(2,1)}, bf16[16,240,768]{2,1,0:T(8,128)(2,1)}) custom-call(s32[2]{0:T(128)} %pad_add_fusion.place_ref, bf16[2,16,96,1024]{3,2,1,0:T(8,128)(2,1)} %bitcast.402, bf16[2,16,96,1024]{3,2,1,0:T(8,128)(2,1)} %bitcast.401, bf16[8,2,48,1024]{3,2,1,0:T(8,128)(2,1)} %bitcast.393, bf16[8,2,48,1024]{3,2,1,0:T(8,128)(2,1)} %bitcast.413, ...), custom_call_target="tpu_custom_call" | custom-call | tf_op jit(solution)/shard_map/early_grads/pallas_call | solution.py:820
  741.5 24.8 %unmix.3 = (bf16[8,2,2,48,1024]{4,3,2,1,0:T(8,128)(2,1)}, f32[2,2,48,2048]{3,2,1,0:T(8,128)}) custom-call(bf16[8,2,48,1024]{3,2,1,0:T(8,128)(2,1)} %all-to-all-done.6.d_ref, bf16[8,2,2,48,1024]{4,3,2,1,0:T(8,128)(2,1)} %copy-done.3, bf16[8,2,2,48,1024]{4,3,2,1,0:T(8,128)(2,1)} %copy-done.3, bf16[2,64,48,128]{3,2,1,0:T(8,128)(2,1)} %get-tuple-element.237.one_ref, ...), custom_call_target="tpu_custom_call" | custom-call | tf_op jit(solution)/shard_map/unmix/pallas_call | solution.py:386
  837.8 24.3 %collective-permute-done.22 = bf16[2,2,2,144,768]{4,3,2,1,0:T(8,128)(2,1)} collective-permute-done((bf16[2,2,2,144,768]{4,3,2,1,0:T(8,128)(2,1)}, bf16[2,2,2,144,768]{4,3,2,1,0:T(8,128)(2,1)}, u32[]{:S(2)}, u32[]{:S(2)}) %collective-permute-start.22) | collective-permute-done | bytes 1769504 | tf_op jit(solution)/shard_map/ppermute | solution.py:880
  909.3 17.4 %collective-permute-done.30 = bf16[2,144,768]{2,1,0:T(8,128)(2,1)S(1)} collective-permute-done((bf16[2,144,768]{2,1,0:T(8,128)(2,1)S(1)}, bf16[2,144,768]{2,1,0:T(8,128)(2,1)S(1)}, u32[]{:S(2)}, u32[]{:S(2)}) %collective-permute-start.30) | collective-permute-done | bytes 442400 | tf_op jit(solution)/shard_map/ppermute | solution.py:880
  945.4 13.1 %collective-permute-done.34 = bf16[144,768]{1,0:T(8,128)(2,1)S(1)} collective-permute-done((bf16[144,768]{1,0:T(8,128)(2,1)S(1)}, bf16[144,768]{1,0:T(8,128)(2,1)S(1)}, u32[]{:S(2)}, u32[]{:S(2)}) %collective-permute-start.34) | collective-permute-done | bytes 221216 | tf_op jit(solution)/shard_map/ppermute | solution.py:880
  (456 shorter events, 377.8 us)
Async XLA Ops:
  7.2 102.7 %all-gather.6.cloned.1.call-start = ((), (), s32[]{:S(2)}) async-start(), calls=%async_computation.9 | async-start | bytes 2506752 | tf_op jit(solution)/shard_map/all_gather | solution.py:1059
  10.6 56.5 %collective-permute-start.4 = (bf16[512,768]{1,0:T(8,128)(2,1)S(1)}, bf16[512,768]{1,0:T(8,128)(2,1)}, u32[]{:S(2)}, u32[]{:S(2)}) collective-permute-start(bf16[512,768]{1,0:T(8,128)(2,1)S(1)} %select_bitcast_fusion.5), channel_id=1, source_target_pairs={{0,8},{1,9},{2,10},{3,11},{4,12},{5,13},{6,14},{7,15},{8,0},{9,1},... | collective-permute-start | bytes 2359304 | tf_op jit(solution)/shard_map/ppermute | solution.py:1027
  13.8 47.5 %collective-permute-start = (bf16[96,768]{1,0:T(8,128)(2,1)S(1)}, bf16[96,768]{1,0:T(8,128)(2,1)S(1)}, u32[]{:S(2)}, u32[]{:S(2)}) collective-permute-start(bf16[96,768]{1,0:T(8,128)(2,1)S(1)} %slice_bitcast_fusion.22), channel_id=1, source_target_pairs={{0,8},{1,9},{2,10},{3,11},{4,12},{5,13},{6,14},{7,15},{8,0},{9,1},... | collective-permute-start | bytes 442376 | tf_op jit(solution)/shard_map/ppermute | solution.py:880
  14.9 49.6 %collective-permute-start.1 = (bf16[96,768]{1,0:T(8,128)(2,1)S(1)}, bf16[96,768]{1,0:T(8,128)(2,1)S(1)}, u32[]{:S(2)}, u32[]{:S(2)}) collective-permute-start(bf16[96,768]{1,0:T(8,128)(2,1)S(1)} %dynamic-slice_bitcast_fusion.1), channel_id=1, source_target_pairs={{0,8},{1,9},{2,10},{3,11},{4,12},{5,13},{6,14},{7,15},{8,0},{9,1},... | collective-permute-start | bytes 442376 | tf_op jit(solution)/shard_map/ppermute | solution.py:880
  131.9 70.9 %all-to-all-start = ((bf16[8,2,2,48,1024]{4,3,2,1,0:T(8,128)(2,1)}), bf16[8,2,2,48,1024]{4,3,2,1,0:T(8,128)(2,1)S(1)}, u32[]{:S(2)}, u32[]{:S(2)}) async-start(bf16[8,2,2,48,1024]{4,3,2,1,0:T(8,128)(2,1)} %bitcast.407), calls=%async_computation | async-start | bytes 6291456 | tf_op jit(solution)/shard_map/all_to_all | solution.py:1035
  135.7 146.7 %all-gather.8.cloned.1.call-start = ((), (), s32[]{:S(2)}) async-start(), calls=%async_computation.11 | async-start | bytes 2506752 | tf_op jit(solution)/shard_map/all_gather | solution.py:1059
  137.2 58.6 %collective-permute-start.9 = (bf16[2,2,2,96,768]{4,3,0,1,2:T(8,128)(2,1)S(1)}, bf16[2,2,2,96,768]{4,3,0,1,2:T(8,128)(2,1)S(1)}, u32[]{:S(2)}, u32[]{:S(2)}) collective-permute-start(bf16[2,2,2,96,768]{4,3,0,1,2:T(8,128)(2,1)S(1)} %pad_maximum_fusion.10), channel_id=1, source_target_pairs={{0,2},{1,3},{2,0},{3,1},{4,6},{5,7},{6,4},{7,5},{8,10},{9,11},{10,... | collective-permute-start | bytes 3538952 | tf_op jit(solution)/shard_map/ppermute | solution.py:880
  138.9 63.9 %collective-permute-start.8 = (bf16[2,2,2,96,768]{4,3,0,1,2:T(8,128)(2,1)S(1)}, bf16[2,2,2,96,768]{4,3,0,1,2:T(8,128)(2,1)}, u32[]{:S(2)}, u32[]{:S(2)}) collective-permute-start(bf16[2,2,2,96,768]{4,3,0,1,2:T(8,128)(2,1)S(1)} %pad_maximum_fusion.9), channel_id=1, source_target_pairs={{0,1},{1,0},{2,3},{3,2},{4,5},{5,4},{6,7},{7,6},{8,9},{9,8},{10,11... | collective-permute-start | bytes 3538952 | tf_op jit(solution)/shard_map/ppermute | solution.py:880
  232.8 200.3 %all-gather.10.cloned.1.call-start = ((), (), s32[]{:S(2)}) async-start(), calls=%async_computation.12 | async-start | bytes 5013504 | tf_op jit(solution)/shard_map/all_gather | solution.py:1059
  282.5 62.8 %collective-permute-start.14 = (bf16[16,96,768]{2,1,0:T(8,128)(2,1)}, bf16[16,96,768]{2,1,0:T(8,128)(2,1)}, u32[]{:S(2)}, u32[]{:S(2)}) collective-permute-start(bf16[16,96,768]{2,1,0:T(8,128)(2,1)} %bitcast.369), channel_id=1, source_target_pairs={{0,16},{16,0},{1,17},{17,1},{2,18},{18,2},{3,19},{19,3},{4,20},{20... | collective-permute-start | bytes 7077896 | tf_op jit(solution)/shard_map/ppermute | solution.py:880
  285.2 51.7 %collective-permute-start.12 = (bf16[512,768]{1,0:T(8,128)(2,1)S(1)}, bf16[512,768]{1,0:T(8,128)(2,1)}, u32[]{:S(2)}, u32[]{:S(2)}) collective-permute-start(bf16[512,768]{1,0:T(8,128)(2,1)S(1)} %select_bitcast_fusion.4), channel_id=1, source_target_pairs={{0,8},{1,9},{2,10},{3,11},{4,12},{5,13},{6,14},{7,15},{8,0},{9,1},... | collective-permute-start | bytes 2359304 | tf_op jit(solution)/shard_map/ppermute | solution.py:1027
  293.4 51.8 %collective-permute-start.13 = (bf16[2,48,2048]{2,1,0:T(8,128)(2,1)S(1)}, bf16[2,48,2048]{2,1,0:T(8,128)(2,1)S(1)}, u32[]{:S(2)}, u32[]{:S(2)}) collective-permute-start(bf16[2,48,2048]{2,1,0:T(8,128)(2,1)S(1)} %copy-done.75), channel_id=1, source_target_pairs={{0,8},{1,9},{2,10},{3,11},{4,12},{5,13},{6,14},{7,15},{8,0},{9,1},... | collective-permute-start | bytes 1179656 | tf_op jit(solution)/shard_map/ppermute | solution.py:1142
  355.8 59.6 %all-to-all-start.2 = ((bf16[8,2,2,48,1024]{4,3,2,1,0:T(8,128)(2,1)}), bf16[8,2,2,48,1024]{4,3,2,1,0:T(8,128)(2,1)S(1)}, u32[]{:S(2)}, u32[]{:S(2)}) async-start(bf16[8,2,2,48,1024]{4,3,2,1,0:T(8,128)(2,1)} %bitcast.408), calls=%async_computation.2 | async-start | bytes 6291456 | tf_op jit(solution)/shard_map/all_to_all | solution.py:1035
  529.5 40.2 %all-to-all-start.4 = ((bf16[8,2,48,1024]{3,2,1,0:T(8,128)(2,1)}), bf16[8,2,48,1024]{3,2,1,0:T(8,128)(2,1)}, u32[]{:S(2)}, u32[]{:S(2)}) async-start(bf16[8,2,48,1024]{3,2,1,0:T(8,128)(2,1)} %bitcast.416), calls=%async_computation.4 | async-start | bytes 3145728 | tf_op jit(solution)/shard_map/all_to_all | solution.py:1035
  598.1 45.7 %all-to-all-start.5 = ((bf16[8,2,2,48,1024]{4,3,2,1,0:T(8,128)(2,1)}), bf16[8,2,2,48,1024]{4,3,2,1,0:T(8,128)(2,1)S(1)}, u32[]{:S(2)}, u32[]{:S(2)}) async-start(bf16[8,2,2,48,1024]{4,3,2,1,0:T(8,128)(2,1)} %get-tuple-element.211), calls=%async_computation.5 | async-start | bytes 6291456 | tf_op jit(solution)/shard_map/all_to_all | solution.py:1035
  601.7 189.9 %reduce-scatter.2.cloned.1.call-start = ((), (), s32[]{:S(2)}) async-start(), calls=%async_computation.10 | async-start | bytes 6266880 | tf_op jit(solution)/shard_map/reduce_scatter | solution.py:995
  685.8 44.6 %all-to-all-start.6 = ((bf16[8,2,48,1024]{3,2,1,0:T(8,128)(2,1)}), bf16[8,2,48,1024]{3,2,1,0:T(8,128)(2,1)}, u32[]{:S(2)}, u32[]{:S(2)}) async-start(bf16[8,2,48,1024]{3,2,1,0:T(8,128)(2,1)} %bitcast.415), calls=%async_computation.6 | async-start | bytes 3145728 | tf_op jit(solution)/shard_map/all_to_all | solution.py:1035
  730.3 43.7 %collective-permute-start.19 = (bf16[16,240,768]{2,1,0:T(8,128)(2,1)}, bf16[16,240,768]{2,1,0:T(8,128)(2,1)}, u32[]{:S(2)}, u32[]{:S(2)}) collective-permute-start(bf16[16,240,768]{2,1,0:T(8,128)(2,1)} %get-tuple-element.234), channel_id=1, source_target_pairs={{0,16},{16,0},{1,17},{17,1},{2,18},{18,2},{3,19},{19,3},{4,20},{20... | collective-permute-start | bytes 17694728 | tf_op jit(solution)/shard_map/ppermute | solution.py:880
  769.6 68.2 %collective-permute-start.23 = (bf16[2,48,2048]{2,1,0:T(8,128)(2,1)}, bf16[2,48,2048]{2,1,0:T(8,128)(2,1)}, u32[]{:S(2)}, u32[]{:S(2)}) collective-permute-start(bf16[2,48,2048]{2,1,0:T(8,128)(2,1)} %select_bitcast_fusion.10), channel_id=1, source_target_pairs={{0,8},{1,9},{2,10},{3,11},{4,12},{5,13},{6,14},{7,15},{8,0},{9,1},... | collective-permute-start | bytes 1179656 | tf_op jit(solution)/shard_map/ppermute | solution.py:1208
  775.1 54.5 %all-to-all-start.7 = ((bf16[8,2,2,48,1024]{4,3,2,1,0:T(8,128)(2,1)}), bf16[8,2,2,48,1024]{4,3,2,1,0:T(8,128)(2,1)S(1)}, u32[]{:S(2)}, u32[]{:S(2)}) async-start(bf16[8,2,2,48,1024]{4,3,2,1,0:T(8,128)(2,1)} %get-tuple-element.244), calls=%async_computation.7 | async-start | bytes 6291456 | tf_op jit(solution)/shard_map/all_to_all | solution.py:1035
  802.5 59.6 %collective-permute-start.22 = (bf16[2,2,2,144,768]{4,3,2,1,0:T(8,128)(2,1)}, bf16[2,2,2,144,768]{4,3,2,1,0:T(8,128)(2,1)}, u32[]{:S(2)}, u32[]{:S(2)}) collective-permute-start(bf16[2,2,2,144,768]{4,3,2,1,0:T(8,128)(2,1)} %fusion.1.outs_1_), channel_id=1, source_target_pairs={{0,2},{1,3},{2,0},{3,1},{4,6},{5,7},{6,4},{7,5},{8,10},{9,11},{10,... | collective-permute-start | bytes 5308424 | tf_op jit(solution)/shard_map/ppermute | solution.py:880
  807.5 54.6 %collective-permute-start.21 = (bf16[2,2,2,144,768]{4,3,1,0,2:T(8,128)(2,1)}, bf16[2,2,2,144,768]{4,3,1,0,2:T(8,128)(2,1)}, u32[]{:S(2)}, u32[]{:S(2)}) collective-permute-start(bf16[2,2,2,144,768]{4,3,1,0,2:T(8,128)(2,1)} %fusion), channel_id=1, source_target_pairs={{0,1},{1,0},{2,3},{3,2},{4,5},{5,4},{6,7},{7,6},{8,9},{9,8},{10,11... | collective-permute-start | bytes 5308424 | tf_op jit(solution)/shard_map/ppermute | solution.py:880
  893.9 42.3 %collective-permute-start.32 = (bf16[2,2,2,48,768]{4,3,1,0,2:T(8,128)(2,1)}, bf16[2,2,2,48,768]{4,3,1,0,2:T(8,128)(2,1)}, u32[]{:S(2)}, u32[]{:S(2)}) collective-permute-start(bf16[2,2,2,48,768]{4,3,1,0,2:T(8,128)(2,1)} %fusion.14), channel_id=1, source_target_pairs={{0,1},{1,0},{2,3},{3,2},{4,5},{5,4},{6,7},{7,6},{8,9},{9,8},{10,11... | collective-permute-start | bytes 1769480 | tf_op jit(solution)/shard_map/ppermute | solution.py:880
  907.9 59.2 %collective-permute-start.28 = (bf16[512,768]{1,0:T(8,128)(2,1)S(1)}, bf16[512,768]{1,0:T(8,128)(2,1)S(1)}, u32[]{:S(2)}, u32[]{:S(2)}) collective-permute-start(bf16[512,768]{1,0:T(8,128)(2,1)S(1)} %select_convert_fusion), channel_id=1, source_target_pairs={{0,8},{1,9},{2,10},{3,11},{4,12},{5,13},{6,14},{7,15},{8,0},{9,1},... | collective-permute-start | bytes 2359304 | tf_op jit(solution)/shard_map/ppermute | solution.py:1249
  (125 other events, 1671.5 us)
Sparse Core Ops, SparseCore 0:
  11.4 98.4 all-gather.5
  211.5 70.8 all-gather.7
  285.8 144.8 all-gather.9
  610.9 180.7 reduce-scatter.1

commit v2 on v1

--- a/solution.py
+++ b/solution.py
@@ -458,15 +458,18 @@
 
 
 class Pieces:
-    def __init__(self, arrays, begin, rows):
-        self.arrays, self.begin, self.rows = arrays, begin, rows
+    def __init__(self, arrays, begins, rows):
+        self.arrays, self.begins, self.rows = arrays, begins, rows
 
     def specs(self):
         mp, _, width = self.arrays[0].shape
-        block = self.begin // self.rows
         shape = (mp, self.rows, width)
-        spec = pl.BlockSpec(shape, lambda *_: (0, block, 0), pipeline_mode=pl.Buffered(1))
-        return [spec] * len(self.arrays)
+        return [
+            pl.BlockSpec(
+                shape, lambda *_, at=begin // self.rows: (0, at, 0), pipeline_mode=pl.Buffered(1)
+            )
+            for begin in self.begins
+        ]
 
     def __len__(self):
         return len(self.arrays)
@@ -515,8 +518,8 @@
     op_ref[:, 1] = y.astype(BF16).reshape(mp, cut, t)
 
 
-def token_tile(length):
-    return min(length, 256)
+def token_tile(length, most=256):
+    return min(length, most)
 
 
 def project(natural, groups, place, x, dense, gain, bias, cut):
@@ -667,7 +670,7 @@
     width, length = s1.shape
     channels = w_out.shape[0]
     hidden = slope.shape[0]
-    t = token_tile(length)
+    t = token_tile(length, 512)
     tall = pl.BlockSpec((t, width), lambda i: (i, 0))
     flat = pl.BlockSpec((width, t), lambda i: (0, i))
     chan = pl.BlockSpec((channels, t), lambda i: (0, i))
@@ -764,112 +767,106 @@
 GROUP = 8
 
 
-def spread(out, rows, low, values):
-    count = values.shape[0]
-    for i in range(count):
-        out[i ^ low, rows, :] = values[i]
-
-
-def by_way(way, ways, a, b):
-    if ways == 1:
-        return jnp.concatenate([a, b], axis=1)
-    return jnp.where(way == 0, a, b)
-
-
-def early_body(ways, _, place_ref, pre_ref, h_ref, two_ref, gated_ref, n1_ref, n2_ref, dm_ref, do_ref, *outs):
+class Plain:
+    def __init__(self, ways, mp, left, right):
+        self.left = left.reshape(ways, mp, left.shape[0] // (ways * mp), left.shape[1])
+        self.rows, self.rights = self.left.shape[2], [right]
+
+    def lefts(self):
+        _, _, part, length = self.left.shape
+        shape = (self.left.shape[0], GROUP, part, length)
+        spec = pl.BlockSpec(shape, lambda i, place: (0, i ^ (place[1] // GROUP), 0, 0))
+        return [(self.left, spec)]
+
+    def pieces(self, way, lefts, rights):
+        ways, count, part, length = lefts[0].shape
+        for w in range(ways):
+            y = rows_product(lefts[0][w].reshape(count * part, length), rights[0])
+            yield y.reshape(count, part, -1)
+
+
+class Mixed:
+    def __init__(self, ways, groups, lefts, rights):
+        self.ways, self.rights = ways, rights
+        self.arrays = [
+            x.reshape((x.shape[0] // groups, groups) + x.shape[1:]) for x in lefts
+        ]
+        self.rows = 2 * self.arrays[0].shape[-2] // ways
+
+    def lefts(self):
+        result = []
+        for x in self.arrays:
+            shape = (GROUP, None) + x.shape[2:]
+            zeros = (0,) * (x.ndim - 2)
+            runs = x.shape[0] // GROUP
+
+            def index(i, place, runs=runs, zeros=zeros):
+                run = i ^ (place[1] // GROUP)
+                return (lax.rem(run, runs), run // runs) + zeros
+
+            result.append((x, pl.BlockSpec(shape, index)))
+        return result
+
+    def pieces(self, way, lefts, rights):
+        if len(lefts) == 1:
+            lefts = [lefts[0].at[:, 0], lefts[0].at[:, 1]]
+        made = []
+        for left, right in zip(lefts, (rights * 2)[:2]):
+            count, cut, length = left.shape
+            y = rows_product(left[...].reshape(count * cut, length), right)
+            made.append(y.reshape(count, cut, -1))
+        a, b = made
+        for w in range(self.ways):
+            if self.ways == 1:
+                yield jnp.concatenate([a, b], axis=1)
+            else:
+                yield jnp.where(way ^ w == 0, a, b)
+
+
+def rows_product(left, right):
+    return jnp.dot(left, right[...], preferred_element_type=F32).astype(BF16)
+
+
+def grads_body(ways, jobs, before, place_ref, *refs):
+    counts = [len(job.lefts()) for job in jobs]
+    lefts, refs = refs[: sum(counts)], refs[sum(counts) :]
+    rights, refs = refs[: sum(len(j.rights) for j in jobs)], refs[sum(len(j.rights) for j in jobs) :]
+    outs = refs[before:]
     low = place_ref[1] % GROUP
-    width = n2_ref.shape[-1]
-    _, count, part, length = pre_ref.shape
-    cut = two_ref.shape[1]
-    a = jnp.dot(
-        two_ref[...].reshape(count * cut, length), n1_ref[...], preferred_element_type=F32
-    ).astype(BF16).reshape(count, cut, width)
-    b = jnp.dot(
-        gated_ref[...].reshape(count * cut, length), do_ref[...], preferred_element_type=F32
-    ).astype(BF16).reshape(count, cut, width)
-    for w in range(ways):
-        rows = by_way(place_ref[0] ^ w, ways, a, b)
-        spread(outs[w], slice(2 * part, 2 * part + rows.shape[1]), low, rows)
-        for ref, right, begin in ((pre_ref, n2_ref, 0), (h_ref, dm_ref, part)):
-            y = jnp.dot(
-                ref[w].reshape(count * part, length), right[...], preferred_element_type=F32
-            )
-            y = y.astype(BF16).reshape(count, part, width)
-            spread(outs[w], slice(begin, begin + part), low, y)
-
-
-def grad_call(body, name, ways, place, mp, rows, width, plain, mixed, fixed, before=()):
-    def spec(a, mixed):
-        if not mixed:
-            shape = (a.shape[0], GROUP) + a.shape[2:]
-            return pl.BlockSpec(shape, lambda i, place: (0, i ^ (place[1] // GROUP), 0, 0))
-        shape = (GROUP, None) + a.shape[2:]
-        zeros = (0,) * (a.ndim - 2)
-        runs = a.shape[0] // GROUP
-
-        def index(i, place):
-            run = i ^ (place[1] // GROUP)
-            return (lax.rem(run, runs), run // runs) + zeros
-
-        return pl.BlockSpec(shape, index)
+    begin = 0
+    for job, count in zip(jobs, counts):
+        mine, lefts = lefts[:count], lefts[count:]
+        right, rights = rights[: len(job.rights)], rights[len(job.rights) :]
+        for out, values in zip(outs, job.pieces(place_ref[0], list(mine), list(right))):
+            for i in range(GROUP):
+                out[i ^ low, begin : begin + job.rows, :] = values[i]
+        begin += job.rows
+
+
+def weight_grads(name, ways, mp, place, jobs, before=()):
+    width = jobs[0].rights[0].shape[1]
+    rows = sum(job.rows for job in jobs)
+    lefts = [pair for job in jobs for pair in job.lefts()]
+    rights = [right for job in jobs for right in job.rights]
 
     def kept(a):
         return pl.BlockSpec(a.shape, lambda i, place: (0, 0), pipeline_mode=pl.Buffered(1))
 
     out = pl.BlockSpec((GROUP, rows, width), lambda i, place: (i, 0, 0))
     return pl.pallas_call(
-        functools.partial(body, ways, len(before)),
+        functools.partial(grads_body, ways, jobs, len(before)),
         grid_spec=pltpu.PrefetchScalarGridSpec(
             num_scalar_prefetch=1,
             grid=(mp // GROUP,),
-            in_specs=[spec(a, False) for a in plain]
-            + [spec(a, True) for a in mixed]
-            + [kept(a) for a in fixed]
+            in_specs=[spec for _, spec in lefts]
+            + [kept(a) for a in rights]
             + [pl.BlockSpec(memory_space=pl.ANY)] * len(before),
             out_specs=[out] * ways,
         ),
         out_shape=[jax.ShapeDtypeStruct((mp, rows, width), BF16)] * ways,
         compiler_params=params(),
         name=name,
-    )(place, *plain, *mixed, *fixed, *before)
-
-
-def early_grads(ways, groups, place, pre, hidden, two, gated, n1, n2, dm, do):
-    mp, cut, length = two.shape
-    shape = (ways, mp, pre.shape[0] // (ways * mp), length)
-    rows = 2 * shape[2] + 2 * cut // ways
-    plain = [pre.reshape(shape), hidden.reshape(shape)]
-    mixed = [x.reshape(mp // groups, groups, cut, length) for x in (two, gated)]
-    width = n1.shape[1]
-    return grad_call(
-        early_body, "early_grads", ways, place, mp, rows, width, plain, mixed, [n1, n2, dm, do]
-    )
-
-
-def late_body(ways, before, place_ref, gm_ref, n1_ref, *outs):
-    outs = outs[before:]
-    low = place_ref[1] % GROUP
-    count, _, cut, length = gm_ref.shape
-    width = n1_ref.shape[-1]
-    a, b = (
-        jnp.dot(
-            gm_ref[:, j].reshape(count * cut, length), n1_ref[...], preferred_element_type=F32
-        ).astype(BF16).reshape(count, cut, width)
-        for j in range(2)
-    )
-    for w in range(ways):
-        rows = by_way(place_ref[0] ^ w, ways, a, b)
-        spread(outs[w], slice(0, rows.shape[1]), low, rows)
-
-
-def late_grads(ways, groups, place, grad_mixed, n1, before=()):
-    mp, _, cut, length = grad_mixed.shape
-    rows = 2 * cut // ways
-    width = n1.shape[1]
-    mixed = [grad_mixed.reshape(mp // groups, groups, 2, cut, length)]
-    return grad_call(
-        late_body, "late_grads", ways, place, mp, rows, width, [], mixed, [n1], before
-    )
+    )(place, *[x for x, _ in lefts], *rights, *before)
 
 
 def together(*arrays):
@@ -878,6 +875,10 @@
 
 def flip(x, axis, size, bit):
     return lax.ppermute(x, axis, [(i, i ^ bit) for i in range(size)])
+
+
+def dp_sum(x, dp):
+    return butterfly(x, [("dp", dp)])
 
 
 def butterfly(x, sizes):
@@ -891,8 +892,8 @@
 
 def stage_order(mp, swapped):
     bits = list(range(mp.bit_length() - 1))
-    first = [1, 0] if swapped else [0, 1]
-    return first + bits[2:]
+    first = [[1], [0]] if swapped else [[0], [1]]
+    return first + [bits[i : i + 2] for i in range(2, len(bits), 2)]
 
 
 def total(parts):
@@ -903,63 +904,132 @@
 
 
 class Hop:
-    def __init__(self, x, axis, size, bit):
-        self.args = x, axis, size, bit
+    def __init__(self, x, axis, size, mask):
+        self.x, self.where = x, (axis, size, mask)
 
     def start(self):
-        return flip(*self.args)
-
-
-def scatter_chain(terms, mp, order):
+        return flip(self.x, *self.where)
+
+
+def masks(bits):
+    return [sum(((k >> i) & 1) << b for i, b in enumerate(bits)) for k in range(1 << len(bits))]
+
+
+def scatter_steps(terms, left, mp, stages):
+    for stage in stages:
+        axes = [left.index(b) for b in stage]
+        left = [b for b in left if b not in stage]
+
+        def take(t, k):
+            index = [slice(None)] * t.ndim
+            for i, axis in enumerate(axes):
+                index[axis] = (k >> i) & 1
+            return t[tuple(index)]
+
+        sums = [
+            total([take(t, k) for t in terms]).astype(BF16) for k in range(1 << len(stage))
+        ]
+        got = yield [Hop(x, "mp", mp, mask) for x, mask in zip(sums[1:], masks(stage)[1:])]
+        terms = sums[:1] + got
+    return terms
+
+
+def scatter_chain(terms, mp, stages, split=False):
     bits = mp.bit_length() - 1
+    left = list(range(bits - 1, -1, -1))
     terms = [t.reshape((2,) * bits + t.shape[1:]) for t in terms]
+    if split:
+        rows = terms[0].shape[-2]
+        middle = (rows // 2 + 15) // 16 * 16
+        orders = stages[:2], stages[1::-1]
+        parts = [
+            scatter_steps([t[..., span, :] for t in terms], left, mp, order)
+            for span, order in zip((slice(0, middle), slice(middle, rows)), orders)
+        ]
+        hops = [next(part) for part in parts]
+        got = yield hops[0] + hops[1]
+        hops = [part.send([x]) for part, x in zip(parts, got)]
+        got = yield hops[0] + hops[1]
+        ended = []
+        for part, x in zip(parts, got):
+            try:
+                part.send([x])
+            except StopIteration as end:
+                ended.append(end.value)
+        terms = [jnp.concatenate(pair, axis=-2) for pair in zip(*ended)]
+        left = [b for b in left if b not in stages[0] + stages[1]]
+        stages = stages[2:]
+    terms = yield from scatter_steps(terms, left, mp, stages)
+    return total(terms)
+
+
+def in_two(x):
+    high = x.astype(BF16)
+    return jnp.concatenate([high, (x - high.astype(F32)).astype(BF16)], axis=0)
+
+
+def from_two(x):
+    half = x.shape[0] // 2
+    return x[:half].astype(F32) + x[half:].astype(F32)
+
+
+def last_chain(terms, norms, mp, stages):
+    bits = mp.bit_length() - 1
     left = list(range(bits - 1, -1, -1))
-    for bit in order:
-        axis = left.index(bit)
-        left.remove(bit)
-        take = lambda t, k: lax.index_in_dim(t, k, axis, keepdims=False)
-        sent = total([take(t, 1) for t in terms]).astype(BF16)
-        got = yield Hop(sent, "mp", mp, 1 << bit)
-        terms = [take(t, 0) for t in terms] + [got]
-    return total(terms)
-
-
-def gather_chain(x, mp, order):
+    terms = [t.reshape((2,) * bits + t.shape[1:]) for t in terms]
+    width = norms.shape[1]
+    for stage in stages:
+        axes = [left.index(b) for b in stage]
+        left = [b for b in left if b not in stage]
+        sums = []
+        for k in range(1 << len(stage)):
+            index = [slice(None)] * terms[0].ndim
+            for i, axis in enumerate(axes):
+                index[axis] = (k >> i) & 1
+            sums.append(total([t[tuple(index)] for t in terms]).astype(BF16))
+        own = in_two(norms)
+        shape, rows = sums[0].shape, sums[0].size // width
+        got = yield [
+            Hop(jnp.concatenate([x.reshape(rows, width), own], axis=0), "mp", mp, mask)
+            for x, mask in zip(sums[1:], masks(stage)[1:])
+        ]
+        terms = sums[:1] + [x[:rows].reshape(shape) for x in got]
+        values = [from_two(x) for x in [own] + [x[rows:] for x in got]]
+        while len(values) > 1:
+            values = [a + b for a, b in zip(values[0::2], values[1::2])]
+        norms = values[0]
+    return total(terms), norms
+
+
+def gather_chain(x, mp, stages):
     me = lax.axis_index("mp")
     done = []
-    for bit in order:
-        got = yield Hop(x, "mp", mp, 1 << bit)
-        upper = (me >> bit) % 2 == 1
-        axis = sum(b > bit for b in done)
-        x = jnp.stack([jnp.where(upper, got, x), jnp.where(upper, x, got)], axis=axis)
-        done.append(bit)
+    for stage in stages:
+        got = yield [Hop(x, "mp", mp, mask) for mask in masks(stage)[1:]]
+        pieces = [x] + got
+        place = sum(((me >> b) & 1) << i for i, b in enumerate(stage))
+        count = len(pieces)
+        if count == 2:
+            pieces = [jnp.where(place == a, x, got[0]) for a in range(2)]
+        else:
+            pieces = [
+                lax.select_n(place, *[pieces[a ^ v] for v in range(count)]) for a in range(count)
+            ]
+        for i, bit in enumerate(stage):
+            axis = sum(b > bit for b in done)
+            pieces = [
+                jnp.stack([pieces[j], pieces[j + 1]], axis=axis) for j in range(0, len(pieces), 2)
+            ]
+            done.append(bit)
+        x = pieces[0]
     return x.reshape((mp,) + x.shape[len(done) :])
 
 
 def chip_chain(pieces, dp):
     if len(pieces) == 1:
         return pieces
-    got = yield Hop(pieces[1], "dp", dp, 1)
-    return [pieces[0], got]
-
-
-def spread_chain(x, ways, dp):
-    if ways == 1:
-        x = yield from sum_chain(x, [("dp", dp)])
-        return (x.astype(BF16),)
-    x = x.astype(BF16)
-    got = yield Hop(x, "dp", dp, 1)
-    zero = lax.axis_index("dp") == 0
-    return jnp.where(zero, x, got), jnp.where(zero, got, x)
-
-
-def sum_chain(x, sizes):
-    for axis, size in sizes:
-        bit = 1
-        while bit < size:
-            x = x + (yield Hop(x, axis, size, bit))
-            bit *= 2
-    return x
+    got = yield [Hop(pieces[1], "dp", dp, 1)]
+    return [pieces[0]] + got
 
 
 class Chains:
@@ -976,26 +1046,29 @@
             self.waiting.pop(name, None)
             self.results[name] = end.value
 
+    def hops(self):
+        return [hop for _, hops in self.waiting.values() for hop in hops]
+
     def operands(self):
-        return [hop.args[0] for _, hop in self.waiting.values()]
+        return [hop.x for hop in self.hops()]
+
+    def tie(self, *others):
+        hops = self.hops()
+        tied = together(*[hop.x for hop in hops], *others)
+        for hop, x in zip(hops, tied):
+            hop.x = x
+        return tied[len(hops) :]
 
     def start(self):
-        names = list(self.waiting)
-        return names, [self.waiting[n][1].start() for n in names]
+        return {name: [hop.start() for hop in hops] for name, (_, hops) in self.waiting.items()}
 
     def finish(self, started, *others):
-        names, got = started
-        tied = together(*got, *others)
-        for name, value in zip(names, tied):
-            self.step(name, self.waiting[name][0], value)
-        return tied[len(names) :]
-
-
-def gathered_sum(terms, whole_rows, dp):
-    y = lax.psum_scatter(total(terms).astype(BF16), "mp", scatter_dimension=0, tiled=True)[0]
-    if whole_rows:
-        y = butterfly(y.astype(F32), [("dp", dp)]).astype(BF16)
-    return y
+        flat = [x for got in started.values() for x in got]
+        tied = list(together(*flat, *others))
+        for name, got in started.items():
+            mine, tied = tied[: len(got)], tied[len(got) :]
+            self.step(name, self.waiting[name][0], mine)
+        return tied
 
 
 def program(dp, mp, inputs, cotangent, norm_gain, norm_bias, in_weight, kernels, *rest):
@@ -1011,7 +1084,6 @@
     dense_rows = 4 * cut // ways
     me, way = lax.axis_index("mp"), lax.axis_index("dp")
     place = jnp.stack([way, me]).astype(jnp.int32)
-    still = jnp.stack([way, jnp.zeros_like(me)]).astype(jnp.int32)
     zero_half = me // peers == 0
     swap = [(i, (i + peers) % mp) for i in range(mp)]
     halves = [[h * peers + q for q in range(peers)] for h in range(groups)]
@@ -1061,10 +1133,12 @@
     def shared(x):
         return [x, flip(x, "dp", dp, 1)] if ways > 1 else [x]
 
-    stream = to_one_sequence(inputs)
     def out_matrix(pieces):
-        begin = pieces.begin + dense_rows - cut
-        rows = [a[:, begin : begin + cut] for a in pieces.arrays]
+        skip = dense_rows - cut
+        rows = [
+            a[:, begin + skip : begin + dense_rows]
+            for a, begin in zip(pieces.arrays, pieces.begins)
+        ]
         rows = jnp.where(way == 1, rows[0], rows[1]) if ways > 1 else rows[0]
         rows = rows.reshape(groups, peers, cut, width)
         return jnp.swapaxes(rows, 0, 1).reshape(mp * cut, width)
@@ -1075,23 +1149,45 @@
     taps = []
 
     chains = Chains()
+    bits = mp.bit_length() - 1
     for i in range(2):
-        rows = ff[0, i * part : (i + 1) * part]
-        chains.add(i, gather_chain(rows, mp, stage_order(mp, i)[::-1]))
-    chains.finish(chains.start())
-    dense_mine = gathered(dense[0])
-    dense_mine, stream = chains.finish(chains.start(), dense_mine, stream)
-    dense_all = [Pieces(shared(dense_mine), 0, dense_rows)]
+        rows = dense[0, i * dense_rows // 2 : (i + 1) * dense_rows // 2]
+        stages = [[b] for b in range(bits - 1, 1, -1)] + [[1 - i], [i]]
+        chains.add(i, gather_chain(rows, mp, stages))
+    own, other = pick(inputs)
+    mine, other = chains.tie(ff[0], other)
+    ff_mine = gathered(mine)
+    (other,) = chains.finish(chains.start(), other)
+    moves = [other[: chunk // 2], other[chunk // 2 :], kept[0]]
+    moved = []
+    while len(moved) < 3:
+        now = moves[len(moved)]
+        started = chains.start()
+        got = lax.ppermute(now, "mp", swap)
+        if len(moved) < 2:
+            got, moves[len(moved) + 1] = chains.finish(started, got, moves[len(moved) + 1])
+        else:
+            (got,) = chains.finish(started, got)
+        moved.append(got)
+    while chains.waiting:
+        chains.finish(chains.start())
+    dense_mine = jnp.concatenate([chains.results.pop(i) for i in range(2)], axis=1)
+    other = jnp.concatenate(moved[:2], axis=0)
+    got_taps = moved[2]
+    stream = ordered(own, other).reshape(length, width)
+    none = [0] * ways
+    dense_all = [Pieces(shared(dense_mine), none, dense_rows)]
     ff_all = []
 
     gains = norm_gain[..., None]
     biases = norm_bias[..., None]
     saved, out_all = [], []
+    own_grad, grad = pick(cotangent)
+    less = chunk // 32 * 12
+    halves_of_grad = [grad[:less], grad[less:]]
     for layer in range(layers):
         natural = layer == 0
         more = layer + 1 < layers
-        if natural:
-            started = chains.start()
         got = project(
             natural,
             groups,
@@ -1105,42 +1201,35 @@
         if natural:
             stream, got = got[0], got[1:]
         operand, gate_two, normed_one = got
-        out_all.append(out_matrix(dense_all[layer]))
         if natural:
-            (operand,) = chains.finish(started, operand)
-            started = chains.start()
+            ff_mine, operand = together(ff_mine, operand)
+            ff_pair = shared(ff_mine)
         if more:
             mine, operand = together(dense[layer + 1], operand)
-            dense_mine = gathered(mine)
+            dense_next = gathered(mine)
+        gates = exchange(operand.reshape(peers, groups, 2, cut, length))
+        taps.append(ordered(kept[layer], got_taps))
         if natural:
-            mine, operand = together(kept[layer], operand)
-            got_taps = lax.ppermute(mine, "mp", swap)
-        gates = exchange(operand.reshape(peers, groups, 2, cut, length))
-        if natural:
-            while len(chains.waiting):
-                gates, got_taps = chains.finish(started, gates, got_taps)
-                started = chains.start()
-            ff_mine = jnp.concatenate([chains.results.pop(i) for i in range(2)], axis=1)
+            gates, *ff_pair = together(gates, *ff_pair)
+        else:
+            ff_mine, gates = together(ff_mine, gates)
             ff_pair = shared(ff_mine)
-        taps.append(ordered(kept[layer], got_taps))
         conv_two, conv_one, carried = mix(gates, taps[layer])
-        if natural:
-            conv_two, *ff_pair = together(conv_two, *ff_pair)
-        else:
-            ff_mine, conv_two = together(ff_mine, conv_two)
-            ff_pair = shared(ff_mine)
-        ff_all.append(Pieces(ff_pair, 0, 2 * part))
+        conv_two, *ff_pair = together(conv_two, *ff_pair)
+        ff_all.append(Pieces(ff_pair, none, 2 * part))
+        out_all.append(out_matrix(dense_all[layer]))
         if more:
             mine, conv_two = together(ff[layer + 1], conv_two)
             ff_mine = gathered(mine)
         conv_two = exchange(conv_two).reshape(mp * cut, length)
-        if natural:
-            grad, conv_two = together(cotangent, conv_two)
-            grad = to_one_sequence(grad)
         if more:
-            dense_mine, mine, conv_two = together(dense_mine, kept[layer + 1], conv_two)
-            got_taps = lax.ppermute(mine, "mp", swap)
-            dense_all.append(Pieces(shared(dense_mine), 0, dense_rows))
+            got_taps, conv_two = together(kept[layer + 1], conv_two)
+            got_taps = lax.ppermute(got_taps, "mp", swap)
+        half = None
+        if layer >= layers - 2:
+            half = halves_of_grad[layer - layers + 2]
+            half, conv_two = together(half, conv_two)
+            half = lax.ppermute(half, "mp", swap)
         gate_two = gate_two.reshape(mp * cut, length)
         s1, s2, active, slope, normed_two, gated = forward_block(
             layer == layers - 1,
@@ -1152,19 +1241,25 @@
             gains[layer, 1],
             biases[layer, 1],
         )
+        if half is not None:
+            half, s2 = together(half, s2)
+            halves_of_grad[layer - layers + 2] = half
         if more:
-            s2, grad, got_taps, *arrays = together(s2, grad, got_taps, *dense_all[-1].arrays)
-            dense_all[-1].arrays = arrays
+            dense_next, got_taps, s2 = together(dense_next, got_taps, s2)
+            dense_all.append(Pieces(shared(dense_next), none, dense_rows))
         saved.append(
             (stream, normed_one, gates, conv_one, carried, conv_two, gate_two)
             + (s1, active, slope, normed_two, gated)
         )
         stream = s2
     own_output, other = pick(stream.reshape(groups, chunk, width))
-    got_output = lax.ppermute(other.astype(BF16), "mp", swap)
+    other = other.astype(BF16)
+    got_output = lax.ppermute(other[: chunk // 2], "mp", swap)
+    other_output = other[chunk // 2 :]
+    grad = ordered(own_grad, jnp.concatenate(halves_of_grad, axis=0)).reshape(length, width)
 
     gain_rows, bias_rows = [None] * layers, [None] * layers
-    early_out, late_out, dks = [None] * layers, [None] * layers, [None] * layers
+    dks = [None] * layers
     later = None
     for layer in reversed(range(layers)):
         (s0, normed_one, gates, conv_one, carried, conv_two, gate_two) = saved[layer][:7]
@@ -1180,58 +1275,53 @@
             ff_all[layer],
             gains[layer, 1],
         )
-        waiting = []
+        gain_rows[layer], bias_rows[layer] = [None, gain_two], [None, bias_two]
+        mixed = None
         if later is not None:
             mixed, grad_conv = together(later[0], grad_conv)
-            waiting = late_grads(ways, groups, place, mixed, later[1])
+            got_dk, grad_conv = chains.finish(started, got_dk, grad_conv)
+            dks[layer + 1] = own_dk.astype(F32) + got_dk.astype(F32)
+        if layer == layers - 1:
+            got_output, grad_conv = together(got_output, grad_conv)
         grad_conv = exchange(grad_conv.reshape(peers, groups, cut, length))
         grad_two = grad_two.reshape(mp, cut, length)
-        where_to = still if layer else place
-        early = early_grads(
-            ways, groups, where_to, pre, active, grad_two, gated, normed_one, normed_two, dm, do
-        )
+        up_job = Plain(ways, mp, pre, normed_two)
+        down_job = Plain(ways, mp, active, dm)
+        two_rows = [grad_two, gated.reshape(mp, cut, length)]
+        mixed_job = Mixed(ways, groups, two_rows, [normed_one, do])
+        late_jobs = [] if mixed is None else [Mixed(ways, groups, [mixed], [later[1]])]
+        jobs = [up_job, down_job, mixed_job] + late_jobs
+        early = weight_grads("early_grads", ways, mp, place, jobs)
+        grad_conv, *early = together(grad_conv, *early)
         if layer == layers - 1:
-            grad_conv, got_output = together(grad_conv, got_output)
-        else:
-            grad_conv, got_dk = together(grad_conv, got_dk)
-            dks[layer + 1] = own_dk.astype(F32) + got_dk.astype(F32)
-        grad_conv, *both = together(grad_conv, *early, *waiting)
-        early, waiting = both[:ways], both[ways:]
-        chains.add("early", chip_chain(early, dp))
-        if later is not None:
-            chains.add("waiting", chip_chain(waiting, dp))
+            other_output, grad_conv = together(other_output, grad_conv)
+            more_output = lax.ppermute(other_output, "mp", swap)
+        chains.add(("flip", layer), chip_chain(early, dp))
+        (grad_conv,) = chains.tie(grad_conv)
         started = chains.start()
         grad_mixed, dk = unmix(grad_conv, gates, conv_one, carried, taps[layer])
         (grad_mixed,) = chains.finish(started, grad_mixed)
+        own_dk, other_dk = pick(dk.astype(BF16))
+        if layer == layers - 1:
+            more_output, grad_mixed = together(more_output, grad_mixed)
         grad_mixed = exchange(grad_mixed).reshape(mp, 2, cut, length)
-        own_dk, other_dk = pick(dk.astype(BF16))
-        got_dk = lax.ppermute(other_dk, "mp", swap)
-        early = chains.results["early"]
-        gain_rows[layer], bias_rows[layer] = [None, gain_two], [None, bias_two]
+        if layer == layers - 1:
+            output = jnp.concatenate([got_output, more_output], axis=0)
+            output = ordered(own_output, output.astype(F32))
+            output, grad_mixed = together(output, grad_mixed)
+        terms = chains.results.pop(("flip", layer))
+        chains.add(layer, scatter_chain(terms, mp, stage_order(mp, 0), True))
         if layer:
-            early_out[layer] = gathered_sum(early, ways == 1, dp)
-            if later is not None:
-                late_out[layer + 1] = gathered_sum(chains.results["waiting"], ways == 1, dp)
             later = grad_mixed, normed_one
         else:
-            if later is not None:
-                pairs = zip(early, chains.results["waiting"])
-                early = [jnp.concatenate(pair, axis=1) for pair in pairs]
-            rows = early[0].shape[1]
-            middle = rows // 32 * 16
-            spans = ((0, middle), (middle, rows))
-            for i, (a, b) in enumerate(spans):
-                terms = [e[:, a:b] for e in early]
-                chains.add(i, scatter_chain(terms, mp, stage_order(mp, i)))
-            before = chains.operands()
             started = chains.start()
-            late = late_grads(ways, groups, place, grad_mixed, normed_one, before)
-            got_dk, grad_mixed, *late = chains.finish(started, got_dk, grad_mixed, *late)
-            dks[0] = own_dk.astype(F32) + got_dk.astype(F32)
-            dk = jnp.stack(dks)
-            chains.add("late", chip_chain(late, dp))
-            chains.add("dk", sum_chain(dk.astype(BF16).astype(F32), [("dp", dp)]))
-            started = chains.start()
+            got_dk = lax.ppermute(other_dk, "mp", swap)
+            late_job = Mixed(ways, groups, [grad_mixed], [normed_one])
+            late = weight_grads("late_grads", ways, mp, place, [late_job])
+            grad_mixed, *late = together(grad_mixed, *late)
+            tail = Chains()
+            tail.add("late", chip_chain(late, dp))
+            last = tail.start()
         grad, gain_one, bias_one = unproject(
             layer == 0,
             groups,
@@ -1244,53 +1334,86 @@
             gains[layer, 0],
         )
         gain_rows[layer][0], bias_rows[layer][0] = gain_one, bias_one
-    grad, gain_rows[0][0] = chains.finish(started, grad, gain_rows[0][0])
+        if layer:
+            grad, other_dk = chains.tie(grad, other_dk)
+            got_dk = lax.ppermute(other_dk, "mp", swap)
+            started = chains.start()
+
+    (grad,) = tail.finish(last, grad)
     own, other = pick(grad.reshape(groups, chunk, width))
     swapped = lax.ppermute(other.astype(BF16), "mp", swap)
+    (gain_rows[0][0],) = chains.finish(started, gain_rows[0][0])
+    chains.results.update(tail.results)
+    bits = list(range(mp.bit_length() - 1))
+    quarters = [bits[i : i + 2] for i in range(0, len(bits), 2)]
     norms = jnp.stack([jnp.stack([jnp.stack(r) for r in rows]) for rows in (gain_rows, bias_rows)])
-    chains.add("norms", sum_chain(norms[..., 0], [("dp", dp), ("mp", mp)]))
-    chains.add("late", scatter_chain(chains.results.pop("late"), mp, stage_order(mp, 0)))
+    shape = norms.shape[:-1]
+    norms = norms.reshape(-1, width)
+    chains.add("late", last_chain(chains.results.pop("late"), norms, mp, quarters))
+    rounds = 0
     while chains.waiting:
-        chains.finish(chains.start())
-        if 0 in chains.results and 1 in chains.results:
-            rest = jnp.concatenate([chains.results.pop(i) for i in range(2)], axis=0)
-            chains.add("rest", spread_chain(rest, ways, dp))
-        if "late" in chains.results:
-            chains.add("last", spread_chain(chains.results.pop("late"), ways, dp))
+        started = chains.start()
+        if rounds == 0:
+            swapped, got_dk = chains.finish(started, swapped, got_dk)
+        else:
+            chains.finish(started)
+        rounds += 1
     input_grad = ordered(own, swapped.astype(F32))
-    output = ordered(own_output, got_output.astype(F32))
-    dk = chains.results["dk"][:, :, :shard]
+    dks[0] = own_dk.astype(F32) + got_dk.astype(F32)
+    dk = jnp.stack(dks).astype(BF16).astype(F32)
+    late, norms = chains.results.pop("late")
+    found = [chains.results.pop(layer) for layer in reversed(range(layers))]
+    final = [x.astype(BF16) for x in found + [late]]
+    if ways == 1:
+        dk, norms = dp_sum(dk, dp), dp_sum(norms, dp)
+        final = [[dp_sum(x, dp)] for x in found + [late]]
+    else:
+        dk = dk + flip(dk.astype(BF16), "dp", dp, 1).astype(F32)
+        norms = in_two(norms)
+        sizes = [x.shape[0] for x in final + [norms]]
+        sent = jnp.concatenate(final + [norms], axis=0)
+        got = flip(sent, "dp", dp, 1)
+        zero = way == 0
+        pair = jnp.where(zero, sent, got).astype(F32), jnp.where(zero, got, sent).astype(F32)
+        begin, pieces = 0, []
+        for size in sizes:
+            pieces.append([x[begin : begin + size] for x in pair])
+            begin += size
+        final, norms = pieces[:-1], pieces[-1]
+        half = norms[0].shape[0] // 2
+        norms = (norms[0][:half] + norms[0][half:]) + (norms[1][:half] + norms[1][half:])
+    norms = norms.reshape(shape)
+    dk = dk[:, :, :shard]
     tap_out = jnp.where(keep[:, None, None, :], dk, 0.0)
-    norms = chains.results["norms"]
-
-    def both_ways(x):
-        if ways == 1:
-            return (x.astype(F32),)
-        got = flip(x, "dp", dp, 1)
-        pair = jnp.where(way == 0, x, got), jnp.where(way == 0, got, x)
-        return tuple(p.astype(F32) for p in pair)
-
-    rest = [x.astype(F32) for x in chains.results["rest"]]
-    tall = 2 * part + 2 * cut // ways
-    early_out = [[r[:tall] for r in rest]] + [both_ways(e) for e in early_out[1:]]
-    late_out[0] = [x.astype(F32) for x in chains.results["last"]]
-    if layers > 1:
-        late_out[1] = [r[tall:] for r in rest]
-    late_out[2:] = [both_ways(x) for x in late_out[2:]]
+
+    def cut_rows(x, *sizes):
+        begin = 0
+        for size in sizes:
+            yield x[begin : begin + size]
+            begin += size
+
+    share = 2 * cut // ways
+    wide = [[None] * layers for _ in range(4)]
+    order = []
+    for layer in range(layers - 1, -1, -1):
+        now = [(0, layer), (1, layer), (2, layer)] + [(3, layer + 1)] * (layer < layers - 1)
+        order.append(now)
+    order.append([(3, 0)])
+    sizes = [part, part, share, share]
+    found = zip(order, final)
+    for order, arrays in found:
+        pieces = zip(*[cut_rows(x, *[sizes[i] for i, _ in order]) for x in arrays])
+        for (i, layer), x in zip(order, pieces):
+            wide[i][layer] = x
+
+    def rows_of_both(arrays):
+        return jnp.concatenate(arrays, axis=0)
 
     parts = [[] for _ in range(6)]
-    for early, late in zip(early_out, late_out):
-        if ways == 1:
-            e, l = early[0], late[0]
-            up, down = e[:part], e[part : 2 * part]
-            two, out = e[2 * part : 2 * part + cut], e[2 * part + cut :]
-            one, value = l[:cut], l[cut:]
-        else:
-            up = jnp.concatenate([e[:part] for e in early], axis=0)
-            down = jnp.concatenate([e[part : 2 * part] for e in early], axis=0)
-            two, out = early[0][2 * part :], early[1][2 * part :]
-            one, value = late
-        for store, x in zip(parts, (one, two, value, out, up, down)):
+    for up, down, early, late in zip(*wide):
+        two, out = (early[0][:cut], early[0][cut:]) if ways == 1 else early
+        one, value = (late[0][:cut], late[0][cut:]) if ways == 1 else late
+        for store, x in zip(parts, (one, two, value, out, rows_of_both(up), rows_of_both(down))):
             store.append(x)
     one, two, value, out, up, down = (jnp.stack(p) for p in parts)
     in_out = jnp.stack([one, two, value], axis=1)[:, :, :shard]

time: 1000 us -> 898 us (0.90); the launches traced: 994 us -> 880 us
  waiting for transfers between devices: 420 us -> 341 us
  other arithmetic: 84.7 us -> 67 us
    ppermute x37, waiting for transfers between devices: 166 us -> 113 us  [flip(): return lax.ppermute(x, axis, [(i, i ^ bit) for i in range(size)])]
    all_to_all x8, waiting for transfers between devices: 134 us -> 98.2 us  [exchange(): lax.all_to_all(x, 'mp', split_axis=0, concat_axis=0, tiled=True, axis_ind...]
    slice x8 -> x18, local copies, waits for them, and re-layouts: 6.03 us -> 24.8 us  [the longest x8 22.1 us: take(): return t[tuple(index)]]
    all_gather x3, waiting for transfers between devices: 49.9 us -> 65.5 us  [gathered(): return lax.all_gather(x, 'mp', axis=0)]
    squeeze x14 -> x3, local copies, waits for them, and re-layouts: 16.1 us -> 1.47 us  [the longest x1 0.84 us: program(): got_taps, conv_two = together(kept[layer + 1], conv_two)]
    all_to_all x8, starting transfers between devices: 55 us -> 41.6 us  [exchange(): lax.all_to_all(x, 'mp', split_axis=0, concat_axis=0, tiled=True, axis_ind...]
    ppermute x37, starting transfers between devices: 45.4 us -> 57.1 us  [flip(): return lax.ppermute(x, axis, [(i, i ^ bit) for i in range(size)])]
    another operation x20 -> x18, other arithmetic: 13.2 us -> 3.04 us  [the longest x15 1.68 us: gather_chain(): jnp.stack([pieces[j], pieces[j + 1]], axis=axis)]
  transfers between devices with their start and end apart: 57 -> 59, of which waited for: 30 -> 25; matrix products, arithmetic and copies ran while one was open for 11% -> 11% of each run, Pallas kernels for 24% -> 32%
where the time goes in v2:
time: 898 us; the launch traced here: 880 us
  waiting for transfers between devices  341 us (38%)
  Pallas kernels  293 us (33%)
  starting transfers between devices  107 us (12%)
  other arithmetic  67 us (7%)
  local copies, waits for them, and re-layouts  56.7 us (6%)
  between operations  15.6 us (2%)
    ppermute x37, waiting for transfers between devices, flip(): return lax.ppermute(x, axis, [(i, i ^ bit) for i in range(size)])  113 us
    all_to_all x8, waiting for transfers between devices, exchange(): lax.all_to_all(x, 'mp', split_axis=0, concat_axis=0, tiled=True, axis_ind...  98.2 us
    all_gather x3, waiting for transfers between devices, gathered(): return lax.all_gather(x, 'mp', axis=0)  65.5 us
    pallas_call x2, Pallas kernels, forward_block(): pl.pallas_call(functools.partial(forward_body, natural, len(ff)), grid=(l...  62.4 us
    ppermute x3, waiting for transfers between devices, program(): got = lax.ppermute(now, 'mp', swap)  60.6 us
    ppermute x37, starting transfers between devices, flip(): return lax.ppermute(x, axis, [(i, i ^ bit) for i in range(size)])  57.1 us
    pallas_call x3, Pallas kernels, weight_grads(): pl.pallas_call(functools.partial(grads_body, ways, jobs, len(before)), gr...  52.3 us
    pallas_call x2, Pallas kernels, backward_block(): pl.pallas_call(functools.partial(backward_body, natural, len(ff)), grid=(...  51.5 us
  transfers between devices with their start and end apart: 59, of which 25 were waited for; matrix products, arithmetic and copies ran while one was open for 11% of the time, Pallas kernels for 32%

profile of v2, /device:TPU:1, one launch (start us, length us, event | category | flops | bytes accessed | tf_op | source)
XLA Modules:
  0.0 880.5 jit_solution(11193583129581761256)
XLA Ops:
  26.4 13.4 %collective-permute-done.3 = bf16[2,48,768]{2,1,0:T(8,128)(2,1)} collective-permute-done((bf16[2,48,768]{2,1,0:T(8,128)(2,1)S(1)}, bf16[2,48,768]{2,1,0:T(8,128)(2,1)}, u32[]{:S(2)}, u32[]{:S(2)}) %collective-permute-start.3) | collective-permute-done | bytes 147488 | tf_op jit(solution)/shard_map/ppermute | solution.py:877
  53.6 11.6 %collective-permute-done.6 = bf16[2,2,48,768]{3,2,0,1:T(8,128)(2,1)S(1)} collective-permute-done((bf16[2,2,48,768]{3,2,0,1:T(8,128)(2,1)S(1)}, bf16[2,2,48,768]{3,2,0,1:T(8,128)(2,1)S(1)}, u32[]{:S(2)}, u32[]{:S(2)}) %collective-permute-start.6) | collective-permute-done | bytes 294944 | tf_op jit(solution)/shard_map/ppermute | solution.py:877
  65.2 16.2 %collective-permute-done.7 = bf16[256,768]{1,0:T(8,128)(2,1)S(1)} collective-permute-done((bf16[256,768]{1,0:T(8,128)(2,1)S(1)}, bf16[256,768]{1,0:T(8,128)(2,1)S(1)}, u32[]{:S(2)}, u32[]{:S(2)}) %collective-permute-start.7) | collective-permute-done | bytes 393248 | tf_op jit(solution)/shard_map/ppermute | solution.py:1166
  84.2 39.2 %collective-permute-done.10 = bf16[2,48,2048]{2,1,0:T(8,128)(2,1)S(1)} collective-permute-done((bf16[2,48,2048]{2,1,0:T(8,128)(2,1)S(1)}, bf16[2,48,2048]{2,1,0:T(8,128)(2,1)S(1)}, u32[]{:S(2)}, u32[]{:S(2)}) %collective-permute-start.10) | collective-permute-done | bytes 393248 | tf_op jit(solution)/shard_map/ppermute | solution.py:1166
  156.6 30.8 %all-to-all-done.v_ref.g_ref = bf16[8,2,2,48,1024]{4,3,2,1,0:T(8,128)(2,1)S(1)} async-done(((bf16[8,2,2,48,1024]{4,3,2,1,0:T(8,128)(2,1)}), bf16[8,2,2,48,1024]{4,3,2,1,0:T(8,128)(2,1)S(1)}, u32[]{:S(2)}, u32[]{:S(2)}) %all-to-all-start) | async-done | bytes 3145760 | tf_op jit(solution)/shard_map/all_to_all | solution.py:1107
  189.0 16.0 %mix.2 = (bf16[8,2,48,1024]{3,2,1,0:T(8,128)(2,1)}, bf16[2,64,48,128]{3,2,1,0:T(8,128)(2,1)}, bf16[2,64,48,128]{3,2,1,0:T(8,128)(2,1)}) custom-call(bf16[8,2,2,48,1024]{4,3,2,1,0:T(8,128)(2,1)} %copy-done.2, bf16[8,2,2,48,1024]{4,3,2,1,0:T(8,128)(2,1)} %copy-done.2, bf16[2,2,48,2048]{3,2,1,0:T(8,128)(2,1)} %pad_maximum_fusion.9.k_ref, ...), custom_call_target="tpu_custom_call" | custom-call | tf_op jit(solution)/shard_map/mix/pallas_call | solution.py:359
  205.0 10.9 %all-to-all-start.1 = ((bf16[8,2,48,1024]{3,2,1,0:T(8,128)(2,1)}), bf16[8,2,48,1024]{3,2,1,0:T(8,128)(2,1)S(1)}, u32[]{:S(2)}, u32[]{:S(2)}) async-start(bf16[8,2,48,1024]{3,2,1,0:T(8,128)(2,1)} %get-tuple-element.203), calls=%async_computation.1 | async-start | bytes 3145728 | tf_op jit(solution)/shard_map/all_to_all | solution.py:1107
  218.2 21.8 %all-to-all-done.1 = bf16[8,2,48,1024]{3,2,1,0:T(8,128)(2,1)S(1)} async-done(((bf16[8,2,48,1024]{3,2,1,0:T(8,128)(2,1)}), bf16[8,2,48,1024]{3,2,1,0:T(8,128)(2,1)S(1)}, u32[]{:S(2)}, u32[]{:S(2)}) %all-to-all-start.1) | async-done | bytes 1572896 | tf_op jit(solution)/shard_map/all_to_all | solution.py:1107
  248.9 31.2 %forward_block.2 = (f32[768,1024]{1,0:T(8,128)}, f32[768,1024]{1,0:T(8,128)}, bf16[3072,1024]{1,0:T(8,128)(2,1)}, bf16[3072,1024]{1,0:T(8,128)(2,1)}, bf16[1024,...) custom-call(f32[768,1024]{1,0:T(8,128)} %get-tuple-element.207.s_ref, bf16[768,1024]{1,0:T(8,128)(2,1)} %bitcast.330, ...), custom_call_target="tpu_custom_call" | custom-call | tf_op jit(solution)/shard_map/forward_block/pallas_call | solution.py:611
  301.8 65.5 %all-gather.9.cloned.1.call-done = bf16[3072,768]{1,0:T(8,128)(2,1)} async-done(((bf16[192,768]{1,0:T(8,128)(2,1)}), bf16[3072,768]{1,0:T(8,128)(2,1)}) %all-gather.9.cloned.1.call-update) | async-done | bytes 4718608 | tf_op jit(solution)/shard_map/all_gather | solution.py:1131
  370.5 16.0 %mix.3 = (bf16[8,2,48,1024]{3,2,1,0:T(8,128)(2,1)}, bf16[2,64,48,128]{3,2,1,0:T(8,128)(2,1)}, bf16[2,64,48,128]{3,2,1,0:T(8,128)(2,1)}) custom-call(bf16[8,2,2,48,1024]{4,3,2,1,0:T(8,128)(2,1)} %copy-done.3, bf16[8,2,2,48,1024]{4,3,2,1,0:T(8,128)(2,1)} %copy-done.3, bf16[2,2,48,2048]{3,2,1,0:T(8,128)(2,1)} %pad_maximum_fusion.10.k_ref, ...), custom_call_target="tpu_custom_call" | custom-call | tf_op jit(solution)/shard_map/mix/pallas_call | solution.py:359
  392.1 19.9 %all-to-all-done.3 = bf16[8,2,48,1024]{3,2,1,0:T(8,128)(2,1)} async-done(((bf16[8,2,48,1024]{3,2,1,0:T(8,128)(2,1)}), bf16[8,2,48,1024]{3,2,1,0:T(8,128)(2,1)}, u32[]{:S(2)}, u32[]{:S(2)}) %all-to-all-start.3) | async-done | bytes 1572896 | tf_op jit(solution)/shard_map/all_to_all | solution.py:1107
  417.9 31.2 %forward_block.3 = (f32[768,1024]{1,0:T(8,128)}, f32[1024,768]{1,0:T(8,128)}, bf16[3072,1024]{1,0:T(8,128)(2,1)}, bf16[3072,1024]{1,0:T(8,128)(2,1)}, bf16[1024,...) custom-call(f32[768,1024]{1,0:T(8,128)} %get-tuple-element.214.x_ref.s_ref, bf16[768,1024]{1,0:T(8,128)(2,1)} %bitcast.62.c_ref, ...), custom_call_target="tpu_custom_call" | custom-call | tf_op jit(solution)/shard_map/forward_block/pallas_call | solution.py:611
  455.0 25.8 %backward_block.2 = (bf16[3072,1024]{1,0:T(8,128)(2,1)}, f32[768,1024]{1,0:T(8,128)}, bf16[768,1024]{1,0:T(8,128)(2,1)}, bf16[768,1024]{1,0:T(8,128)(2,1)}, bf16...) custom-call(bf16[1024,768]{1,0:T(8,128)(2,1)} %bitcast.347, ...), custom_call_target="tpu_custom_call" | custom-call | tf_op jit(solution)/shard_map/backward_block/pallas_call | solution.py:679
  485.6 21.0 %early_grads.2 = (bf16[16,240,768]{2,1,0:T(8,128)(2,1)}, bf16[16,240,768]{2,1,0:T(8,128)(2,1)}) custom-call(s32[2]{0:T(128)} %pad_add_fusion.place_ref, bf16[2,16,96,1024]{3,2,1,0:T(8,128)(2,1)} %bitcast.352, bf16[2,16,96,1024]{3,2,1,0:T(8,128)(2,1)} %bitcast.350, bf16[8,2,48,1024]{3,2,1,0:T(8,128)(2,1)} %bitcast.343, bf16[8,2,48,1024]{3,2,1,0:T(8,128)(2,1)} %bitcast.361, ...), custom_call_target="tpu_custom_call" | custom-call | tf_op jit(solution)/shard_map/early_grads/pallas_call | solution.py:856
  511.0 24.7 %unmix.2 = (bf16[8,2,2,48,1024]{4,3,2,1,0:T(8,128)(2,1)}, f32[2,2,48,2048]{3,2,1,0:T(8,128)}) custom-call(bf16[8,2,48,1024]{3,2,1,0:T(8,128)(2,1)} %copy-done.23, bf16[8,2,2,48,1024]{4,3,2,1,0:T(8,128)(2,1)} %copy-done.3, bf16[8,2,2,48,1024]{4,3,2,1,0:T(8,128)(2,1)} %copy-done.3, bf16[2,64,48,128]{3,2,1,0:T(8,128)(2,1)} %get-tuple-element.252.one_ref, ...), custom_call_target="tpu_custom_call" | custom-call | tf_op jit(solution)/shard_map/unmix/pallas_call | solution.py:386
  562.3 16.6 %all-to-all-done.5 = bf16[8,2,2,48,1024]{4,3,2,1,0:T(8,128)(2,1)S(1)} async-done(((bf16[8,2,2,48,1024]{4,3,2,1,0:T(8,128)(2,1)}), bf16[8,2,2,48,1024]{4,3,2,1,0:T(8,128)(2,1)S(1)}, u32[]{:S(2)}, u32[]{:S(2)}) %all-to-all-start.5) | async-done | bytes 3145760 | tf_op jit(solution)/shard_map/all_to_all | solution.py:1107
  580.6 12.2 %unproject.2 = (f32[768,1024]{1,0:T(8,128)}, f32[768,1]{1,0:T(8,128)}, f32[768,1]{1,0:T(8,128)}) custom-call(s32[2]{0:T(128)} %pad_add_fusion.place_ref, bf16[16,2,48,1024]{3,2,1,0:T(8,128)(2,1)} %bitcast.319, bf16[16,48,1024]{2,1,0:T(8,128)(2,1)} %bitcast.344, f32[768,1024]{1,0:T(8,128)} %get-tuple-element.214.x_ref.s_ref, ...), custom_call_target="tpu_custom_call" | custom-call | tf_op jit(solution)/shard_map/unproject/pallas_call | solution.py:740
  598.6 25.6 %backward_block.3 = (bf16[3072,1024]{1,0:T(8,128)(2,1)}, f32[768,1024]{1,0:T(8,128)}, bf16[768,1024]{1,0:T(8,128)(2,1)}, bf16[768,1024]{1,0:T(8,128)(2,1)}, bf16...) custom-call(f32[768,1024]{1,0:T(8,128)} %get-tuple-element.268.gs_ref, ...), custom_call_target="tpu_custom_call" | custom-call | tf_op jit(solution)/shard_map/backward_block/pallas_call | solution.py:679
  638.5 24.8 %early_grads.3 = (bf16[16,288,768]{2,1,0:T(8,128)(2,1)}, bf16[16,288,768]{2,1,0:T(8,128)(2,1)}) custom-call(s32[2]{0:T(128)} %pad_add_fusion.place_ref, bf16[2,16,96,1024]{3,2,1,0:T(8,128)(2,1)} %bitcast.351, bf16[2,16,96,1024]{3,2,1,0:T(8,128)(2,1)} %bitcast.349, bf16[8,2,48,1024]{3,2,1,0:T(8,128)(2,1)} %bitcast.341, bf16[8,2,48,1024]{3,2,1,0:T(8,128)(2,1)} %bitcast.360, ...), custom_call_target="tpu_custom_call" | custom-call | tf_op jit(solution)/shard_map/early_grads/pallas_call | solution.py:856
  671.7 24.7 %unmix.3 = (bf16[8,2,2,48,1024]{4,3,2,1,0:T(8,128)(2,1)}, f32[2,2,48,2048]{3,2,1,0:T(8,128)}) custom-call(bf16[8,2,48,1024]{3,2,1,0:T(8,128)(2,1)} %copy-done.22, bf16[8,2,2,48,1024]{4,3,2,1,0:T(8,128)(2,1)} %copy-done.2, bf16[8,2,2,48,1024]{4,3,2,1,0:T(8,128)(2,1)} %copy-done.2, bf16[2,64,48,128]{3,2,1,0:T(8,128)(2,1)} %get-tuple-element.293.one_ref, ...), custom_call_target="tpu_custom_call" | custom-call | tf_op jit(solution)/shard_map/unmix/pallas_call | solution.py:386
  753.1 12.3 %unproject.3 = (f32[1024,768]{1,0:T(8,128)}, f32[768,1]{1,0:T(8,128)}, f32[768,1]{1,0:T(8,128)}) custom-call(s32[2]{0:T(128)} %pad_add_fusion.place_ref, bf16[16,2,48,1024]{3,2,1,0:T(8,128)(2,1)} %bitcast.318, bf16[16,48,1024]{2,1,0:T(8,128)(2,1)} %bitcast.342, f32[768,1024]{1,0:T(8,128)} %get-tuple-element.207.s_ref, ...), custom_call_target="tpu_custom_call" | custom-call | tf_op jit(solution)/shard_map/unproject/pallas_call | solution.py:740
  788.4 13.9 %collective-permute-done.34 = bf16[2,2,144,768]{3,2,1,0:T(8,128)(2,1)S(1)} collective-permute-done((bf16[2,2,144,768]{3,2,1,0:T(8,128)(2,1)S(1)}, bf16[2,2,144,768]{3,2,1,0:T(8,128)(2,1)S(1)}, u32[]{:S(2)}, u32[]{:S(2)}) %collective-permute-start.34) | collective-permute-done | bytes 884768 | tf_op jit(solution)/shard_map/ppermute | solution.py:877
  835.5 23.9 %collective-permute-done.45 = bf16[64,768]{1,0:T(8,128)(2,1)S(1)} collective-permute-done((bf16[64,768]{1,0:T(8,128)(2,1)S(1)}, bf16[64,768]{1,0:T(8,128)(2,1)S(1)}, u32[]{:S(2)}, u32[]{:S(2)}) %collective-permute-start.45) | collective-permute-done | bytes 98336 | tf_op jit(solution)/shard_map/ppermute | solution.py:877
  (403 shorter events, 315.5 us)
Async XLA Ops:
  7.2 137.2 %all-gather.7.cloned.1.call-start = ((), (), s32[]{:S(2)}) async-start(), calls=%async_computation.8 | async-start | bytes 5013504 | tf_op jit(solution)/shard_map/all_gather | solution.py:1131
  81.6 41.8 %collective-permute-start.9 = (bf16[2,2,2,48,768]{4,3,0,1,2:T(8,128)(2,1)S(1)}, bf16[2,2,2,48,768]{4,3,0,1,2:T(8,128)(2,1)S(1)}, u32[]{:S(2)}, u32[]{:S(2)}) collective-permute-start(bf16[2,2,2,48,768]{4,3,0,1,2:T(8,128)(2,1)S(1)} %pad_maximum_fusion.15), channel_id=1, source_target_pairs={{0,2},{1,3},{2,0},{3,1},{4,6},{5,7},{6,4},{7,5},{8,10},{9,11},{10,... | collective-permute-start | bytes 1769480 | tf_op jit(solution)/shard_map/ppermute | solution.py:877
  83.0 41.2 %collective-permute-start.8 = (bf16[2,2,2,48,768]{4,3,0,1,2:T(8,128)(2,1)S(1)}, bf16[2,2,2,48,768]{4,3,0,1,2:T(8,128)(2,1)S(1)}, u32[]{:S(2)}, u32[]{:S(2)}) collective-permute-start(bf16[2,2,2,48,768]{4,3,0,1,2:T(8,128)(2,1)S(1)} %pad_maximum_fusion.14), channel_id=1, source_target_pairs={{0,1},{1,0},{2,3},{3,2},{4,5},{5,4},{6,7},{7,6},{8,9},{9,8},{10,11... | collective-permute-start | bytes 1769480 | tf_op jit(solution)/shard_map/ppermute | solution.py:877
  84.2 39.2 %collective-permute-start.10 = (bf16[2,48,2048]{2,1,0:T(8,128)(2,1)S(1)}, bf16[2,48,2048]{2,1,0:T(8,128)(2,1)S(1)}, u32[]{:S(2)}, u32[]{:S(2)}) collective-permute-start(bf16[2,48,2048]{2,1,0:T(8,128)(2,1)S(1)} %get-tuple-element.188), channel_id=1, source_target_pairs={{0,8},{1,9},{2,10},{3,11},{4,12},{5,13},{6,14},{7,15},{8,0},{9,1},... | collective-permute-start | bytes 1179656 | tf_op jit(solution)/shard_map/ppermute | solution.py:1166
  144.4 42.9 %all-to-all-start = ((bf16[8,2,2,48,1024]{4,3,2,1,0:T(8,128)(2,1)}), bf16[8,2,2,48,1024]{4,3,2,1,0:T(8,128)(2,1)S(1)}, u32[]{:S(2)}, u32[]{:S(2)}) async-start(bf16[8,2,2,48,1024]{4,3,2,1,0:T(8,128)(2,1)} %bitcast.358), calls=%async_computation | async-start | bytes 6291456 | tf_op jit(solution)/shard_map/all_to_all | solution.py:1107
  148.2 131.9 %all-gather.11.cloned.1.call-start = ((), (), s32[]{:S(2)}) async-start(), calls=%async_computation.10 | async-start | bytes 2506752 | tf_op jit(solution)/shard_map/all_gather | solution.py:1131
  205.0 35.0 %all-to-all-start.1 = ((bf16[8,2,48,1024]{3,2,1,0:T(8,128)(2,1)}), bf16[8,2,48,1024]{3,2,1,0:T(8,128)(2,1)S(1)}, u32[]{:S(2)}, u32[]{:S(2)}) async-start(bf16[8,2,48,1024]{3,2,1,0:T(8,128)(2,1)} %get-tuple-element.203), calls=%async_computation.1 | async-start | bytes 3145728 | tf_op jit(solution)/shard_map/all_to_all | solution.py:1107
  215.9 151.4 %all-gather.9.cloned.1.call-start = ((), (), s32[]{:S(2)}) async-start(), calls=%async_computation.9 | async-start | bytes 5013504 | tf_op jit(solution)/shard_map/all_gather | solution.py:1131
  240.0 40.1 %collective-permute-start.13 = (bf16[2,48,2048]{2,1,0:T(8,128)(2,1)}, bf16[2,48,2048]{2,1,0:T(8,128)(2,1)}, u32[]{:S(2)}, u32[]{:S(2)}) collective-permute-start(bf16[2,48,2048]{2,1,0:T(8,128)(2,1)} %get-tuple-element.204), channel_id=1, source_target_pairs={{0,8},{1,9},{2,10},{3,11},{4,12},{5,13},{6,14},{7,15},{8,0},{9,1},... | collective-permute-start | bytes 1179656 | tf_op jit(solution)/shard_map/ppermute | solution.py:1227
  245.0 35.1 %collective-permute-start.14 = (bf16[192,768]{1,0:T(8,128)(2,1)}, bf16[192,768]{1,0:T(8,128)(2,1)}, u32[]{:S(2)}, u32[]{:S(2)}) collective-permute-start(bf16[192,768]{1,0:T(8,128)(2,1)} %slice_bitcast_fusion.5), channel_id=1, source_target_pairs={{0,8},{1,9},{2,10},{3,11},{4,12},{5,13},{6,14},{7,15},{8,0},{9,1},... | collective-permute-start | bytes 884744 | tf_op jit(solution)/shard_map/ppermute | solution.py:1232
  297.6 69.8 %all-to-all-start.2 = ((bf16[8,2,2,48,1024]{4,3,2,1,0:T(8,128)(2,1)}), bf16[8,2,2,48,1024]{4,3,2,1,0:T(8,128)(2,1)S(1)}, u32[]{:S(2)}, u32[]{:S(2)}) async-start(bf16[8,2,2,48,1024]{4,3,2,1,0:T(8,128)(2,1)} %bitcast.359), calls=%async_computation.2 | async-start | bytes 6291456 | tf_op jit(solution)/shard_map/all_to_all | solution.py:1107
  412.1 37.1 %collective-permute-start.17 = (bf16[320,768]{1,0:T(8,128)(2,1)}, bf16[320,768]{1,0:T(8,128)(2,1)S(1)}, u32[]{:S(2)}, u32[]{:S(2)}) collective-permute-start(bf16[320,768]{1,0:T(8,128)(2,1)} %slice_bitcast_fusion), channel_id=1, source_target_pairs={{0,8},{1,9},{2,10},{3,11},{4,12},{5,13},{6,14},{7,15},{8,0},{9,1},... | collective-permute-start | bytes 1474568 | tf_op jit(solution)/shard_map/ppermute | solution.py:1232
  536.5 42.5 %all-to-all-start.5 = ((bf16[8,2,2,48,1024]{4,3,2,1,0:T(8,128)(2,1)}), bf16[8,2,2,48,1024]{4,3,2,1,0:T(8,128)(2,1)S(1)}, u32[]{:S(2)}, u32[]{:S(2)}) async-start(bf16[8,2,2,48,1024]{4,3,2,1,0:T(8,128)(2,1)} %get-tuple-element.257), calls=%async_computation.5 | async-start | bytes 6291456 | tf_op jit(solution)/shard_map/all_to_all | solution.py:1107
  592.9 37.8 %collective-permute-start.21 = (bf16[2,2,2,128,768]{4,3,1,0,2:T(8,128)(2,1)S(1)}, bf16[2,2,2,128,768]{4,3,1,0,2:T(8,128)(2,1)S(1)}, u32[]{:S(2)}, u32[]{:S(2)}) collective-permute-start(bf16[2,2,2,128,768]{4,3,1,0,2:T(8,128)(2,1)S(1)} %copy-done.37), channel_id=1, source_target_pairs={{0,1},{1,0},{2,3},{3,2},{4,5},{5,4},{6,7},{7,6},{8,9},{9,8},{10,11... | collective-permute-start | bytes 4718600 | tf_op jit(solution)/shard_map/ppermute | solution.py:877
  697.5 47.6 %all-to-all-start.7 = ((bf16[8,2,2,48,1024]{4,3,2,1,0:T(8,128)(2,1)}), bf16[8,2,2,48,1024]{4,3,2,1,0:T(8,128)(2,1)S(1)}, u32[]{:S(2)}, u32[]{:S(2)}) async-start(bf16[8,2,2,48,1024]{4,3,2,1,0:T(8,128)(2,1)} %get-tuple-element.296), calls=%async_computation.7 | async-start | bytes 6291456 | tf_op jit(solution)/shard_map/all_to_all | solution.py:1107
  718.3 58.6 %collective-permute-start.32 = (bf16[2,2,2,144,768]{4,3,1,0,2:T(8,128)(2,1)}, bf16[2,2,2,144,768]{4,3,1,0,2:T(8,128)(2,1)}, u32[]{:S(2)}, u32[]{:S(2)}) collective-permute-start(bf16[2,2,2,144,768]{4,3,1,0,2:T(8,128)(2,1)} %fusion.2), channel_id=1, source_target_pairs={{0,2},{1,3},{2,0},{3,1},{4,6},{5,7},{6,4},{7,5},{8,10},{9,11},{10,... | collective-permute-start | bytes 5308424 | tf_op jit(solution)/shard_map/ppermute | solution.py:877
  723.7 53.3 %collective-permute-start.31 = (bf16[2,2,2,144,768]{4,3,1,0,2:T(8,128)(2,1)}, bf16[2,2,2,144,768]{4,3,1,0,2:T(8,128)(2,1)}, u32[]{:S(2)}, u32[]{:S(2)}) collective-permute-start(bf16[2,2,2,144,768]{4,3,1,0,2:T(8,128)(2,1)} %fusion.1), channel_id=1, source_target_pairs={{0,1},{1,0},{2,3},{3,2},{4,5},{5,4},{6,7},{7,6},{8,9},{9,8},{10,11... | collective-permute-start | bytes 5308424 | tf_op jit(solution)/shard_map/ppermute | solution.py:877
  729.1 36.3 %collective-permute-start.28 = (bf16[240,768]{1,0:T(8,128)(2,1)}, bf16[240,768]{1,0:T(8,128)(2,1)}, u32[]{:S(2)}, u32[]{:S(2)}) collective-permute-start(bf16[240,768]{1,0:T(8,128)(2,1)} %get-tuple-element.391), channel_id=1, source_target_pairs={{0,4},{1,5},{2,6},{3,7},{4,0},{5,1},{6,2},{7,3},{8,12},{9,13},{10,... | collective-permute-start | bytes 1105928 | tf_op jit(solution)/shard_map/ppermute | solution.py:877
  730.3 35.1 %collective-permute-start.29 = (bf16[240,768]{1,0:T(8,128)(2,1)}, bf16[240,768]{1,0:T(8,128)(2,1)}, u32[]{:S(2)}, u32[]{:S(2)}) collective-permute-start(bf16[240,768]{1,0:T(8,128)(2,1)} %get-tuple-element.392), channel_id=1, source_target_pairs={{0,8},{1,9},{2,10},{3,11},{4,12},{5,13},{6,14},{7,15},{8,0},{9,1},... | collective-permute-start | bytes 1105928 | tf_op jit(solution)/shard_map/ppermute | solution.py:877
  730.3 37.6 %collective-permute-start.30 = (bf16[240,768]{1,0:T(8,128)(2,1)}, bf16[240,768]{1,0:T(8,128)(2,1)}, u32[]{:S(2)}, u32[]{:S(2)}) collective-permute-start(bf16[240,768]{1,0:T(8,128)(2,1)} %get-tuple-element.390), channel_id=1, source_target_pairs={{0,12},{1,13},{2,14},{3,15},{4,8},{5,9},{6,10},{7,11},{8,4},{9,5},... | collective-permute-start | bytes 1105928 | tf_op jit(solution)/shard_map/ppermute | solution.py:877
  786.7 35.3 %collective-permute-start.38 = (bf16[512,768]{1,0:T(8,128)(2,1)S(1)}, bf16[512,768]{1,0:T(8,128)(2,1)S(1)}, u32[]{:S(2)}, u32[]{:S(2)}) collective-permute-start(bf16[512,768]{1,0:T(8,128)(2,1)S(1)} %select_convert_fusion), channel_id=1, source_target_pairs={{0,8},{1,9},{2,10},{3,11},{4,12},{5,13},{6,14},{7,15},{8,0},{9,1},... | collective-permute-start | bytes 2359304 | tf_op jit(solution)/shard_map/ppermute | solution.py:1344
  826.1 35.2 %collective-permute-start.41 = (bf16[288,768]{1,0:T(8,128)(2,1)S(1)}, bf16[288,768]{1,0:T(8,128)(2,1)S(1)}, u32[]{:S(2)}, u32[]{:S(2)}) collective-permute-start(bf16[288,768]{1,0:T(8,128)(2,1)S(1)} %get-tuple-element.382), channel_id=1, source_target_pairs={{0,8},{1,9},{2,10},{3,11},{4,12},{5,13},{6,14},{7,15},{8,0},{9,1},... | collective-permute-start | bytes 1327112 | tf_op jit(solution)/shard_map/ppermute | solution.py:877
  826.7 34.6 %collective-permute-start.42 = (bf16[288,768]{1,0:T(8,128)(2,1)S(1)}, bf16[288,768]{1,0:T(8,128)(2,1)S(1)}, u32[]{:S(2)}, u32[]{:S(2)}) collective-permute-start(bf16[288,768]{1,0:T(8,128)(2,1)S(1)} %get-tuple-element.381), channel_id=1, source_target_pairs={{0,12},{1,13},{2,14},{3,15},{4,8},{5,9},{6,10},{7,11},{8,4},{9,5},... | collective-permute-start | bytes 1327112 | tf_op jit(solution)/shard_map/ppermute | solution.py:877
  831.3 34.7 %collective-permute-start.47 = (bf16[2,2,48,2048]{3,2,1,0:T(8,128)(2,1)S(1)}, bf16[2,2,48,2048]{3,2,1,0:T(8,128)(2,1)S(1)}, u32[]{:S(2)}, u32[]{:S(2)}) collective-permute-start(bf16[2,2,48,2048]{3,2,1,0:T(8,128)(2,1)S(1)} %pad_maximum_fusion.13), channel_id=1, source_target_pairs={{0,16},{16,0},{1,17},{17,1},{2,18},{18,2},{3,19},{19,3},{4,20},{20... | collective-permute-start | bytes 2359304 | tf_op jit(solution)/shard_map/ppermute | solution.py:877
  (102 other events, 1295.7 us)
Sparse Core Ops, SparseCore 0:
  11.4 117.4 all-gather.6
  151.8 78.7 all-gather.10
  233.4 133.8 all-gather.8

commit v3 on v2

--- a/solution.py
+++ b/solution.py
@@ -288,9 +288,9 @@
     cv.store(gs, out_ref)
 
 
-def unmix_body(shape, d_ref, v_ref, g_ref, one_ref, carried_ref, k_ref, *refs):
-    (fwd, bwd, cos, sin, out_ref, dk_ref, xs, gs, left, right, freq) = refs
-    cv = Convolver(*shape, v_ref.shape[1], (fwd, bwd, cos, sin, left, right, freq))
+def unmix_body(shape, d_ref, g_ref, one_ref, k_ref, *refs):
+    (fwd, bwd, cos, sin, out_ref, grad_ref, xs, gs, left, right, freq) = refs
+    cv = Convolver(*shape, g_ref.shape[1], (fwd, bwd, cos, sin, left, right, freq))
     n = cv.blocks
     cv.load(d_ref, xs)
     cv.load(g_ref, gs)
@@ -298,39 +298,57 @@
     def read(b, i, rows):
         return xs[b * HALF + i, rows, :]
 
-    def read_carried(b, i, rows):
-        return carried_ref[b * HALF + i].astype(F32)[rows.start : rows.start + rows.size]
-
-    def put(j):
-        def write(_, i, rows, value):
-            dk_ref[j, rows, i * LANES : (i + 1) * LANES] = value
-
-        return write
-
-    cv.spectrum(kernel_reader(k_ref, 1), 1, 2 * n)
+    cv.spectrum(kernel_reader(k_ref, 1), 1, n)
     cv.spectrum(read, n, 0)
-    cv.spectrum(read_carried, n, n)
-    cv.taps(n, 0, put(1))
 
     def gate(b, i, rows, value):
         r = b * HALF + i
         xs[r, rows, :] = (gs[r, rows, :] * value).astype(BF16).astype(F32)
         gs[r, rows, :] = value
 
-    cv.convolve(0, 2 * n, True, gate)
+    cv.convolve(0, n, True, gate)
+    grad_ref[...] = xs[...].astype(BF16)
     gs[...] = gs[...] * one_ref[...].astype(F32)
     cv.store(gs, out_ref, 0)
+    cv.spectrum(kernel_reader(k_ref, 0), 1, n)
     cv.spectrum(read, n, 0)
-    cv.load(v_ref, xs)
-    cv.spectrum(kernel_reader(k_ref, 0), 1, 2 * n)
-    cv.spectrum(read, n, n)
-    cv.taps(n, 0, put(0))
 
     def keep(b, i, rows, value):
         gs[b * HALF + i, rows, :] = value
 
-    cv.convolve(0, 2 * n, True, keep)
+    cv.convolve(0, n, True, keep)
     cv.store(gs, out_ref, 1)
+
+
+def tap_body(shape, before, d_ref, v_ref, carried_ref, grad_ref, *refs):
+    (fwd, bwd, cos, sin), refs = refs[:4], refs[4 + before :]
+    (dk_ref, xs, gs, left, right, freq) = refs
+    cv = Convolver(*shape, v_ref.shape[1], (fwd, bwd, cos, sin, left, right, freq))
+    n = cv.blocks
+    cv.load(d_ref, xs)
+    cv.load(v_ref, gs)
+
+    def reader(ref):
+        return lambda b, i, rows: ref[b * HALF + i, rows, :]
+
+    def half_reader(ref):
+        def read(b, i, rows):
+            return ref[b * HALF + i].astype(F32)[rows.start : rows.start + rows.size]
+
+        return read
+
+    def put(j):
+        def write(_, i, rows, value):
+            dk_ref[j, rows, i * LANES : (i + 1) * LANES] = value
+
+        return write
+
+    cv.spectrum(reader(xs), n, 0)
+    cv.spectrum(half_reader(carried_ref), n, n)
+    cv.taps(n, 0, put(1))
+    cv.spectrum(half_reader(grad_ref), n, 0)
+    cv.spectrum(reader(gs), n, n)
+    cv.taps(n, 0, put(0))
 
 
 def conv_sizes(gates):
@@ -377,36 +395,56 @@
     )(gates, gates, taps, *consts)
 
 
-def unmix(grads, gates, conv_one, carried, taps):
+def unmix(grads, gates, conv_one, taps):
     q, g, shard, length, tile, pieces, rows, blocks = conv_sizes(gates)
     consts = tables()
     by_source = (q, None, None, tile, length)
     nat = pl.BlockSpec((None, rows, tile, LANES), lambda a, b: (a, 0, b, 0))
-    kern = pl.BlockSpec((None, 2, tile, SPAN), lambda a, b: (a, 0, b, 0))
     return pl.pallas_call(
         functools.partial(unmix_body, (q, g, pieces, blocks)),
         grid=(g, shard // tile),
         in_specs=[
             pl.BlockSpec((q, None, tile, length), lambda a, b: (0, a, b, 0)),
-            pl.BlockSpec(by_source, lambda a, b: (0, a, 1, b, 0)),
             pl.BlockSpec(by_source, lambda a, b: (0, a, 0, b, 0)),
             nat,
-            nat,
-            kern,
+            pl.BlockSpec((None, 2, tile, SPAN), lambda a, b: (a, 0, b, 0)),
         ]
         + [whole(c) for c in consts],
         out_specs=[
             pl.BlockSpec((q, None, 2, tile, length), lambda a, b: (0, a, 0, b, 0)),
-            kern,
+            nat,
         ],
         out_shape=[
             jax.ShapeDtypeStruct((q, g, 2, shard, length), BF16),
-            jax.ShapeDtypeStruct((g, 2, shard, SPAN), F32),
+            jax.ShapeDtypeStruct((g, rows, shard, LANES), BF16),
         ],
-        scratch_shapes=conv_scratch(tile, rows, blocks, 2 * blocks + 1),
+        scratch_shapes=conv_scratch(tile, rows, blocks, blocks + 1),
         compiler_params=params(),
         name="unmix",
-    )(grads, gates, gates, conv_one, carried, taps, *consts)
+    )(grads, gates, conv_one, taps, *consts)
+
+
+def tap_grads(grads, gates, carried, grad_one, before=()):
+    q, g, shard, length, tile, pieces, rows, blocks = conv_sizes(gates)
+    consts = tables()
+    nat = pl.BlockSpec((None, rows, tile, LANES), lambda a, b: (a, 0, b, 0))
+    return pl.pallas_call(
+        functools.partial(tap_body, (q, g, pieces, blocks), len(before)),
+        grid=(g, shard // tile),
+        in_specs=[
+            pl.BlockSpec((q, None, tile, length), lambda a, b: (0, a, b, 0)),
+            pl.BlockSpec((q, None, None, tile, length), lambda a, b: (0, a, 1, b, 0)),
+            nat,
+            nat,
+        ]
+        + [whole(c) for c in consts]
+        + [pl.BlockSpec(memory_space=pl.ANY)] * len(before),
+        out_specs=pl.BlockSpec((None, 2, tile, SPAN), lambda a, b: (a, 0, b, 0)),
+        out_shape=jax.ShapeDtypeStruct((g, 2, shard, SPAN), F32),
+        scratch_shapes=conv_scratch(tile, rows, blocks, 2 * blocks),
+        compiler_params=params(),
+        name="tap_grads",
+    )(grads, gates, carried, grad_one, *consts, *before)
 
 
 def standardise(stream):
@@ -429,6 +467,15 @@
 
 def transposed(x):
     return jnp.transpose(x.astype(F32))
+
+
+def column(row_ref):
+    row = row_ref[...]
+    return jnp.transpose(jnp.broadcast_to(row, (8, row.shape[1])))[:, 0:1]
+
+
+def as_row(column):
+    return jnp.transpose(jnp.broadcast_to(column, (column.shape[0], LANES)))[0:1]
 
 
 def gelu_pair(x):
@@ -504,7 +551,7 @@
         first(place_ref[0] == 0, dense, cut, body)
 
     unit, _ = standardise(x)
-    normed = unit * gain_ref[...] + bias_ref[...]
+    normed = unit * column(gain_ref) + column(bias_ref)
     n_ref[...] = transposed(normed).astype(BF16)
     normed = normed.astype(BF16)
     width = normed.shape[0]
@@ -584,7 +631,7 @@
     s1 = s_ref[...] + jnp.dot(wo_t[...], gated, preferred_element_type=F32)
     s1_ref[...] = s1
     unit, _ = standardise(s1)
-    normed = unit * gain_ref[...] + bias_ref[...]
+    normed = unit * column(gain_ref) + column(bias_ref)
     n_ref[...] = transposed(normed).astype(BF16)
     normed = normed.astype(BF16)
     total = s1
@@ -629,13 +676,14 @@
 
 def backward_body(natural, ways, gs_ref, d_ref, s1_ref, c_ref, g_ref, wo_ref, gain_ref, *rest):
     ff, rest = rest[:ways], rest[ways:]
-    pre_ref, gs1_ref, gc_ref, two_ref, dm_ref, do_ref, gain_out, bias_out, up_n = rest
+    pre_ref, gs1_ref, gc_ref, two_ref, dm_ref, do_ref, gain_out, bias_out = rest[:8]
+    up_n, gain_sum, bias_sum = rest[8:]
     width = ff[0].shape[-1]
 
     @pl.when(pl.program_id(0) == 0)
     def _():
-        gain_out[...] = jnp.zeros_like(gain_out)
-        bias_out[...] = jnp.zeros_like(bias_out)
+        gain_sum[...] = jnp.zeros_like(gain_sum)
+        bias_sum[...] = jnp.zeros_like(bias_sum)
         for ref, blocks, part, units in ff_chunks(ff):
             block = ref[blocks, 0:part, :].reshape(units.stop - units.start, width)
             up_n[:, units] = transposed(block).astype(BF16)
@@ -654,9 +702,15 @@
         pre = pre.astype(BF16)
         pre_ref[units, :] = pre
         total = add(total, jnp.dot(up_n[:, units], pre, preferred_element_type=F32))
-    back, gain_part, bias_part = standardise_back(total, gain_ref[...], s1_ref[...])
-    gain_out[...] += gain_part
-    bias_out[...] += bias_part
+    back, gain_part, bias_part = standardise_back(total, column(gain_ref), s1_ref[...])
+    gain_sum[...] += gain_part
+    bias_sum[...] += bias_part
+
+    @pl.when(pl.program_id(0) == pl.num_programs(0) - 1)
+    def _():
+        gain_out[...] = as_row(gain_sum[...])
+        bias_out[...] = as_row(bias_sum[...])
+
     grad = grad + back
     gs1_ref[...] = grad
     do_ref[...] = transposed(grad).astype(BF16)
@@ -675,14 +729,14 @@
     flat = pl.BlockSpec((width, t), lambda i: (0, i))
     chan = pl.BlockSpec((channels, t), lambda i: (0, i))
     high = pl.BlockSpec((hidden, t), lambda i: (0, i))
-    column = pl.BlockSpec((width, 1), lambda i: (0, 0))
+    row = pl.BlockSpec((1, width), lambda i: (0, 0))
     return pl.pallas_call(
         functools.partial(backward_body, natural, len(ff)),
         grid=(length // t,),
         in_specs=[tall if natural else flat, high, flat, chan, chan]
         + [whole(w_out), whole(gain)]
         + ff.specs(),
-        out_specs=[high, flat, chan, chan, tall, tall, column, column],
+        out_specs=[high, flat, chan, chan, tall, tall, row, row],
         out_shape=[
             jax.ShapeDtypeStruct((hidden, length), BF16),
             jax.ShapeDtypeStruct((width, length), F32),
@@ -690,10 +744,14 @@
             jax.ShapeDtypeStruct((channels, length), BF16),
             jax.ShapeDtypeStruct((length, width), BF16),
             jax.ShapeDtypeStruct((length, width), BF16),
-            jax.ShapeDtypeStruct((width, 1), F32),
-            jax.ShapeDtypeStruct((width, 1), F32),
+            jax.ShapeDtypeStruct((1, width), F32),
+            jax.ShapeDtypeStruct((1, width), F32),
         ],
-        scratch_shapes=[pltpu.VMEM((width, hidden), BF16)],
+        scratch_shapes=[
+            pltpu.VMEM((width, hidden), BF16),
+            pltpu.VMEM((width, 1), F32),
+            pltpu.VMEM((width, 1), F32),
+        ],
         compiler_params=params(),
         name="backward_block",
     )(grad, slope, s1, conv_two, gate_two, w_out, gain, *ff.arrays)
@@ -701,14 +759,14 @@
 
 def unproject_body(natural, ways, groups, place_ref, gm_ref, two_ref, s_ref, gs_ref, gain_ref, *rest):
     dense, rest = rest[:ways], rest[ways:]
-    out_ref, gain_out, bias_out, pair_t, value_t = rest
+    out_ref, gain_out, bias_out, pair_t, value_t, gain_sum, bias_sum = rest
     mp, cut, t = two_ref.shape
     width = dense[0].shape[-1]
 
     @pl.when(pl.program_id(0) == 0)
     def _():
-        gain_out[...] = jnp.zeros_like(gain_out)
-        bias_out[...] = jnp.zeros_like(bias_out)
+        gain_sum[...] = jnp.zeros_like(gain_sum)
+        bias_sum[...] = jnp.zeros_like(bias_sum)
 
         def body(pair, value):
             rows = by_channel(pair, groups).reshape(mp * 2 * cut, width)
@@ -722,9 +780,15 @@
     grad = jnp.dot(pair_t[...], pair.reshape(mp * 2 * cut, t), preferred_element_type=F32)
     value = gm_ref[:, 1].reshape(mp * cut, t)
     grad = grad + jnp.dot(value_t[...], value, preferred_element_type=F32)
-    back, gain_part, bias_part = standardise_back(grad, gain_ref[...], s_ref[...])
-    gain_out[...] += gain_part
-    bias_out[...] += bias_part
+    back, gain_part, bias_part = standardise_back(grad, column(gain_ref), s_ref[...])
+    gain_sum[...] += gain_part
+    bias_sum[...] += bias_part
+
+    @pl.when(pl.program_id(0) == pl.num_programs(0) - 1)
+    def _():
+        gain_out[...] = as_row(gain_sum[...])
+        bias_out[...] = as_row(bias_sum[...])
+
     result = gs_ref[...] + back
     out_ref[...] = transposed(result) if natural else result
 
@@ -735,7 +799,7 @@
     t = token_tile(length)
     tall = pl.BlockSpec((t, width), lambda i: (i, 0))
     flat = pl.BlockSpec((width, t), lambda i: (0, i))
-    column = pl.BlockSpec((width, 1), lambda i: (0, 0))
+    row = pl.BlockSpec((1, width), lambda i: (0, 0))
     last = (length, width) if natural else (width, length)
     return pl.pallas_call(
         functools.partial(unproject_body, natural, len(dense), groups),
@@ -749,15 +813,17 @@
             whole(gain),
         ]
         + dense.specs(),
-        out_specs=[tall if natural else flat, column, column],
+        out_specs=[tall if natural else flat, row, row],
         out_shape=[
             jax.ShapeDtypeStruct(last, F32),
-            jax.ShapeDtypeStruct((width, 1), F32),
-            jax.ShapeDtypeStruct((width, 1), F32),
+            jax.ShapeDtypeStruct((1, width), F32),
+            jax.ShapeDtypeStruct((1, width), F32),
         ],
         scratch_shapes=[
             pltpu.VMEM((width, mp * 2 * cut), BF16),
             pltpu.VMEM((width, mp * cut), BF16),
+            pltpu.VMEM((width, 1), F32),
+            pltpu.VMEM((width, 1), F32),
         ],
         compiler_params=params(),
         name="unproject",
@@ -1148,14 +1214,18 @@
     kept = widen(kept, 2)
     taps = []
 
-    chains = Chains()
-    bits = mp.bit_length() - 1
-    for i in range(2):
-        rows = dense[0, i * dense_rows // 2 : (i + 1) * dense_rows // 2]
-        stages = [[b] for b in range(bits - 1, 1, -1)] + [[1 - i], [i]]
-        chains.add(i, gather_chain(rows, mp, stages))
+    def dense_chains(layer):
+        result = Chains()
+        bits = mp.bit_length() - 1
+        for i in range(2):
+            rows = dense[layer, i * dense_rows // 2 : (i + 1) * dense_rows // 2]
+            stages = [[b] for b in range(bits - 1, 1, -1)] + [[1 - i], [i]]
+            result.add(i, gather_chain(rows, mp, stages))
+        return result
+
+    chains = dense_chains(0)
     own, other = pick(inputs)
-    mine, other = chains.tie(ff[0], other)
+    mine, other = chains.tie(ff.reshape(-1, width), other)
     ff_mine = gathered(mine)
     (other,) = chains.finish(chains.start(), other)
     moves = [other[: chunk // 2], other[chunk // 2 :], kept[0]]
@@ -1177,10 +1247,9 @@
     stream = ordered(own, other).reshape(length, width)
     none = [0] * ways
     dense_all = [Pieces(shared(dense_mine), none, dense_rows)]
-    ff_all = []
-
-    gains = norm_gain[..., None]
-    biases = norm_bias[..., None]
+
+    gains = norm_gain[:, :, None]
+    biases = norm_bias[:, :, None]
     saved, out_all = [], []
     own_grad, grad = pick(cotangent)
     less = chunk // 32 * 12
@@ -1201,29 +1270,29 @@
         if natural:
             stream, got = got[0], got[1:]
         operand, gate_two, normed_one = got
-        if natural:
-            ff_mine, operand = together(ff_mine, operand)
-            ff_pair = shared(ff_mine)
-        if more:
-            mine, operand = together(dense[layer + 1], operand)
-            dense_next = gathered(mine)
         gates = exchange(operand.reshape(peers, groups, 2, cut, length))
         taps.append(ordered(kept[layer], got_taps))
+        if more:
+            following = Chains()
+            whole_bits = list(range(mp.bit_length() - 1))
+            stages = [whole_bits[i : i + 2] for i in range(2, len(whole_bits), 2)]
+            following.add(0, gather_chain(dense[layer + 1], mp, stages + [whole_bits[:2]]))
+            (gates,) = following.tie(gates)
+            started = following.start()
         if natural:
-            gates, *ff_pair = together(gates, *ff_pair)
-        else:
             ff_mine, gates = together(ff_mine, gates)
             ff_pair = shared(ff_mine)
         conv_two, conv_one, carried = mix(gates, taps[layer])
-        conv_two, *ff_pair = together(conv_two, *ff_pair)
-        ff_all.append(Pieces(ff_pair, none, 2 * part))
         out_all.append(out_matrix(dense_all[layer]))
         if more:
-            mine, conv_two = together(ff[layer + 1], conv_two)
-            ff_mine = gathered(mine)
+            (conv_two,) = following.finish(started, conv_two)
         conv_two = exchange(conv_two).reshape(mp * cut, length)
+        if natural:
+            conv_two, *ff_pair = together(conv_two, *ff_pair)
+            ff_all = [Pieces(ff_pair, [2 * part * i] * ways, 2 * part) for i in range(layers)]
         if more:
-            got_taps, conv_two = together(kept[layer + 1], conv_two)
+            got_taps, conv_two = following.tie(kept[layer + 1], conv_two)
+            started = following.start()
             got_taps = lax.ppermute(got_taps, "mp", swap)
         half = None
         if layer >= layers - 2:
@@ -1245,7 +1314,10 @@
             half, s2 = together(half, s2)
             halves_of_grad[layer - layers + 2] = half
         if more:
-            dense_next, got_taps, s2 = together(dense_next, got_taps, s2)
+            got_taps, s2 = following.finish(started, got_taps, s2)
+            while following.waiting:
+                following.finish(following.start())
+            dense_next = following.results[0]
             dense_all.append(Pieces(shared(dense_next), none, dense_rows))
         saved.append(
             (stream, normed_one, gates, conv_one, carried, conv_two, gate_two)
@@ -1299,9 +1371,8 @@
         chains.add(("flip", layer), chip_chain(early, dp))
         (grad_conv,) = chains.tie(grad_conv)
         started = chains.start()
-        grad_mixed, dk = unmix(grad_conv, gates, conv_one, carried, taps[layer])
+        grad_mixed, grad_one = unmix(grad_conv, gates, conv_one, taps[layer])
         (grad_mixed,) = chains.finish(started, grad_mixed)
-        own_dk, other_dk = pick(dk.astype(BF16))
         if layer == layers - 1:
             more_output, grad_mixed = together(more_output, grad_mixed)
         grad_mixed = exchange(grad_mixed).reshape(mp, 2, cut, length)
@@ -1310,7 +1381,13 @@
             output = ordered(own_output, output.astype(F32))
             output, grad_mixed = together(output, grad_mixed)
         terms = chains.results.pop(("flip", layer))
-        chains.add(layer, scatter_chain(terms, mp, stage_order(mp, 0), True))
+        stages = stage_order(mp, 0)
+        if layer == 0:
+            stages = [[b] for stage in stages for b in stage]
+        chains.add(layer, scatter_chain(terms, mp, stages, True))
+        dk = tap_grads(grad_conv, gates, carried, grad_one, [] if layer else chains.operands())
+        grad_mixed, dk = together(grad_mixed, dk)
+        own_dk, other_dk = pick(dk.astype(BF16))
         if layer:
             later = grad_mixed, normed_one
         else:
@@ -1339,29 +1416,30 @@
             got_dk = lax.ppermute(other_dk, "mp", swap)
             started = chains.start()
 
-    (grad,) = tail.finish(last, grad)
+    grad, got_dk = tail.finish(last, grad, got_dk)
     own, other = pick(grad.reshape(groups, chunk, width))
     swapped = lax.ppermute(other.astype(BF16), "mp", swap)
     (gain_rows[0][0],) = chains.finish(started, gain_rows[0][0])
-    chains.results.update(tail.results)
     bits = list(range(mp.bit_length() - 1))
     quarters = [bits[i : i + 2] for i in range(0, len(bits), 2)]
     norms = jnp.stack([jnp.stack([jnp.stack(r) for r in rows]) for rows in (gain_rows, bias_rows)])
-    shape = norms.shape[:-1]
+    shape = norms.shape[:-2] + (width,)
     norms = norms.reshape(-1, width)
-    chains.add("late", last_chain(chains.results.pop("late"), norms, mp, quarters))
-    rounds = 0
-    while chains.waiting:
-        started = chains.start()
-        if rounds == 0:
-            swapped, got_dk = chains.finish(started, swapped, got_dk)
-        else:
+    tail.add("late", last_chain(tail.results.pop("late"), norms, mp, quarters))
+    first_round = True
+    while chains.waiting or tail.waiting:
+        started, last = chains.start(), tail.start()
+        if started:
             chains.finish(started)
-        rounds += 1
+        if first_round:
+            (swapped,) = tail.finish(last, swapped)
+        elif last:
+            tail.finish(last)
+        first_round = False
     input_grad = ordered(own, swapped.astype(F32))
     dks[0] = own_dk.astype(F32) + got_dk.astype(F32)
     dk = jnp.stack(dks).astype(BF16).astype(F32)
-    late, norms = chains.results.pop("late")
+    late, norms = tail.results.pop("late")
     found = [chains.results.pop(layer) for layer in reversed(range(layers))]
     final = [x.astype(BF16) for x in found + [late]]
     if ways == 1:

time: 898 us -> 870 us (0.969); the launches traced: 880 us -> 862 us
  waiting for transfers between devices: 341 us -> 310 us
  local copies, waits for them, and re-layouts: 56.7 us -> 39.6 us
  Pallas kernels: 293 us -> 310 us
  starting transfers between devices: 107 us -> 120 us
    all_gather x3 -> x1, waiting for transfers between devices: 65.5 us -> 0.01 us  [gathered(): return lax.all_gather(x, 'mp', axis=0)]
    all_to_all x8, waiting for transfers between devices: 98.2 us -> 136 us  [exchange(): lax.all_to_all(x, 'mp', split_axis=0, concat_axis=0, tiled=True, axis_ind...]
    pallas_call x0 -> x2, Pallas kernels: none -> 32.7 us  [tap_grads(): pl.pallas_call(functools.partial(tap_body, (q, g, pieces, blocks), len(be...]
    ppermute x37 -> x41, waiting for transfers between devices: 113 us -> 92.5 us  [flip(): return lax.ppermute(x, axis, [(i, i ^ bit) for i in range(size)])]
    pallas_call x2, Pallas kernels: 49.3 us -> 32.4 us  [unmix(): pl.pallas_call(functools.partial(unmix_body, (q, g, pieces, blocks)), gri...]
    ppermute x37 -> x41, starting transfers between devices: 57.1 us -> 73.8 us  [flip(): return lax.ppermute(x, axis, [(i, i ^ bit) for i in range(size)])]
    ppermute x1, waiting for transfers between devices: 3.23 us -> 15.7 us  [program(): swapped = lax.ppermute(other.astype(BF16), 'mp', swap)]
    slice x8 -> x6, local copies, waits for them, and re-layouts: 22.1 us -> 13.4 us  [take(): return t[tuple(index)]]
  transfers between devices with their start and end apart: 59 -> 61, of which waited for: 25 -> 26; matrix products, arithmetic and copies ran while one was open for 11% -> 10% of each run, Pallas kernels for 32% -> 31%
where the time goes in v3:
time: 870 us; the launch traced here: 862 us
  waiting for transfers between devices  310 us (36%)
  Pallas kernels  310 us (36%)
  starting transfers between devices  120 us (14%)
  other arithmetic  66.6 us (8%)
  local copies, waits for them, and re-layouts  39.6 us (5%)
  between operations  15.9 us (2%)
    all_to_all x8, waiting for transfers between devices, exchange(): lax.all_to_all(x, 'mp', split_axis=0, concat_axis=0, tiled=True, axis_ind...  136 us
    ppermute x41, waiting for transfers between devices, flip(): return lax.ppermute(x, axis, [(i, i ^ bit) for i in range(size)])  92.5 us
    ppermute x41, starting transfers between devices, flip(): return lax.ppermute(x, axis, [(i, i ^ bit) for i in range(size)])  73.8 us
    ppermute x3, waiting for transfers between devices, program(): got = lax.ppermute(now, 'mp', swap)  62.7 us
    pallas_call x2, Pallas kernels, forward_block(): pl.pallas_call(functools.partial(forward_body, natural, len(ff)), grid=(l...  61.8 us
    pallas_call x3, Pallas kernels, weight_grads(): pl.pallas_call(functools.partial(grads_body, ways, jobs, len(before)), gr...  52.7 us
    pallas_call x2, Pallas kernels, backward_block(): pl.pallas_call(functools.partial(backward_body, natural, len(ff)), grid=(...  51 us
    all_to_all x8, starting transfers between devices, exchange(): lax.all_to_all(x, 'mp', split_axis=0, concat_axis=0, tiled=True, axis_ind...  38.7 us
  transfers between devices with their start and end apart: 61, of which 26 were waited for; matrix products, arithmetic and copies ran while one was open for 10% of the time, Pallas kernels for 31%

profile of v3, /device:TPU:1, one launch (start us, length us, event | category | flops | bytes accessed | tf_op | source)
XLA Modules:
  0.0 861.8 jit_solution(13886714813376586869)
XLA Ops:
  27.4 12.8 %collective-permute-done.3 = bf16[2,48,768]{2,1,0:T(8,128)(2,1)} collective-permute-done((bf16[2,48,768]{2,1,0:T(8,128)(2,1)S(1)}, bf16[2,48,768]{2,1,0:T(8,128)(2,1)}, u32[]{:S(2)}, u32[]{:S(2)}) %collective-permute-start.3) | collective-permute-done | bytes 147488 | tf_op jit(solution)/shard_map/ppermute | solution.py:943
  72.1 27.3 %collective-permute-done.7 = bf16[256,768]{1,0:T(8,128)(2,1)S(1)} collective-permute-done((bf16[256,768]{1,0:T(8,128)(2,1)S(1)}, bf16[256,768]{1,0:T(8,128)(2,1)S(1)}, u32[]{:S(2)}, u32[]{:S(2)}) %collective-permute-start.7) | collective-permute-done | bytes 393248 | tf_op jit(solution)/shard_map/ppermute | solution.py:1236
  99.8 26.4 %collective-permute-done.10 = bf16[2,48,2048]{2,1,0:T(8,128)(2,1)S(1)} collective-permute-done((bf16[2,48,2048]{2,1,0:T(8,128)(2,1)S(1)}, bf16[2,48,2048]{2,1,0:T(8,128)(2,1)S(1)}, u32[]{:S(2)}, u32[]{:S(2)}) %collective-permute-start.10) | collective-permute-done | bytes 393248 | tf_op jit(solution)/shard_map/ppermute | solution.py:1236
  149.7 55.0 %all-to-all-done.v_ref.g_ref = bf16[8,2,2,48,1024]{4,3,2,1,0:T(8,128)(2,1)} async-done(((bf16[8,2,2,48,1024]{4,3,2,1,0:T(8,128)(2,1)}), bf16[8,2,2,48,1024]{4,3,2,1,0:T(8,128)(2,1)}, u32[]{:S(2)}, u32[]{:S(2)}) %all-to-all-start) | async-done | bytes 3145760 | tf_op jit(solution)/shard_map/all_to_all | solution.py:1173
  209.8 16.0 %mix.2 = (bf16[8,2,48,1024]{3,2,1,0:T(8,128)(2,1)}, bf16[2,64,48,128]{3,2,1,0:T(8,128)(2,1)}, bf16[2,64,48,128]{3,2,1,0:T(8,128)(2,1)}) custom-call(bf16[8,2,2,48,1024]{4,3,2,1,0:T(8,128)(2,1)} %all-to-all-done.v_ref.g_ref, bf16[8,2,2,48,1024]{4,3,2,1,0:T(8,128)(2,1)} %all-to-all-done.v_ref.g_ref, bf16[2,2,48,2048]{3,2,1,0:T(8,128)(2,1)} %pad_maximum_fusion.11.k_ref, ...), custom_call_target="tpu_custom_call" | custom-call | tf_op jit(solution)/shard_map/mix/pallas_call | solution.py:377
  230.6 19.1 %all-to-all-done.1 = bf16[8,2,48,1024]{3,2,1,0:T(8,128)(2,1)} async-done(((bf16[8,2,48,1024]{3,2,1,0:T(8,128)(2,1)}), bf16[8,2,48,1024]{3,2,1,0:T(8,128)(2,1)}, u32[]{:S(2)}, u32[]{:S(2)}) %all-to-all-start.1) | async-done | bytes 1572896 | tf_op jit(solution)/shard_map/all_to_all | solution.py:1173
  259.7 30.8 %forward_block.2 = (f32[768,1024]{1,0:T(8,128)}, f32[768,1024]{1,0:T(8,128)}, bf16[3072,1024]{1,0:T(8,128)(2,1)}, bf16[3072,1024]{1,0:T(8,128)(2,1)}, bf16[1024,...) custom-call(f32[768,1024]{1,0:T(8,128)} %get-tuple-element.213.s_ref, bf16[768,1024]{1,0:T(8,128)(2,1)} %bitcast.52.c_ref, ...), custom_call_target="tpu_custom_call" | custom-call | tf_op jit(solution)/shard_map/forward_block/pallas_call | solution.py:658
  319.1 35.6 %all-to-all-done.2.v_ref.g_ref = bf16[8,2,2,48,1024]{4,3,2,1,0:T(8,128)(2,1)} async-done(((bf16[8,2,2,48,1024]{4,3,2,1,0:T(8,128)(2,1)}), bf16[8,2,2,48,1024]{4,3,2,1,0:T(8,128)(2,1)}, u32[]{:S(2)}, u32[]{:S(2)}) %all-to-all-start.2) | async-done | bytes 3145760 | tf_op jit(solution)/shard_map/all_to_all | solution.py:1173
  354.6 16.0 %mix.3 = (bf16[8,2,48,1024]{3,2,1,0:T(8,128)(2,1)}, bf16[2,64,48,128]{3,2,1,0:T(8,128)(2,1)}, bf16[2,64,48,128]{3,2,1,0:T(8,128)(2,1)}) custom-call(bf16[8,2,2,48,1024]{4,3,2,1,0:T(8,128)(2,1)} %all-to-all-done.2.v_ref.g_ref, bf16[8,2,2,48,1024]{4,3,2,1,0:T(8,128)(2,1)} %all-to-all-done.2.v_ref.g_ref, bf16[2,2,48,2048]{3,2,1,0:T(8,128)(2,1)} %pad_maximum_fusion.12.k_ref, ...), custom_call_target="tpu_custom_call" | custom-call | tf_op jit(solution)/shard_map/mix/pallas_call | solution.py:377
  378.5 19.7 %all-to-all-done.3 = bf16[8,2,48,1024]{3,2,1,0:T(8,128)(2,1)} async-done(((bf16[8,2,48,1024]{3,2,1,0:T(8,128)(2,1)}), bf16[8,2,48,1024]{3,2,1,0:T(8,128)(2,1)}, u32[]{:S(2)}, u32[]{:S(2)}) %all-to-all-start.3) | async-done | bytes 1572896 | tf_op jit(solution)/shard_map/all_to_all | solution.py:1173
  401.3 31.0 %forward_block.3 = (f32[768,1024]{1,0:T(8,128)}, f32[1024,768]{1,0:T(8,128)}, bf16[3072,1024]{1,0:T(8,128)(2,1)}, bf16[3072,1024]{1,0:T(8,128)(2,1)}, bf16[1024,...) custom-call(f32[768,1024]{1,0:T(8,128)} %get-tuple-element.220.x_ref.s_ref, bf16[768,1024]{1,0:T(8,128)(2,1)} %bitcast.72.c_ref, ...), custom_call_target="tpu_custom_call" | custom-call | tf_op jit(solution)/shard_map/forward_block/pallas_call | solution.py:658
  438.1 25.0 %backward_block.2 = (bf16[3072,1024]{1,0:T(8,128)(2,1)}, f32[768,1024]{1,0:T(8,128)}, bf16[768,1024]{1,0:T(8,128)(2,1)}, bf16[768,1024]{1,0:T(8,128)(2,1)}, bf16...) custom-call(bf16[1024,768]{1,0:T(8,128)(2,1)} %bitcast.397, ...), custom_call_target="tpu_custom_call" | custom-call | tf_op jit(solution)/shard_map/backward_block/pallas_call | solution.py:733
  467.0 21.1 %early_grads.2 = (bf16[16,240,768]{2,1,0:T(8,128)(2,1)}, bf16[16,240,768]{2,1,0:T(8,128)(2,1)}) custom-call(s32[2]{0:T(128)} %pad_add_fusion.place_ref, bf16[2,16,96,1024]{3,2,1,0:T(8,128)(2,1)} %bitcast.406, bf16[2,16,96,1024]{3,2,1,0:T(8,128)(2,1)} %bitcast.404, bf16[8,2,48,1024]{3,2,1,0:T(8,128)(2,1)} %bitcast.400, bf16[8,2,48,1024]{3,2,1,0:T(8,128)(2,1)} %bitcast.420, ...), custom_call_target="tpu_custom_call" | custom-call | tf_op jit(solution)/shard_map/early_grads/pallas_call | solution.py:922
  490.5 16.2 %unmix.2 = (bf16[8,2,2,48,1024]{4,3,2,1,0:T(8,128)(2,1)}, bf16[2,64,48,128]{3,2,1,0:T(8,128)(2,1)}) custom-call(bf16[8,2,48,1024]{3,2,1,0:T(8,128)(2,1)} %copy-done.9, bf16[8,2,2,48,1024]{4,3,2,1,0:T(8,128)(2,1)} %all-to-all-done.2.v_ref.g_ref, bf16[2,64,48,128]{3,2,1,0:T(8,128)(2,1)} %get-tuple-element.255.one_ref, ...), custom_call_target="tpu_custom_call" | custom-call | tf_op jit(solution)/shard_map/unmix/pallas_call | solution.py:403
  514.9 16.4 %tap_grads.2 = f32[2,2,48,2048]{3,2,1,0:T(8,128)} custom-call(bf16[8,2,48,1024]{3,2,1,0:T(8,128)(2,1)} %copy-done.9, bf16[8,2,2,48,1024]{4,3,2,1,0:T(8,128)(2,1)} %all-to-all-done.2.v_ref.g_ref, bf16[2,64,48,128]{3,2,1,0:T(8,128)(2,1)} %get-tuple-element.264.carried_ref, bf16[2,64,48,128]{3,2,1,0:T(8,128)(2,1)} %get-tuple-element.265.grad_ref, ...), custom_call_target="tpu_custom_call" | custom-call | tf_op jit(solution)/shard_map/tap_grads/pallas_call | solution.py:431
  553.1 12.8 %unproject.2 = (f32[768,1024]{1,0:T(8,128)}, f32[1,768]{1,0:T(1,128)}, f32[1,768]{1,0:T(1,128)}) custom-call(s32[2]{0:T(128)} %pad_add_fusion.place_ref, bf16[16,2,48,1024]{3,2,1,0:T(8,128)(2,1)} %bitcast.89.gm_ref, bf16[16,48,1024]{2,1,0:T(8,128)(2,1)} %bitcast.401, f32[768,1024]{1,0:T(8,128)} %get-tuple-element.220.x_ref.s_ref, ...), custom_call_target="tpu_custom_call" | custom-call | tf_op jit(solution)/shard_map/unproject/pallas_call | solution.py:804
  573.0 26.0 %backward_block.3 = (bf16[3072,1024]{1,0:T(8,128)(2,1)}, f32[768,1024]{1,0:T(8,128)}, bf16[768,1024]{1,0:T(8,128)(2,1)}, bf16[768,1024]{1,0:T(8,128)(2,1)}, bf16...) custom-call(f32[768,1024]{1,0:T(8,128)} %get-tuple-element.273.gs_ref, ...), custom_call_target="tpu_custom_call" | custom-call | tf_op jit(solution)/shard_map/backward_block/pallas_call | solution.py:733
  611.0 25.0 %early_grads.3 = (bf16[16,288,768]{2,1,0:T(8,128)(2,1)}, bf16[16,288,768]{2,1,0:T(8,128)(2,1)}) custom-call(s32[2]{0:T(128)} %pad_add_fusion.place_ref, bf16[2,16,96,1024]{3,2,1,0:T(8,128)(2,1)} %bitcast.405, bf16[2,16,96,1024]{3,2,1,0:T(8,128)(2,1)} %bitcast.403, bf16[8,2,48,1024]{3,2,1,0:T(8,128)(2,1)} %bitcast.398, bf16[8,2,48,1024]{3,2,1,0:T(8,128)(2,1)} %bitcast.419, ...), custom_call_target="tpu_custom_call" | custom-call | tf_op jit(solution)/shard_map/early_grads/pallas_call | solution.py:922
  645.6 16.2 %unmix.3 = (bf16[8,2,2,48,1024]{4,3,2,1,0:T(8,128)(2,1)}, bf16[2,64,48,128]{3,2,1,0:T(8,128)(2,1)}) custom-call(bf16[8,2,48,1024]{3,2,1,0:T(8,128)(2,1)} %copy-done.8, bf16[8,2,2,48,1024]{4,3,2,1,0:T(8,128)(2,1)} %all-to-all-done.v_ref.g_ref, bf16[2,64,48,128]{3,2,1,0:T(8,128)(2,1)} %get-tuple-element.298.one_ref, ...), custom_call_target="tpu_custom_call" | custom-call | tf_op jit(solution)/shard_map/unmix/pallas_call | solution.py:403
  690.2 16.3 %tap_grads.3 = f32[2,2,48,2048]{3,2,1,0:T(8,128)} custom-call(bf16[8,2,48,1024]{3,2,1,0:T(8,128)(2,1)} %copy-done.8, bf16[8,2,2,48,1024]{4,3,2,1,0:T(8,128)(2,1)} %all-to-all-done.v_ref.g_ref, bf16[2,64,48,128]{3,2,1,0:T(8,128)(2,1)} %get-tuple-element.301.carried_ref, bf16[2,64,48,128]{3,2,1,0:T(8,128)(2,1)} %get-tuple-element.302.grad_ref, ...), custom_call_target="tpu_custom_call" | custom-call | tf_op jit(solution)/shard_map/tap_grads/pallas_call | solution.py:431
  718.5 13.5 %unproject.3 = (f32[1024,768]{1,0:T(8,128)}, f32[1,768]{1,0:T(1,128)}, f32[1,768]{1,0:T(1,128)}) custom-call(s32[2]{0:T(128)} %pad_add_fusion.place_ref, bf16[16,2,48,1024]{3,2,1,0:T(8,128)(2,1)} %bitcast.106.gm_ref, bf16[16,48,1024]{2,1,0:T(8,128)(2,1)} %bitcast.399, f32[768,1024]{1,0:T(8,128)} %get-tuple-element.213.s_ref, ...), custom_call_target="tpu_custom_call" | custom-call | tf_op jit(solution)/shard_map/unproject/pallas_call | solution.py:804
  754.7 10.5 %collective-permute-done.44 = bf16[2,2,144,768]{3,2,1,0:T(8,128)(2,1)} collective-permute-done((bf16[2,2,144,768]{3,2,1,0:T(8,128)(2,1)}, bf16[2,2,144,768]{3,2,1,0:T(8,128)(2,1)}, u32[]{:S(2)}, u32[]{:S(2)}) %collective-permute-start.44) | collective-permute-done | bytes 884768 | tf_op jit(solution)/shard_map/ppermute | solution.py:943
  783.4 23.4 %collective-permute-done.45 = bf16[2,288,768]{2,1,0:T(8,128)(2,1)S(1)} collective-permute-done((bf16[2,288,768]{2,1,0:T(8,128)(2,1)S(1)}, bf16[2,288,768]{2,1,0:T(8,128)(2,1)S(1)}, u32[]{:S(2)}, u32[]{:S(2)}) %collective-permute-start.45) | collective-permute-done | bytes 884768 | tf_op jit(solution)/shard_map/ppermute | solution.py:943
  808.3 15.7 %collective-permute-done.42 = bf16[512,768]{1,0:T(8,128)(2,1)S(1)} collective-permute-done((bf16[512,768]{1,0:T(8,128)(2,1)S(1)}, bf16[512,768]{1,0:T(8,128)(2,1)S(1)}, u32[]{:S(2)}, u32[]{:S(2)}) %collective-permute-start.42) | collective-permute-done | bytes 786464 | tf_op jit(solution)/shard_map/ppermute | solution.py:1421
  (377 shorter events, 318.1 us)
Async XLA Ops:
  7.2 197.5 %all-gather.3.cloned.1.call-start = ((), (), s32[]{:S(2)}) async-start(), calls=%async_computation.8 | async-start | bytes 10027008 | tf_op jit(solution)/shard_map/all_gather | solution.py:1197
  58.6 40.7 %collective-permute-start.7 = (bf16[256,768]{1,0:T(8,128)(2,1)S(1)}, bf16[256,768]{1,0:T(8,128)(2,1)S(1)}, u32[]{:S(2)}, u32[]{:S(2)}) collective-permute-start(bf16[256,768]{1,0:T(8,128)(2,1)S(1)} %copy-done.37), channel_id=1, source_target_pairs={{0,8},{1,9},{2,10},{3,11},{4,12},{5,13},{6,14},{7,15},{8,0},{9,1},... | collective-permute-start | bytes 1179656 | tf_op jit(solution)/shard_map/ppermute | solution.py:1236
  145.1 59.7 %all-to-all-start = ((bf16[8,2,2,48,1024]{4,3,2,1,0:T(8,128)(2,1)}), bf16[8,2,2,48,1024]{4,3,2,1,0:T(8,128)(2,1)}, u32[]{:S(2)}, u32[]{:S(2)}) async-start(bf16[8,2,2,48,1024]{4,3,2,1,0:T(8,128)(2,1)} %bitcast.417), calls=%async_computation | async-start | bytes 6291456 | tf_op jit(solution)/shard_map/all_to_all | solution.py:1173
  204.7 45.0 %collective-permute-start.15 = (bf16[16,384,768]{2,1,0:T(8,128)(2,1)}, bf16[16,384,768]{2,1,0:T(8,128)(2,1)}, u32[]{:S(2)}, u32[]{:S(2)}) collective-permute-start(bf16[16,384,768]{2,1,0:T(8,128)(2,1)} %bitcast.378), channel_id=1, source_target_pairs={{0,16},{16,0},{1,17},{17,1},{2,18},{18,2},{3,19},{19,3},{4,20},{20... | collective-permute-start | bytes 28311560 | tf_op jit(solution)/shard_map/ppermute | solution.py:943
  249.7 40.9 %collective-permute-start.16 = (bf16[2,2,96,768]{3,2,1,0:T(8,128)(2,1)S(1)}, bf16[2,2,96,768]{3,2,1,0:T(8,128)(2,1)}, u32[]{:S(2)}, u32[]{:S(2)}) collective-permute-start(bf16[2,2,96,768]{3,2,1,0:T(8,128)(2,1)S(1)} %pad_maximum_fusion.19), channel_id=1, source_target_pairs={{0,1},{1,0},{2,3},{3,2},{4,5},{5,4},{6,7},{7,6},{8,9},{9,8},{10,11... | collective-permute-start | bytes 1769480 | tf_op jit(solution)/shard_map/ppermute | solution.py:943
  251.4 39.2 %collective-permute-start.17 = (bf16[2,2,96,768]{3,2,1,0:T(8,128)(2,1)S(1)}, bf16[2,2,96,768]{3,2,1,0:T(8,128)(2,1)}, u32[]{:S(2)}, u32[]{:S(2)}) collective-permute-start(bf16[2,2,96,768]{3,2,1,0:T(8,128)(2,1)S(1)} %pad_maximum_fusion.19), channel_id=1, source_target_pairs={{0,2},{1,3},{2,0},{3,1},{4,6},{5,7},{6,4},{7,5},{8,10},{9,11},{10,... | collective-permute-start | bytes 1769480 | tf_op jit(solution)/shard_map/ppermute | solution.py:943
  252.6 38.0 %collective-permute-start.18 = (bf16[2,2,96,768]{3,2,1,0:T(8,128)(2,1)S(1)}, bf16[2,2,96,768]{3,2,1,0:T(8,128)(2,1)}, u32[]{:S(2)}, u32[]{:S(2)}) collective-permute-start(bf16[2,2,96,768]{3,2,1,0:T(8,128)(2,1)S(1)} %pad_maximum_fusion.19), channel_id=1, source_target_pairs={{0,3},{1,2},{2,1},{3,0},{4,7},{5,6},{6,5},{7,4},{8,11},{9,10},{10,... | collective-permute-start | bytes 1769480 | tf_op jit(solution)/shard_map/ppermute | solution.py:943
  254.0 36.5 %collective-permute-start.19 = (bf16[2,48,2048]{2,1,0:T(8,128)(2,1)}, bf16[2,48,2048]{2,1,0:T(8,128)(2,1)}, u32[]{:S(2)}, u32[]{:S(2)}) collective-permute-start(bf16[2,48,2048]{2,1,0:T(8,128)(2,1)} %get-tuple-element.210), channel_id=1, source_target_pairs={{0,8},{1,9},{2,10},{3,11},{4,12},{5,13},{6,14},{7,15},{8,0},{9,1},... | collective-permute-start | bytes 1179656 | tf_op jit(solution)/shard_map/ppermute | solution.py:1296
  255.7 34.9 %collective-permute-start.20 = (bf16[192,768]{1,0:T(8,128)(2,1)}, bf16[192,768]{1,0:T(8,128)(2,1)S(1)}, u32[]{:S(2)}, u32[]{:S(2)}) collective-permute-start(bf16[192,768]{1,0:T(8,128)(2,1)} %slice_bitcast_fusion.10), channel_id=1, source_target_pairs={{0,8},{1,9},{2,10},{3,11},{4,12},{5,13},{6,14},{7,15},{8,0},{9,1},... | collective-permute-start | bytes 884744 | tf_op jit(solution)/shard_map/ppermute | solution.py:1301
  312.0 42.6 %all-to-all-start.2 = ((bf16[8,2,2,48,1024]{4,3,2,1,0:T(8,128)(2,1)}), bf16[8,2,2,48,1024]{4,3,2,1,0:T(8,128)(2,1)}, u32[]{:S(2)}, u32[]{:S(2)}) async-start(bf16[8,2,2,48,1024]{4,3,2,1,0:T(8,128)(2,1)} %bitcast.416), calls=%async_computation.2 | async-start | bytes 6291456 | tf_op jit(solution)/shard_map/all_to_all | solution.py:1173
  398.2 34.1 %collective-permute-start.22 = (bf16[320,768]{1,0:T(8,128)(2,1)S(1)}, bf16[320,768]{1,0:T(8,128)(2,1)S(1)}, u32[]{:S(2)}, u32[]{:S(2)}) collective-permute-start(bf16[320,768]{1,0:T(8,128)(2,1)S(1)} %slice_bitcast_fusion.3), channel_id=1, source_target_pairs={{0,8},{1,9},{2,10},{3,11},{4,12},{5,13},{6,14},{7,15},{8,0},{9,1},... | collective-permute-start | bytes 1474568 | tf_op jit(solution)/shard_map/ppermute | solution.py:1301
  510.0 42.0 %all-to-all-start.5 = ((bf16[8,2,2,48,1024]{4,3,2,1,0:T(8,128)(2,1)}), bf16[8,2,2,48,1024]{4,3,2,1,0:T(8,128)(2,1)}, u32[]{:S(2)}, u32[]{:S(2)}) async-start(bf16[8,2,2,48,1024]{4,3,2,1,0:T(8,128)(2,1)} %get-tuple-element.259), calls=%async_computation.5 | async-start | bytes 6291456 | tf_op jit(solution)/shard_map/all_to_all | solution.py:1173
  565.9 37.6 %collective-permute-start.26 = (bf16[2,2,2,128,768]{4,3,1,0,2:T(8,128)(2,1)S(1)}, bf16[2,2,2,128,768]{4,3,1,0,2:T(8,128)(2,1)}, u32[]{:S(2)}, u32[]{:S(2)}) collective-permute-start(bf16[2,2,2,128,768]{4,3,1,0,2:T(8,128)(2,1)S(1)} %copy-done.30), channel_id=1, source_target_pairs={{0,1},{1,0},{2,3},{3,2},{4,5},{5,4},{6,7},{7,6},{8,9},{9,8},{10,11... | collective-permute-start | bytes 4718600 | tf_op jit(solution)/shard_map/ppermute | solution.py:943
  603.4 36.7 %all-to-all-start.6 = ((bf16[8,2,48,1024]{3,2,1,0:T(8,128)(2,1)}), bf16[8,2,48,1024]{3,2,1,0:T(8,128)(2,1)S(1)}, u32[]{:S(2)}, u32[]{:S(2)}) async-start(bf16[8,2,48,1024]{3,2,1,0:T(8,128)(2,1)} %bitcast.421), calls=%async_computation.6 | async-start | bytes 3145728 | tf_op jit(solution)/shard_map/all_to_all | solution.py:1173
  662.6 49.2 %all-to-all-start.7 = ((bf16[8,2,2,48,1024]{4,3,2,1,0:T(8,128)(2,1)}), bf16[8,2,2,48,1024]{4,3,2,1,0:T(8,128)(2,1)}, u32[]{:S(2)}, u32[]{:S(2)}) async-start(bf16[8,2,2,48,1024]{4,3,2,1,0:T(8,128)(2,1)} %get-tuple-element.300), calls=%async_computation.7 | async-start | bytes 6291456 | tf_op jit(solution)/shard_map/all_to_all | solution.py:1173
  673.4 66.9 %collective-permute-start.38 = (bf16[2,2,2,144,768]{4,3,2,1,0:T(8,128)(2,1)}, bf16[2,2,2,144,768]{4,3,2,1,0:T(8,128)(2,1)}, u32[]{:S(2)}, u32[]{:S(2)}) collective-permute-start(bf16[2,2,2,144,768]{4,3,2,1,0:T(8,128)(2,1)} %fusion.1.refs_8_), channel_id=1, source_target_pairs={{0,2},{1,3},{2,0},{3,1},{4,6},{5,7},{6,4},{7,5},{8,10},{9,11},{10,... | collective-permute-start | bytes 5308424 | tf_op jit(solution)/shard_map/ppermute | solution.py:943
  678.8 63.3 %collective-permute-start.37 = (bf16[2,2,2,144,768]{4,3,1,0,2:T(8,128)(2,1)}, bf16[2,2,2,144,768]{4,3,1,0,2:T(8,128)(2,1)}, u32[]{:S(2)}, u32[]{:S(2)}) collective-permute-start(bf16[2,2,2,144,768]{4,3,1,0,2:T(8,128)(2,1)} %fusion), channel_id=1, source_target_pairs={{0,1},{1,0},{2,3},{3,2},{4,5},{5,4},{6,7},{7,6},{8,9},{9,8},{10,11... | collective-permute-start | bytes 5308424 | tf_op jit(solution)/shard_map/ppermute | solution.py:943
  686.7 46.1 %collective-permute-start.34 = (bf16[240,768]{1,0:T(8,128)(2,1)}, bf16[240,768]{1,0:T(8,128)(2,1)}, u32[]{:S(2)}, u32[]{:S(2)}) collective-permute-start(bf16[240,768]{1,0:T(8,128)(2,1)} %get-tuple-element.388.refs_4_), channel_id=1, source_target_pairs={{0,4},{1,5},{2,6},{3,7},{4,0},{5,1},{6,2},{7,3},{8,12},{9,13},{10,... | collective-permute-start | bytes 1105928 | tf_op jit(solution)/shard_map/ppermute | solution.py:943
  687.9 47.8 %collective-permute-start.35 = (bf16[240,768]{1,0:T(8,128)(2,1)}, bf16[240,768]{1,0:T(8,128)(2,1)}, u32[]{:S(2)}, u32[]{:S(2)}) collective-permute-start(bf16[240,768]{1,0:T(8,128)(2,1)} %get-tuple-element.389.refs_5_), channel_id=1, source_target_pairs={{0,8},{1,9},{2,10},{3,11},{4,12},{5,13},{6,14},{7,15},{8,0},{9,1},... | collective-permute-start | bytes 1105928 | tf_op jit(solution)/shard_map/ppermute | solution.py:943
  688.8 46.9 %collective-permute-start.36 = (bf16[240,768]{1,0:T(8,128)(2,1)S(1)}, bf16[240,768]{1,0:T(8,128)(2,1)}, u32[]{:S(2)}, u32[]{:S(2)}) collective-permute-start(bf16[240,768]{1,0:T(8,128)(2,1)S(1)} %get-tuple-element.387.refs_6_), channel_id=1, source_target_pairs={{0,12},{1,13},{2,14},{3,15},{4,8},{5,9},{6,10},{7,11},{8,4},{9,5},... | collective-permute-start | bytes 1105928 | tf_op jit(solution)/shard_map/ppermute | solution.py:943
  732.8 43.1 %collective-permute-start.32 = (bf16[16,48,768]{2,1,0:T(8,128)(2,1)}, bf16[16,48,768]{2,1,0:T(8,128)(2,1)}, u32[]{:S(2)}, u32[]{:S(2)}) collective-permute-start(bf16[16,48,768]{2,1,0:T(8,128)(2,1)} %get-tuple-element.310), channel_id=1, source_target_pairs={{0,16},{16,0},{1,17},{17,1},{2,18},{18,2},{3,19},{19,3},{4,20},{20... | collective-permute-start | bytes 3538952 | tf_op jit(solution)/shard_map/ppermute | solution.py:943
  735.7 40.2 %collective-permute-start.33 = (bf16[2,48,2048]{2,1,0:T(8,128)(2,1)}, bf16[2,48,2048]{2,1,0:T(8,128)(2,1)}, u32[]{:S(2)}, u32[]{:S(2)}) collective-permute-start(bf16[2,48,2048]{2,1,0:T(8,128)(2,1)} %select_bitcast_fusion.9), channel_id=1, source_target_pairs={{0,8},{1,9},{2,10},{3,11},{4,12},{5,13},{6,14},{7,15},{8,0},{9,1},... | collective-permute-start | bytes 1179656 | tf_op jit(solution)/shard_map/ppermute | solution.py:1395
  772.4 34.5 %collective-permute-start.45 = (bf16[2,288,768]{2,1,0:T(8,128)(2,1)S(1)}, bf16[2,288,768]{2,1,0:T(8,128)(2,1)S(1)}, u32[]{:S(2)}, u32[]{:S(2)}) collective-permute-start(bf16[2,288,768]{2,1,0:T(8,128)(2,1)S(1)} %get-tuple-element.382), channel_id=1, source_target_pairs={{0,4},{1,5},{2,6},{3,7},{4,0},{5,1},{6,2},{7,3},{8,12},{9,13},{10,... | collective-permute-start | bytes 2654216 | tf_op jit(solution)/shard_map/ppermute | solution.py:943
  780.4 43.6 %collective-permute-start.42 = (bf16[512,768]{1,0:T(8,128)(2,1)S(1)}, bf16[512,768]{1,0:T(8,128)(2,1)S(1)}, u32[]{:S(2)}, u32[]{:S(2)}) collective-permute-start(bf16[512,768]{1,0:T(8,128)(2,1)S(1)} %select_convert_fusion), channel_id=1, source_target_pairs={{0,8},{1,9},{2,10},{3,11},{4,12},{5,13},{6,14},{7,15},{8,0},{9,1},... | collective-permute-start | bytes 2359304 | tf_op jit(solution)/shard_map/ppermute | solution.py:1421
  (96 other events, 1386.5 us)
Sparse Core Ops, SparseCore 0:
  11.4 173.9 all-gather.2

commit v4 on v3

--- a/solution.py
+++ b/solution.py
@@ -1237,7 +1237,7 @@
         if len(moved) < 2:
             got, moves[len(moved) + 1] = chains.finish(started, got, moves[len(moved) + 1])
         else:
-            (got,) = chains.finish(started, got)
+            chains.finish(started)
         moved.append(got)
     while chains.waiting:
         chains.finish(chains.start())
@@ -1271,6 +1271,8 @@
             stream, got = got[0], got[1:]
         operand, gate_two, normed_one = got
         gates = exchange(operand.reshape(peers, groups, 2, cut, length))
+        if natural:
+            gates, got_taps = together(gates, got_taps)
         taps.append(ordered(kept[layer], got_taps))
         if more:
             following = Chains()

time: 870 us -> 875 us (level)
    all_to_all x8, waiting for transfers between devices: 136 us -> 83.6 us  [exchange(): lax.all_to_all(x, 'mp', split_axis=0, concat_axis=0, tiled=True, axis_ind...]
    ppermute x3, waiting for transfers between devices: 62.7 us -> 96 us  [program(): got = lax.ppermute(now, 'mp', swap)]
    ppermute x41, waiting for transfers between devices: 92.5 us -> 111 us  [flip(): return lax.ppermute(x, axis, [(i, i ^ bit) for i in range(size)])]
  transfers between devices with their start and end apart: 61 -> 61, of which waited for: 26 -> 28; matrix products, arithmetic and copies ran while one was open for 10% -> 10% of each run, Pallas kernels for 31% -> 31%
where the time goes in v4:
time: 875 us; the launch traced here: 866 us
  waiting for transfers between devices  309 us (35%)
  Pallas kernels  309 us (35%)
  starting transfers between devices  126 us (14%)
  other arithmetic  66.4 us (8%)
  local copies, waits for them, and re-layouts  39.4 us (5%)
  between operations  15.9 us (2%)
    ppermute x41, waiting for transfers between devices, flip(): return lax.ppermute(x, axis, [(i, i ^ bit) for i in range(size)])  111 us
    ppermute x3, waiting for transfers between devices, program(): got = lax.ppermute(now, 'mp', swap)  96 us
    all_to_all x8, waiting for transfers between devices, exchange(): lax.all_to_all(x, 'mp', split_axis=0, concat_axis=0, tiled=True, axis_ind...  83.6 us
    ppermute x41, starting transfers between devices, flip(): return lax.ppermute(x, axis, [(i, i ^ bit) for i in range(size)])  77.3 us
    pallas_call x2, Pallas kernels, forward_block(): pl.pallas_call(functools.partial(forward_body, natural, len(ff)), grid=(l...  61.8 us
    pallas_call x3, Pallas kernels, weight_grads(): pl.pallas_call(functools.partial(grads_body, ways, jobs, len(before)), gr...  52.6 us
    pallas_call x2, Pallas kernels, backward_block(): pl.pallas_call(functools.partial(backward_body, natural, len(ff)), grid=(...  50.9 us
    all_to_all x8, starting transfers between devices, exchange(): lax.all_to_all(x, 'mp', split_axis=0, concat_axis=0, tiled=True, axis_ind...  41.4 us
  transfers between devices with their start and end apart: 61, of which 28 were waited for; matrix products, arithmetic and copies ran while one was open for 10% of the time, Pallas kernels for 31%

profile of v4, /device:TPU:1, one launch (start us, length us, event | category | flops | bytes accessed | tf_op | source)
XLA Modules:
  0.0 866.3 jit_solution(2137314252056976278)
XLA Ops:
  27.4 12.8 %collective-permute-done.3 = bf16[2,48,768]{2,1,0:T(8,128)(2,1)} collective-permute-done((bf16[2,48,768]{2,1,0:T(8,128)(2,1)S(1)}, bf16[2,48,768]{2,1,0:T(8,128)(2,1)}, u32[]{:S(2)}, u32[]{:S(2)}) %collective-permute-start.3) | collective-permute-done | bytes 147488 | tf_op jit(solution)/shard_map/ppermute | solution.py:943
  72.1 27.3 %collective-permute-done.7 = bf16[256,768]{1,0:T(8,128)(2,1)S(1)} collective-permute-done((bf16[256,768]{1,0:T(8,128)(2,1)S(1)}, bf16[256,768]{1,0:T(8,128)(2,1)S(1)}, u32[]{:S(2)}, u32[]{:S(2)}) %collective-permute-start.7) | collective-permute-done | bytes 393248 | tf_op jit(solution)/shard_map/ppermute | solution.py:1236
  99.7 17.7 %collective-permute-done.9 = bf16[2,2,2,48,768]{4,3,0,1,2:T(8,128)(2,1)S(1)} collective-permute-done((bf16[2,2,2,48,768]{4,3,0,1,2:T(8,128)(2,1)S(1)}, bf16[2,2,2,48,768]{4,3,0,1,2:T(8,128)(2,1)S(1)}, u32[]{:S(2)}, u32[]{:S(2)}) %collective-permute-start.9) | collective-permute-done | bytes 589856 | tf_op jit(solution)/shard_map/ppermute | solution.py:943
  144.6 59.7 %collective-permute-done.11 = bf16[2,48,2048]{2,1,0:T(8,128)(2,1)S(1)} collective-permute-done((bf16[2,48,2048]{2,1,0:T(8,128)(2,1)S(1)}, bf16[2,48,2048]{2,1,0:T(8,128)(2,1)S(1)}, u32[]{:S(2)}, u32[]{:S(2)}) %collective-permute-start.11) | collective-permute-done | bytes 393248 | tf_op jit(solution)/shard_map/ppermute | solution.py:1236
  211.3 16.0 %mix.2 = (bf16[8,2,48,1024]{3,2,1,0:T(8,128)(2,1)}, bf16[2,64,48,128]{3,2,1,0:T(8,128)(2,1)}, bf16[2,64,48,128]{3,2,1,0:T(8,128)(2,1)}) custom-call(bf16[8,2,2,48,1024]{4,3,2,1,0:T(8,128)(2,1)} %all-to-all-done.v_ref.g_ref, bf16[8,2,2,48,1024]{4,3,2,1,0:T(8,128)(2,1)} %all-to-all-done.v_ref.g_ref, bf16[2,2,48,2048]{3,2,1,0:T(8,128)(2,1)} %pad_maximum_fusion.11.k_ref, ...), custom_call_target="tpu_custom_call" | custom-call | tf_op jit(solution)/shard_map/mix/pallas_call | solution.py:377
  234.8 20.2 %all-to-all-done.1 = bf16[8,2,48,1024]{3,2,1,0:T(8,128)(2,1)} async-done(((bf16[8,2,48,1024]{3,2,1,0:T(8,128)(2,1)}), bf16[8,2,48,1024]{3,2,1,0:T(8,128)(2,1)}, u32[]{:S(2)}, u32[]{:S(2)}) %all-to-all-start.1) | async-done | bytes 1572896 | tf_op jit(solution)/shard_map/all_to_all | solution.py:1173
  264.8 30.8 %forward_block.2 = (f32[768,1024]{1,0:T(8,128)}, f32[768,1024]{1,0:T(8,128)}, bf16[3072,1024]{1,0:T(8,128)(2,1)}, bf16[3072,1024]{1,0:T(8,128)(2,1)}, bf16[1024,...) custom-call(f32[768,1024]{1,0:T(8,128)} %get-tuple-element.215.s_ref, bf16[768,1024]{1,0:T(8,128)(2,1)} %bitcast.52.c_ref, ...), custom_call_target="tpu_custom_call" | custom-call | tf_op jit(solution)/shard_map/forward_block/pallas_call | solution.py:658
  323.7 35.6 %all-to-all-done.2.v_ref.g_ref = bf16[8,2,2,48,1024]{4,3,2,1,0:T(8,128)(2,1)} async-done(((bf16[8,2,2,48,1024]{4,3,2,1,0:T(8,128)(2,1)}), bf16[8,2,2,48,1024]{4,3,2,1,0:T(8,128)(2,1)}, u32[]{:S(2)}, u32[]{:S(2)}) %all-to-all-start.2) | async-done | bytes 3145760 | tf_op jit(solution)/shard_map/all_to_all | solution.py:1173
  359.3 16.0 %mix.3 = (bf16[8,2,48,1024]{3,2,1,0:T(8,128)(2,1)}, bf16[2,64,48,128]{3,2,1,0:T(8,128)(2,1)}, bf16[2,64,48,128]{3,2,1,0:T(8,128)(2,1)}) custom-call(bf16[8,2,2,48,1024]{4,3,2,1,0:T(8,128)(2,1)} %all-to-all-done.2.v_ref.g_ref, bf16[8,2,2,48,1024]{4,3,2,1,0:T(8,128)(2,1)} %all-to-all-done.2.v_ref.g_ref, bf16[2,2,48,2048]{3,2,1,0:T(8,128)(2,1)} %pad_maximum_fusion.12.k_ref, ...), custom_call_target="tpu_custom_call" | custom-call | tf_op jit(solution)/shard_map/mix/pallas_call | solution.py:377
  383.1 19.7 %all-to-all-done.3 = bf16[8,2,48,1024]{3,2,1,0:T(8,128)(2,1)} async-done(((bf16[8,2,48,1024]{3,2,1,0:T(8,128)(2,1)}), bf16[8,2,48,1024]{3,2,1,0:T(8,128)(2,1)}, u32[]{:S(2)}, u32[]{:S(2)}) %all-to-all-start.3) | async-done | bytes 1572896 | tf_op jit(solution)/shard_map/all_to_all | solution.py:1173
  405.9 31.0 %forward_block.3 = (f32[768,1024]{1,0:T(8,128)}, f32[1024,768]{1,0:T(8,128)}, bf16[3072,1024]{1,0:T(8,128)(2,1)}, bf16[3072,1024]{1,0:T(8,128)(2,1)}, bf16[1024,...) custom-call(f32[768,1024]{1,0:T(8,128)} %get-tuple-element.222.x_ref.s_ref, bf16[768,1024]{1,0:T(8,128)(2,1)} %bitcast.72.c_ref, ...), custom_call_target="tpu_custom_call" | custom-call | tf_op jit(solution)/shard_map/forward_block/pallas_call | solution.py:658
  442.7 25.0 %backward_block.2 = (bf16[3072,1024]{1,0:T(8,128)(2,1)}, f32[768,1024]{1,0:T(8,128)}, bf16[768,1024]{1,0:T(8,128)(2,1)}, bf16[768,1024]{1,0:T(8,128)(2,1)}, bf16...) custom-call(bf16[1024,768]{1,0:T(8,128)(2,1)} %bitcast.397, ...), custom_call_target="tpu_custom_call" | custom-call | tf_op jit(solution)/shard_map/backward_block/pallas_call | solution.py:733
  471.5 21.1 %early_grads.2 = (bf16[16,240,768]{2,1,0:T(8,128)(2,1)}, bf16[16,240,768]{2,1,0:T(8,128)(2,1)}) custom-call(s32[2]{0:T(128)} %pad_add_fusion.place_ref, bf16[2,16,96,1024]{3,2,1,0:T(8,128)(2,1)} %bitcast.406, bf16[2,16,96,1024]{3,2,1,0:T(8,128)(2,1)} %bitcast.404, bf16[8,2,48,1024]{3,2,1,0:T(8,128)(2,1)} %bitcast.400, bf16[8,2,48,1024]{3,2,1,0:T(8,128)(2,1)} %bitcast.420, ...), custom_call_target="tpu_custom_call" | custom-call | tf_op jit(solution)/shard_map/early_grads/pallas_call | solution.py:922
  495.1 16.1 %unmix.2 = (bf16[8,2,2,48,1024]{4,3,2,1,0:T(8,128)(2,1)}, bf16[2,64,48,128]{3,2,1,0:T(8,128)(2,1)}) custom-call(bf16[8,2,48,1024]{3,2,1,0:T(8,128)(2,1)} %copy-done.9, bf16[8,2,2,48,1024]{4,3,2,1,0:T(8,128)(2,1)} %all-to-all-done.2.v_ref.g_ref, bf16[2,64,48,128]{3,2,1,0:T(8,128)(2,1)} %get-tuple-element.257.one_ref, ...), custom_call_target="tpu_custom_call" | custom-call | tf_op jit(solution)/shard_map/unmix/pallas_call | solution.py:403
  519.4 16.4 %tap_grads.2 = f32[2,2,48,2048]{3,2,1,0:T(8,128)} custom-call(bf16[8,2,48,1024]{3,2,1,0:T(8,128)(2,1)} %copy-done.9, bf16[8,2,2,48,1024]{4,3,2,1,0:T(8,128)(2,1)} %all-to-all-done.2.v_ref.g_ref, bf16[2,64,48,128]{3,2,1,0:T(8,128)(2,1)} %get-tuple-element.266.carried_ref, bf16[2,64,48,128]{3,2,1,0:T(8,128)(2,1)} %get-tuple-element.267.grad_ref, ...), custom_call_target="tpu_custom_call" | custom-call | tf_op jit(solution)/shard_map/tap_grads/pallas_call | solution.py:431
  557.7 12.7 %unproject.2 = (f32[768,1024]{1,0:T(8,128)}, f32[1,768]{1,0:T(1,128)}, f32[1,768]{1,0:T(1,128)}) custom-call(s32[2]{0:T(128)} %pad_add_fusion.place_ref, bf16[16,2,48,1024]{3,2,1,0:T(8,128)(2,1)} %bitcast.89.gm_ref, bf16[16,48,1024]{2,1,0:T(8,128)(2,1)} %bitcast.401, f32[768,1024]{1,0:T(8,128)} %get-tuple-element.222.x_ref.s_ref, ...), custom_call_target="tpu_custom_call" | custom-call | tf_op jit(solution)/shard_map/unproject/pallas_call | solution.py:804
  577.6 25.9 %backward_block.3 = (bf16[3072,1024]{1,0:T(8,128)(2,1)}, f32[768,1024]{1,0:T(8,128)}, bf16[768,1024]{1,0:T(8,128)(2,1)}, bf16[768,1024]{1,0:T(8,128)(2,1)}, bf16...) custom-call(f32[768,1024]{1,0:T(8,128)} %get-tuple-element.275.gs_ref, ...), custom_call_target="tpu_custom_call" | custom-call | tf_op jit(solution)/shard_map/backward_block/pallas_call | solution.py:733
  615.6 25.0 %early_grads.3 = (bf16[16,288,768]{2,1,0:T(8,128)(2,1)}, bf16[16,288,768]{2,1,0:T(8,128)(2,1)}) custom-call(s32[2]{0:T(128)} %pad_add_fusion.place_ref, bf16[2,16,96,1024]{3,2,1,0:T(8,128)(2,1)} %bitcast.405, bf16[2,16,96,1024]{3,2,1,0:T(8,128)(2,1)} %bitcast.403, bf16[8,2,48,1024]{3,2,1,0:T(8,128)(2,1)} %bitcast.398, bf16[8,2,48,1024]{3,2,1,0:T(8,128)(2,1)} %bitcast.419, ...), custom_call_target="tpu_custom_call" | custom-call | tf_op jit(solution)/shard_map/early_grads/pallas_call | solution.py:922
  650.1 16.1 %unmix.3 = (bf16[8,2,2,48,1024]{4,3,2,1,0:T(8,128)(2,1)}, bf16[2,64,48,128]{3,2,1,0:T(8,128)(2,1)}) custom-call(bf16[8,2,48,1024]{3,2,1,0:T(8,128)(2,1)} %copy-done.8, bf16[8,2,2,48,1024]{4,3,2,1,0:T(8,128)(2,1)} %all-to-all-done.v_ref.g_ref, bf16[2,64,48,128]{3,2,1,0:T(8,128)(2,1)} %get-tuple-element.300.one_ref, ...), custom_call_target="tpu_custom_call" | custom-call | tf_op jit(solution)/shard_map/unmix/pallas_call | solution.py:403
  694.7 16.3 %tap_grads.3 = f32[2,2,48,2048]{3,2,1,0:T(8,128)} custom-call(bf16[8,2,48,1024]{3,2,1,0:T(8,128)(2,1)} %copy-done.8, bf16[8,2,2,48,1024]{4,3,2,1,0:T(8,128)(2,1)} %all-to-all-done.v_ref.g_ref, bf16[2,64,48,128]{3,2,1,0:T(8,128)(2,1)} %get-tuple-element.303.carried_ref, bf16[2,64,48,128]{3,2,1,0:T(8,128)(2,1)} %get-tuple-element.304.grad_ref, ...), custom_call_target="tpu_custom_call" | custom-call | tf_op jit(solution)/shard_map/tap_grads/pallas_call | solution.py:431
  723.0 13.5 %unproject.3 = (f32[1024,768]{1,0:T(8,128)}, f32[1,768]{1,0:T(1,128)}, f32[1,768]{1,0:T(1,128)}) custom-call(s32[2]{0:T(128)} %pad_add_fusion.place_ref, bf16[16,2,48,1024]{3,2,1,0:T(8,128)(2,1)} %bitcast.106.gm_ref, bf16[16,48,1024]{2,1,0:T(8,128)(2,1)} %bitcast.399, f32[768,1024]{1,0:T(8,128)} %get-tuple-element.215.s_ref, ...), custom_call_target="tpu_custom_call" | custom-call | tf_op jit(solution)/shard_map/unproject/pallas_call | solution.py:804
  759.2 10.5 %collective-permute-done.44 = bf16[2,2,144,768]{3,2,1,0:T(8,128)(2,1)} collective-permute-done((bf16[2,2,144,768]{3,2,1,0:T(8,128)(2,1)}, bf16[2,2,144,768]{3,2,1,0:T(8,128)(2,1)}, u32[]{:S(2)}, u32[]{:S(2)}) %collective-permute-start.44) | collective-permute-done | bytes 884768 | tf_op jit(solution)/shard_map/ppermute | solution.py:943
  788.1 23.4 %collective-permute-done.45 = bf16[2,288,768]{2,1,0:T(8,128)(2,1)S(1)} collective-permute-done((bf16[2,288,768]{2,1,0:T(8,128)(2,1)S(1)}, bf16[2,288,768]{2,1,0:T(8,128)(2,1)S(1)}, u32[]{:S(2)}, u32[]{:S(2)}) %collective-permute-start.45) | collective-permute-done | bytes 884768 | tf_op jit(solution)/shard_map/ppermute | solution.py:943
  812.8 15.7 %collective-permute-done.42 = bf16[512,768]{1,0:T(8,128)(2,1)S(1)} collective-permute-done((bf16[512,768]{1,0:T(8,128)(2,1)S(1)}, bf16[512,768]{1,0:T(8,128)(2,1)S(1)}, u32[]{:S(2)}, u32[]{:S(2)}) %collective-permute-start.42) | collective-permute-done | bytes 786464 | tf_op jit(solution)/shard_map/ppermute | solution.py:1423
  (375 shorter events, 325.8 us)
Async XLA Ops:
  7.2 198.5 %all-gather.3.cloned.1.call-start = ((), (), s32[]{:S(2)}) async-start(), calls=%async_computation.8 | async-start | bytes 10027008 | tf_op jit(solution)/shard_map/all_gather | solution.py:1197
  58.6 40.7 %collective-permute-start.7 = (bf16[256,768]{1,0:T(8,128)(2,1)S(1)}, bf16[256,768]{1,0:T(8,128)(2,1)S(1)}, u32[]{:S(2)}, u32[]{:S(2)}) collective-permute-start(bf16[256,768]{1,0:T(8,128)(2,1)S(1)} %copy-done.38), channel_id=1, source_target_pairs={{0,8},{1,9},{2,10},{3,11},{4,12},{5,13},{6,14},{7,15},{8,0},{9,1},... | collective-permute-start | bytes 1179656 | tf_op jit(solution)/shard_map/ppermute | solution.py:1236
  139.8 65.8 %all-to-all-start = ((bf16[8,2,2,48,1024]{4,3,2,1,0:T(8,128)(2,1)}), bf16[8,2,2,48,1024]{4,3,2,1,0:T(8,128)(2,1)}, u32[]{:S(2)}, u32[]{:S(2)}) async-start(bf16[8,2,2,48,1024]{4,3,2,1,0:T(8,128)(2,1)} %bitcast.416), calls=%async_computation | async-start | bytes 6291456 | tf_op jit(solution)/shard_map/all_to_all | solution.py:1173
  144.5 59.8 %collective-permute-start.11 = (bf16[2,48,2048]{2,1,0:T(8,128)(2,1)S(1)}, bf16[2,48,2048]{2,1,0:T(8,128)(2,1)S(1)}, u32[]{:S(2)}, u32[]{:S(2)}) collective-permute-start(bf16[2,48,2048]{2,1,0:T(8,128)(2,1)S(1)} %copy-done.37), channel_id=1, source_target_pairs={{0,8},{1,9},{2,10},{3,11},{4,12},{5,13},{6,14},{7,15},{8,0},{9,1},... | collective-permute-start | bytes 1179656 | tf_op jit(solution)/shard_map/ppermute | solution.py:1236
  205.7 49.4 %collective-permute-start.15 = (bf16[16,384,768]{2,1,0:T(8,128)(2,1)}, bf16[16,384,768]{2,1,0:T(8,128)(2,1)}, u32[]{:S(2)}, u32[]{:S(2)}) collective-permute-start(bf16[16,384,768]{2,1,0:T(8,128)(2,1)} %bitcast.378), channel_id=1, source_target_pairs={{0,16},{16,0},{1,17},{17,1},{2,18},{18,2},{3,19},{19,3},{4,20},{20... | collective-permute-start | bytes 28311560 | tf_op jit(solution)/shard_map/ppermute | solution.py:943
  255.0 40.6 %collective-permute-start.16 = (bf16[2,2,96,768]{3,2,1,0:T(8,128)(2,1)S(1)}, bf16[2,2,96,768]{3,2,1,0:T(8,128)(2,1)}, u32[]{:S(2)}, u32[]{:S(2)}) collective-permute-start(bf16[2,2,96,768]{3,2,1,0:T(8,128)(2,1)S(1)} %pad_maximum_fusion.19), channel_id=1, source_target_pairs={{0,1},{1,0},{2,3},{3,2},{4,5},{5,4},{6,7},{7,6},{8,9},{9,8},{10,11... | collective-permute-start | bytes 1769480 | tf_op jit(solution)/shard_map/ppermute | solution.py:943
  255.4 40.2 %collective-permute-start.17 = (bf16[2,2,96,768]{3,2,1,0:T(8,128)(2,1)S(1)}, bf16[2,2,96,768]{3,2,1,0:T(8,128)(2,1)}, u32[]{:S(2)}, u32[]{:S(2)}) collective-permute-start(bf16[2,2,96,768]{3,2,1,0:T(8,128)(2,1)S(1)} %pad_maximum_fusion.19), channel_id=1, source_target_pairs={{0,2},{1,3},{2,0},{3,1},{4,6},{5,7},{6,4},{7,5},{8,10},{9,11},{10,... | collective-permute-start | bytes 1769480 | tf_op jit(solution)/shard_map/ppermute | solution.py:943
  256.1 39.6 %collective-permute-start.18 = (bf16[2,2,96,768]{3,2,1,0:T(8,128)(2,1)S(1)}, bf16[2,2,96,768]{3,2,1,0:T(8,128)(2,1)}, u32[]{:S(2)}, u32[]{:S(2)}) collective-permute-start(bf16[2,2,96,768]{3,2,1,0:T(8,128)(2,1)S(1)} %pad_maximum_fusion.19), channel_id=1, source_target_pairs={{0,3},{1,2},{2,1},{3,0},{4,7},{5,6},{6,5},{7,4},{8,11},{9,10},{10,... | collective-permute-start | bytes 1769480 | tf_op jit(solution)/shard_map/ppermute | solution.py:943
  259.2 36.5 %collective-permute-start.19 = (bf16[2,48,2048]{2,1,0:T(8,128)(2,1)}, bf16[2,48,2048]{2,1,0:T(8,128)(2,1)}, u32[]{:S(2)}, u32[]{:S(2)}) collective-permute-start(bf16[2,48,2048]{2,1,0:T(8,128)(2,1)} %get-tuple-element.212), channel_id=1, source_target_pairs={{0,8},{1,9},{2,10},{3,11},{4,12},{5,13},{6,14},{7,15},{8,0},{9,1},... | collective-permute-start | bytes 1179656 | tf_op jit(solution)/shard_map/ppermute | solution.py:1298
  260.8 34.8 %collective-permute-start.20 = (bf16[192,768]{1,0:T(8,128)(2,1)}, bf16[192,768]{1,0:T(8,128)(2,1)S(1)}, u32[]{:S(2)}, u32[]{:S(2)}) collective-permute-start(bf16[192,768]{1,0:T(8,128)(2,1)} %slice_bitcast_fusion.10), channel_id=1, source_target_pairs={{0,8},{1,9},{2,10},{3,11},{4,12},{5,13},{6,14},{7,15},{8,0},{9,1},... | collective-permute-start | bytes 884744 | tf_op jit(solution)/shard_map/ppermute | solution.py:1303
  316.7 42.6 %all-to-all-start.2 = ((bf16[8,2,2,48,1024]{4,3,2,1,0:T(8,128)(2,1)}), bf16[8,2,2,48,1024]{4,3,2,1,0:T(8,128)(2,1)}, u32[]{:S(2)}, u32[]{:S(2)}) async-start(bf16[8,2,2,48,1024]{4,3,2,1,0:T(8,128)(2,1)} %bitcast.417), calls=%async_computation.2 | async-start | bytes 6291456 | tf_op jit(solution)/shard_map/all_to_all | solution.py:1173
  514.6 42.0 %all-to-all-start.5 = ((bf16[8,2,2,48,1024]{4,3,2,1,0:T(8,128)(2,1)}), bf16[8,2,2,48,1024]{4,3,2,1,0:T(8,128)(2,1)}, u32[]{:S(2)}, u32[]{:S(2)}) async-start(bf16[8,2,2,48,1024]{4,3,2,1,0:T(8,128)(2,1)} %get-tuple-element.261), calls=%async_computation.5 | async-start | bytes 6291456 | tf_op jit(solution)/shard_map/all_to_all | solution.py:1173
  570.4 37.5 %collective-permute-start.26 = (bf16[2,2,2,128,768]{4,3,1,0,2:T(8,128)(2,1)S(1)}, bf16[2,2,2,128,768]{4,3,1,0,2:T(8,128)(2,1)}, u32[]{:S(2)}, u32[]{:S(2)}) collective-permute-start(bf16[2,2,2,128,768]{4,3,1,0,2:T(8,128)(2,1)S(1)} %copy-done.30), channel_id=1, source_target_pairs={{0,1},{1,0},{2,3},{3,2},{4,5},{5,4},{6,7},{7,6},{8,9},{9,8},{10,11... | collective-permute-start | bytes 4718600 | tf_op jit(solution)/shard_map/ppermute | solution.py:943
  608.0 36.6 %all-to-all-start.6 = ((bf16[8,2,48,1024]{3,2,1,0:T(8,128)(2,1)}), bf16[8,2,48,1024]{3,2,1,0:T(8,128)(2,1)S(1)}, u32[]{:S(2)}, u32[]{:S(2)}) async-start(bf16[8,2,48,1024]{3,2,1,0:T(8,128)(2,1)} %bitcast.421), calls=%async_computation.6 | async-start | bytes 3145728 | tf_op jit(solution)/shard_map/all_to_all | solution.py:1173
  667.1 49.2 %all-to-all-start.7 = ((bf16[8,2,2,48,1024]{4,3,2,1,0:T(8,128)(2,1)}), bf16[8,2,2,48,1024]{4,3,2,1,0:T(8,128)(2,1)}, u32[]{:S(2)}, u32[]{:S(2)}) async-start(bf16[8,2,2,48,1024]{4,3,2,1,0:T(8,128)(2,1)} %get-tuple-element.302), calls=%async_computation.7 | async-start | bytes 6291456 | tf_op jit(solution)/shard_map/all_to_all | solution.py:1173
  677.9 66.9 %collective-permute-start.38 = (bf16[2,2,2,144,768]{4,3,2,1,0:T(8,128)(2,1)}, bf16[2,2,2,144,768]{4,3,2,1,0:T(8,128)(2,1)}, u32[]{:S(2)}, u32[]{:S(2)}) collective-permute-start(bf16[2,2,2,144,768]{4,3,2,1,0:T(8,128)(2,1)} %fusion.1.refs_8_), channel_id=1, source_target_pairs={{0,2},{1,3},{2,0},{3,1},{4,6},{5,7},{6,4},{7,5},{8,10},{9,11},{10,... | collective-permute-start | bytes 5308424 | tf_op jit(solution)/shard_map/ppermute | solution.py:943
  683.2 63.3 %collective-permute-start.37 = (bf16[2,2,2,144,768]{4,3,1,0,2:T(8,128)(2,1)}, bf16[2,2,2,144,768]{4,3,1,0,2:T(8,128)(2,1)}, u32[]{:S(2)}, u32[]{:S(2)}) collective-permute-start(bf16[2,2,2,144,768]{4,3,1,0,2:T(8,128)(2,1)} %fusion), channel_id=1, source_target_pairs={{0,1},{1,0},{2,3},{3,2},{4,5},{5,4},{6,7},{7,6},{8,9},{9,8},{10,11... | collective-permute-start | bytes 5308424 | tf_op jit(solution)/shard_map/ppermute | solution.py:943
  691.2 46.1 %collective-permute-start.34 = (bf16[240,768]{1,0:T(8,128)(2,1)}, bf16[240,768]{1,0:T(8,128)(2,1)}, u32[]{:S(2)}, u32[]{:S(2)}) collective-permute-start(bf16[240,768]{1,0:T(8,128)(2,1)} %get-tuple-element.390.refs_4_), channel_id=1, source_target_pairs={{0,4},{1,5},{2,6},{3,7},{4,0},{5,1},{6,2},{7,3},{8,12},{9,13},{10,... | collective-permute-start | bytes 1105928 | tf_op jit(solution)/shard_map/ppermute | solution.py:943
  692.4 47.7 %collective-permute-start.35 = (bf16[240,768]{1,0:T(8,128)(2,1)}, bf16[240,768]{1,0:T(8,128)(2,1)}, u32[]{:S(2)}, u32[]{:S(2)}) collective-permute-start(bf16[240,768]{1,0:T(8,128)(2,1)} %get-tuple-element.391.refs_5_), channel_id=1, source_target_pairs={{0,8},{1,9},{2,10},{3,11},{4,12},{5,13},{6,14},{7,15},{8,0},{9,1},... | collective-permute-start | bytes 1105928 | tf_op jit(solution)/shard_map/ppermute | solution.py:943
  693.5 46.9 %collective-permute-start.36 = (bf16[240,768]{1,0:T(8,128)(2,1)S(1)}, bf16[240,768]{1,0:T(8,128)(2,1)}, u32[]{:S(2)}, u32[]{:S(2)}) collective-permute-start(bf16[240,768]{1,0:T(8,128)(2,1)S(1)} %get-tuple-element.389.refs_6_), channel_id=1, source_target_pairs={{0,12},{1,13},{2,14},{3,15},{4,8},{5,9},{6,10},{7,11},{8,4},{9,5},... | collective-permute-start | bytes 1105928 | tf_op jit(solution)/shard_map/ppermute | solution.py:943
  737.3 43.0 %collective-permute-start.32 = (bf16[16,48,768]{2,1,0:T(8,128)(2,1)}, bf16[16,48,768]{2,1,0:T(8,128)(2,1)}, u32[]{:S(2)}, u32[]{:S(2)}) collective-permute-start(bf16[16,48,768]{2,1,0:T(8,128)(2,1)} %get-tuple-element.312), channel_id=1, source_target_pairs={{0,16},{16,0},{1,17},{17,1},{2,18},{18,2},{3,19},{19,3},{4,20},{20... | collective-permute-start | bytes 3538952 | tf_op jit(solution)/shard_map/ppermute | solution.py:943
  740.1 40.2 %collective-permute-start.33 = (bf16[2,48,2048]{2,1,0:T(8,128)(2,1)}, bf16[2,48,2048]{2,1,0:T(8,128)(2,1)}, u32[]{:S(2)}, u32[]{:S(2)}) collective-permute-start(bf16[2,48,2048]{2,1,0:T(8,128)(2,1)} %select_bitcast_fusion.9), channel_id=1, source_target_pairs={{0,8},{1,9},{2,10},{3,11},{4,12},{5,13},{6,14},{7,15},{8,0},{9,1},... | collective-permute-start | bytes 1179656 | tf_op jit(solution)/shard_map/ppermute | solution.py:1397
  776.8 34.7 %collective-permute-start.45 = (bf16[2,288,768]{2,1,0:T(8,128)(2,1)S(1)}, bf16[2,288,768]{2,1,0:T(8,128)(2,1)S(1)}, u32[]{:S(2)}, u32[]{:S(2)}) collective-permute-start(bf16[2,288,768]{2,1,0:T(8,128)(2,1)S(1)} %get-tuple-element.384), channel_id=1, source_target_pairs={{0,4},{1,5},{2,6},{3,7},{4,0},{5,1},{6,2},{7,3},{8,12},{9,13},{10,... | collective-permute-start | bytes 2654216 | tf_op jit(solution)/shard_map/ppermute | solution.py:943
  784.8 43.6 %collective-permute-start.42 = (bf16[512,768]{1,0:T(8,128)(2,1)S(1)}, bf16[512,768]{1,0:T(8,128)(2,1)S(1)}, u32[]{:S(2)}, u32[]{:S(2)}) collective-permute-start(bf16[512,768]{1,0:T(8,128)(2,1)S(1)} %select_convert_fusion), channel_id=1, source_target_pairs={{0,8},{1,9},{2,10},{3,11},{4,12},{5,13},{6,14},{7,15},{8,0},{9,1},... | collective-permute-start | bytes 2359304 | tf_op jit(solution)/shard_map/ppermute | solution.py:1423
  (95 other events, 1343.8 us)
Sparse Core Ops, SparseCore 0:
  11.4 174.0 all-gather.2
